TPU v7x, 128 devices: a whole 4x4x4 slice. The times are simulated.
128 devices in a mesh: sec: 4 (over y), dev: 32 (over z, x, core).
Axes of the slice: x: 4, y: 4, z: 4, core: 2. Of those that a mesh axis runs over, the one named last changes fastest.
Arguments:
- query: bfloat16 [256, 8192], P(('sec', 'dev')), may hold values from -160 to 160
- fresh_key_value: bfloat16 [256, 4, 256], P(('sec', 'dev')), may hold values from -6 to 6
- kv_cache: bfloat16 [256, 1024, 4, 256], P(('sec', 'dev')), may hold values from -6 to 6
- cache_lengths: int32 [256], P(('sec', 'dev')), may hold values from 2 to 1024, as said below
- hidden: bfloat16 [1536, 4096], P(('sec', 'dev')), may hold values from -6 to 6
- routes: int32 [1536, 8], P(('sec', 'dev')), may hold values from 0 to 15, all different within a row; in each aligned block of 12 rows (0 to 11, 12 to 23, ...) at most 9 rows name the same one
- gates: float32 [1536, 8], P(('sec', 'dev')), may hold values from 0.05 to 1
- w_gate_up: bfloat16 [128, 4096, 1536], P(('sec', 'dev')), may hold values from -0.09375 to 0.09375
- w_down: bfloat16 [128, 768, 4096], P(('sec', 'dev')), may hold values from -0.15625 to 0.15625
Outputs:
- attention_out: bfloat16 [256, 8192], P(('sec', 'dev'))
- moe_out: bfloat16 [1536, 4096], P(('sec', 'dev'))
Inputs may be any that keep to these rules, and one draw needn't show every extreme that they name: `cache_lengths`: one served request holds all 1024 entries. `routes`: each row names 8 different experts; among the 12 rows of one device no expert is named more than 9 times.
All inputs are finite; a program needn't handle non-finite values.
Results may differ from a plain program's by a relative error of at most 0.005.
Values may be sent and summed in bfloat16 or wider, within the bound.
No kernel may reach another device: no remote copies, remote signals or barrier semaphores. Data moves between devices by JAX's collectives and lax.ppermute only.
A program may use at most 128 MiB of HBM per device.

v0:
```python
import jax
import jax.numpy as jnp
from jax import lax
from jax.sharding import PartitionSpec as P


def swapped(shard, axis, distance):
    return lax.ppermute(shard, axis, [(i, i ^ 1 << distance) for i in range(lax.axis_size(axis))])


def spread_2(block, axis, owner):
    block = jnp.where(lax.axis_index(axis) == owner, block, jnp.zeros_like(block))
    return lax.psum(block, axis)


def attention_block(query, fresh_key_value, kv_cache, cache_lengths):
    count_req = query.shape[0]
    heads_kv = fresh_key_value.shape[1]
    head_size = fresh_key_value.shape[2] // 2
    group_size = query.shape[1] // (heads_kv * head_size)
    query_heads = query.reshape(count_req, heads_kv, group_size, head_size)
    score_scale = head_size ** (-0.5)
    scores = (
        jnp.einsum(
            "rghd,rtgd->rght",
            query_heads,
            kv_cache[..., :head_size],
            preferred_element_type=jnp.float32,
        )
        * score_scale
    )
    valid = jnp.arange(kv_cache.shape[1], dtype=jnp.int32)[None, :] < cache_lengths[:, None]
    scores = jnp.where(valid[:, None, None, :], scores, -jnp.inf)
    own_score = (
        jnp.einsum(
            "rghd,rgd->rgh",
            query_heads,
            fresh_key_value[..., :head_size],
            preferred_element_type=jnp.float32,
        )
        * score_scale
    )
    peak = jnp.maximum(jnp.max(scores, axis=-1), own_score)
    weights = jnp.exp(scores - peak[..., None])
    own_weight = jnp.exp(own_score - peak)
    denominator = jnp.sum(weights, axis=-1) + own_weight
    own_low = lax.optimization_barrier(own_weight.astype(jnp.bfloat16)).astype(jnp.float32)
    mixture = jnp.einsum(
        "rght,rtgd->rghd",
        weights.astype(jnp.bfloat16),
        kv_cache[..., head_size:],
        preferred_element_type=jnp.float32,
    )
    mixture = (
        mixture
        + own_low[..., None] * fresh_key_value[..., head_size:].astype(jnp.float32)[:, :, None, :]
    )
    return (mixture / denominator[..., None]).astype(jnp.bfloat16).reshape(count_req, -1)


def run_attention(items):
    return attention_block(items[0], items[1], items[2], items[3])


def skip_attention(items):
    return jnp.zeros(items[0].shape, jnp.bfloat16)


def per_device(
    query, fresh_key_value, kv_cache, cache_lengths, hidden, routes, gates, w_gate_up, w_down
):
    sections = lax.axis_size("sec")
    owners = lax.axis_size("dev")
    section = lax.axis_index("sec")
    expert_side = section == sections - 1
    attention_out = lax.cond(
        expert_side,
        skip_attention,
        run_attention,
        (query, fresh_key_value, kv_cache, cache_lengths),
    )
    token_count, top_count = routes.shape
    model_width = hidden.shape[1]
    half_width = model_width // 2
    experts = owners // 2
    capacity = max(2, (3 * token_count * top_count + 2 * experts - 1) // (2 * experts))
    flat_routes = routes.reshape(-1)
    expert_hot = (flat_routes[:, None] == jnp.arange(experts, dtype=jnp.int32)[None, :]).astype(
        jnp.int32
    )
    before = jnp.cumsum(expert_hot, axis=0) - expert_hot
    slot_index = jnp.sum(before * expert_hot, axis=1)
    position = flat_routes * capacity + slot_index
    place_hot = position[:, None] == jnp.arange(experts * capacity, dtype=jnp.int32)[None, :]
    owner_row = jnp.arange(token_count * top_count, dtype=jnp.int32) // top_count
    row_hot = owner_row[:, None] == jnp.arange(token_count, dtype=jnp.int32)[None, :]
    spread = jnp.einsum(
        "as,ar->sr",
        place_hot.astype(jnp.bfloat16),
        row_hot.astype(jnp.bfloat16),
        preferred_element_type=jnp.float32,
    )
    spread = spread.astype(jnp.bfloat16).reshape(experts, capacity, token_count)
    combine = gates / jnp.sum(gates, axis=1, keepdims=True)
    mixer = jnp.einsum(
        "ar,as->rs",
        row_hot.astype(jnp.float32) * combine.reshape(-1)[:, None],
        place_hot.astype(jnp.float32),
        precision=lax.Precision.HIGHEST,
    )
    mixer = mixer.reshape(token_count, experts, capacity)
    packed = jnp.einsum("ecr,rk->eck", spread, hidden, preferred_element_type=jnp.float32).astype(
        jnp.bfloat16
    )
    outgoing = jnp.broadcast_to(packed[:, None], (experts, 2, capacity, model_width)).reshape(
        owners, capacity, model_width
    )
    collected = lax.all_gather(outgoing[None], "sec", axis=0, tiled=True)
    rows = lax.all_to_all(collected[: sections - 1], "dev", split_axis=1, concat_axis=1, tiled=True)
    parity = lax.axis_index("dev") % 2
    gate_up = w_gate_up[0]
    down_weight = w_down[0]
    inner_width = down_weight.shape[0]

    def serve_rows(rows_in):
        flat_rows = rows_in.reshape(-1, model_width)
        projected = jnp.dot(flat_rows, gate_up, preferred_element_type=jnp.float32)
        activated = (jax.nn.silu(projected[:, :inner_width]) * projected[:, inner_width:]).astype(
            jnp.bfloat16
        )
        return jnp.dot(activated, down_weight, preferred_element_type=jnp.float32).reshape(
            rows_in.shape
        )

    def skip_experts(rows_in):
        return jnp.zeros(rows_in.shape, jnp.float32)

    partial_value = lax.cond(expert_side, serve_rows, skip_experts, rows)
    own_block = jnp.minimum(section, sections - 2)
    kept_part = lax.dynamic_slice_in_dim(partial_value, parity * half_width, half_width, 3)
    sent_part = lax.dynamic_slice_in_dim(partial_value, (1 - parity) * half_width, half_width, 3)
    summed = kept_part + swapped(sent_part, "dev", 0)
    landed = spread_2(summed, "sec", sections - 1)
    mine = lax.dynamic_index_in_dim(landed, own_block, 0, keepdims=False)
    returned = lax.all_to_all(mine, "dev", split_axis=0, concat_axis=0, tiled=True)
    result = jnp.einsum(
        "tec,ehck->thk",
        mixer,
        returned.reshape(experts, 2, capacity, half_width),
        precision=lax.Precision.HIGHEST,
    )
    result = result.reshape(token_count, model_width)
    result = jnp.where(expert_side, 0.0, result)
    return (attention_out, result.astype(jnp.bfloat16))


def solution(mesh):
    return jax.shard_map(
        per_device,
        mesh=mesh,
        in_specs=(
            P(("sec", "dev"), None),
            P(("sec", "dev"), None, None),
            P(("sec", "dev"), None, None, None),
            P(("sec", "dev")),
            P(("sec", "dev"), None),
            P(("sec", "dev"), None),
            P(("sec", "dev"), None),
            P(("sec", "dev"), None, None),
            P(("sec", "dev"), None, None),
        ),
        out_specs=(P(("sec", "dev"), None), P(("sec", "dev"), None)),
        check_vma=False,
    )
```

profile of v0, /device:TPU:0, one launch (start us, length us, event | category | flops | bytes accessed | tf_op | source)
XLA Modules:
  0.0 549.2 jit_solution(8833601591684362549)
XLA Ops:
  7.2 0.8 copy.34
  9.6 2.4 broadcast_in_dim.27
  12.0 2.4 broadcast_in_dim_reshape.2
  14.3 94.6 %all-gather.2.cloned.1.call-done = bf16[4,32,9,4096]{3,1,2,0:T(8,128)(2,1)} async-done(((bf16[1,32,9,4096]{3,1,2,0:T(8,128)(2,1)}), bf16[4,32,9,4096]{3,1,2,0:T(8,128)(2,1)}) %all-gather.2.cloned.1.call-update) | async-done | bytes 9437200 | tf_op jit(solution)/shard_map/all_gather | solution.py:118
  108.9 3.0 slice-done
  111.9 7.3 %copy.36 = bf16[3,32,9,4096]{3,0,2,1:T(4,128)(2,1)} copy(bf16[3,32,9,4096]{3,1,2,0:T(8,128)(2,1)S(1)} %slice-done) | data formatting | bytes 14155776 | tf_op jit(solution)/shard_map/slice | solution.py:119
  119.2 7.3 %all-to-all-start = ((bf16[3,32,9,4096]{3,0,2,1:T(4,128)(2,1)}), bf16[3,32,9,4096]{3,0,2,1:T(4,128)(2,1)}, u32[]{:S(2)}, u32[]{:S(2)}) async-start(bf16[3,32,9,4096]{3,0,2,1:T(4,128)(2,1)} %copy.36), calls=%async_computation | async-start | bytes 18874368 | tf_op jit(solution)/shard_map/all_to_all | solution.py:119
  126.6 119.2 %all-to-all-done = bf16[3,32,9,4096]{3,0,2,1:T(4,128)(2,1)} async-done(((bf16[3,32,9,4096]{3,0,2,1:T(4,128)(2,1)}), bf16[3,32,9,4096]{3,0,2,1:T(4,128)(2,1)}, u32[]{:S(2)}, u32[]{:S(2)}) %all-to-all-start) | async-done | bytes 7077920 | tf_op jit(solution)/shard_map/all_to_all | solution.py:119
  245.8 6.8 %conditional.3 = (f32[3,32,9,4096]{3,1,2,0:T(8,128)}) conditional(s32[]{:T(128)} %convert_element_type.38, () %tuple.22, (bf16[3,32,9,4096]{3,0,2,1:T(4,128)(2,1)}, bf16[1,4096,1536]{2,1,0:T(8,128)(2,1)}, bf16[1,768,4096]{2,1,0:T(8,128)(2,1)}) %tuple.23), branch_computations={%region_7.8_spmd, %region_8.9_spmd} | conditional | flops 16311435264 | bytes 84344840 | solution.py:138
  245.8 6.8 %broadcast.67 = f32[3,32,9,4096]{3,1,2,0:T(8,128)} broadcast(f32[]{:T(128)} %constant.58.clone), dimensions={} | broadcast | bytes 14155780 | tf_op jit(solution)/shard_map/broadcast.7
  252.6 6.8 %constant_dynamic-slice_fusion = f32[3,32,9,2048]{3,1,2,0:T(8,128)} fusion(f32[3,32,9,4096]{3,1,2,0:T(8,128)} %get-tuple-element.67, s32[]{:T(128)S(6)} %select_n.53), kind=kLoop, calls=%fused_computation.57 | loop fusion | bytes 14155780 | tf_op jit(solution)/shard_map/dynamic_slice | solution.py:141
  259.4 11.6 %collective-permute-done = f32[3,32,9,2048]{3,1,2,0:T(8,128)} collective-permute-done((f32[3,32,9,2048]{3,1,2,0:T(8,128)}, f32[3,32,9,2048]{3,1,2,0:T(8,128)}, u32[]{:S(2)}, u32[]{:S(2)}) %collective-permute-start) | collective-permute-done | bytes 7077920 | tf_op jit(solution)/shard_map/ppermute | solution.py:8
  271.1 10.3 %add_select_fusion = f32[3,32,9,2048]{3,1,2,0:T(8,128)} fusion(f32[3,32,9,2048]{3,1,2,0:T(8,128)} %collective-permute-done, f32[3,32,9,4096]{3,1,2,0:T(8,128)} %get-tuple-element.67, s32[]{:T(128)S(6)} %select_n.52, pred[]{:T(512)S(6)} %eq.51), kind=kLoop, calls=%fused_computation.30 | loop fusion | flops 3538944 | bytes 21233668 | tf_op jit(solution)/shard_map/jit(_where)/select_n | solution.py:12
  281.4 182.5 %all-reduce.2.cloned.1.call-done = f32[3,32,9,2048]{3,1,2,0:T(8,128)} async-done(((f32[3,32,9,2048]{3,1,2,0:T(8,128)}), f32[3,32,9,2048]{3,1,2,0:T(8,128)}) %all-reduce.2.cloned.1.call-update) | async-done | bytes 7077904 | tf_op jit(solution)/shard_map/psum | solution.py:13
  463.8 1.8 constant_dynamic-slice_fusion.1
  465.7 3.5 copy.54
  469.1 7.5 %all-to-all-start.1 = ((f32[32,9,2048]{2,1,0:T(8,128)}), f32[32,9,2048]{2,1,0:T(8,128)}, u32[]{:S(2)}, u32[]{:S(2)}) async-start(f32[32,9,2048]{2,1,0:T(8,128)} %bitcast.50), calls=%async_computation.1 | async-start | bytes 8388608 | tf_op jit(solution)/shard_map/all_to_all | solution.py:145
  477.4 4.5 conditional.2
  477.5 2.7 copy.32
  480.3 0.7 fusion.46
  482.0 48.1 %all-to-all-done.1 = f32[32,9,2048]{2,1,0:T(8,128)} async-done(((f32[32,9,2048]{2,1,0:T(8,128)}), f32[32,9,2048]{2,1,0:T(8,128)}, u32[]{:S(2)}, u32[]{:S(2)}) %all-to-all-start.1) | async-done | bytes 2359328 | tf_op jit(solution)/shard_map/all_to_all | solution.py:145
  530.1 4.0 copy.55
  534.2 3.1 dot_general.37
  537.3 5.1 fusion.34
  (46 shorter events, 3.4 us)
Async XLA Ops:
  7.2 2.0 copy-start
  7.2 101.8 %all-gather.2.cloned.1.call-start = ((), (), s32[]{:S(2)}) async-start(), calls=%async_computation.2 | async-start | bytes 11796480 | tf_op jit(solution)/shard_map/all_gather | solution.py:118
  108.9 3.0 slice-start
  119.2 126.6 %all-to-all-start = ((bf16[3,32,9,4096]{3,0,2,1:T(4,128)(2,1)}), bf16[3,32,9,4096]{3,0,2,1:T(4,128)(2,1)}, u32[]{:S(2)}, u32[]{:S(2)}) async-start(bf16[3,32,9,4096]{3,0,2,1:T(4,128)(2,1)} %copy.36), calls=%async_computation | async-start | bytes 18874368 | tf_op jit(solution)/shard_map/all_to_all | solution.py:119
  126.6 337.3 %all-reduce.2.cloned.1.call-start = ((), (), s32[]{:S(2)}) async-start(), calls=%async_computation.3 | async-start | bytes 14155776 | tf_op jit(solution)/shard_map/psum | solution.py:13
  259.4 11.6 %collective-permute-start = (f32[3,32,9,2048]{3,1,2,0:T(8,128)}, f32[3,32,9,2048]{3,1,2,0:T(8,128)}, u32[]{:S(2)}, u32[]{:S(2)}) collective-permute-start(f32[3,32,9,2048]{3,1,2,0:T(8,128)} %constant_dynamic-slice_fusion), channel_id=1, source_target_pairs={{0,1},{1,0},{2,3},{3,2},{4,5},{5,4},{6,7},{7,6},{8,9},{9,8},{10,11... | collective-permute-start | bytes 21233672 | tf_op jit(solution)/shard_map/ppermute | solution.py:8
  469.1 7.5 %copy-start.4 = (f32[12,8]{0,1:T(8,128)S(1)}, f32[12,8]{0,1:T(8,128)}, u32[]{:S(2)}) copy-start(f32[12,8]{0,1:T(8,128)} %param.19) | copy-start | bytes 1156
  469.1 8.3 %copy-start.2 = (bf16[2,8192]{1,0:T(2,128)(2,1)S(1)}, bf16[2,8192]{1,0:T(2,128)(2,1)}, u32[]{:S(2)}) copy-start(bf16[2,8192]{1,0:T(2,128)(2,1)} %param.13) | copy-start | bytes 98308
  469.1 8.3 %copy-start.5 = (bf16[2,4,256]{2,1,0:T(4,128)(2,1)S(1)}, bf16[2,4,256]{2,1,0:T(4,128)(2,1)}, u32[]{:S(2)}) copy-start(bf16[2,4,256]{2,1,0:T(4,128)(2,1)} %param.14) | copy-start | bytes 12292
  469.1 8.3 %copy-start.6 = (s32[2]{0:T(128)S(1)}, s32[2]{0:T(128)}, u32[]{:S(2)}) copy-start(s32[2]{0:T(128)} %param.16) | copy-start | bytes 28
  469.1 61.0 %all-to-all-start.1 = ((f32[32,9,2048]{2,1,0:T(8,128)}), f32[32,9,2048]{2,1,0:T(8,128)}, u32[]{:S(2)}, u32[]{:S(2)}) async-start(f32[32,9,2048]{2,1,0:T(8,128)} %bitcast.50), calls=%async_computation.1 | async-start | bytes 8388608 | tf_op jit(solution)/shard_map/all_to_all | solution.py:145
  482.0 55.3 %copy-start.3 = (bf16[2,8192]{1,0:T(2,128)(2,1)}, bf16[2,8192]{1,0:T(2,128)(2,1)S(1)}, u32[]{:S(2)}) copy-start(bf16[2,8192]{1,0:T(2,128)(2,1)S(1)} %get-tuple-element.66) | copy-start | bytes 98308
  530.1 12.2 %copy-start.1 = (bf16[12,4096]{1,0:T(8,128)(2,1)S(1)}, bf16[12,4096]{1,0:T(8,128)(2,1)}, u32[]{:S(2)}) copy-start(bf16[12,4096]{1,0:T(8,128)(2,1)} %param.17) | copy-start | bytes 294916
Sparse Core Ops, SparseCore 0:
  14.5 94.4 all-gather.1
  281.5 182.3 all-reduce.1
where the time goes:
time: 550 us; the launch traced here: 549 us
  waiting for transfers between devices  456 us (83%)
  local copies, waits for them, and re-layouts  45.5 us (8%)
  starting transfers between devices  14.9 us (3%)
  between operations  14.2 us (3%)
  other arithmetic  11 us (2%)
  matrix products  7.41 us (1%)
    psum x1, waiting for transfers between devices, spread_2(): return lax.psum(block, axis)  182 us
    all_to_all x1, waiting for transfers between devices, per_device(): lax.all_to_all(collected[:sections - 1], 'dev', split_axis=1, concat_axis...  119 us
    all_gather x1, waiting for transfers between devices, per_device(): collected = lax.all_gather(outgoing[None], 'sec', axis=0, tiled=True)  94.6 us
    all_to_all x1, waiting for transfers between devices, per_device(): lax.all_to_all(mine, 'dev', split_axis=0, concat_axis=0, tiled=True)  48.1 us
    ppermute x1, waiting for transfers between devices, swapped(): lax.ppermute(shard, axis, [(i, i ^ 1 << distance) for i in range(lax.axis...  11.6 us
  transfers between devices with their start and end apart: 5, of which 5 were waited for; matrix products, arithmetic and copies ran while one was open for 1% of the time, Pallas kernels for 0%

commit v1 on v0

v1 whole, which is shorter than its diff:
```python
import jax
import jax.numpy as jnp
from jax import lax
from jax.sharding import PartitionSpec as P

SIDE = 4
EXTRA = 128


def along(first, distance):
    pairs = []
    for i in range(2 * SIDE * SIDE):
        z, x, core = i // (2 * SIDE), i // 2 % SIDE, i % 2
        if first == (core == 0):
            x = (x + distance) % SIDE
        else:
            z = (z + distance) % SIDE
        pairs.append((i, (z * SIDE + x) * 2 + core))
    return pairs


def step_u(block, distance):
    return lax.ppermute(block, "dev", along(True, distance))


def step_v(block, distance):
    return lax.ppermute(block, "dev", along(False, distance))


def step_sec(block, distance):
    return lax.ppermute(block, "sec", [(i, (i + distance) % SIDE) for i in range(SIDE)])


def other_core(block):
    return lax.ppermute(block, "dev", [(i, i ^ 1) for i in range(2 * SIDE * SIDE)])


def attention_block(query, fresh_key_value, kv_cache, cache_lengths):
    count_req = query.shape[0]
    heads_kv = fresh_key_value.shape[1]
    head_size = fresh_key_value.shape[2] // 2
    group_size = query.shape[1] // (heads_kv * head_size)
    query_heads = query.reshape(count_req, heads_kv, group_size, head_size)
    score_scale = head_size ** (-0.5)
    scores = (
        jnp.einsum(
            "rghd,rtgd->rght",
            query_heads,
            kv_cache[..., :head_size],
            preferred_element_type=jnp.float32,
        )
        * score_scale
    )
    valid = jnp.arange(kv_cache.shape[1], dtype=jnp.int32)[None, :] < cache_lengths[:, None]
    scores = jnp.where(valid[:, None, None, :], scores, -jnp.inf)
    own_score = (
        jnp.einsum(
            "rghd,rgd->rgh",
            query_heads,
            fresh_key_value[..., :head_size],
            preferred_element_type=jnp.float32,
        )
        * score_scale
    )
    peak = jnp.maximum(jnp.max(scores, axis=-1), own_score)
    weights = jnp.exp(scores - peak[..., None])
    own_weight = jnp.exp(own_score - peak)
    denominator = jnp.sum(weights, axis=-1) + own_weight
    own_low = lax.optimization_barrier(own_weight.astype(jnp.bfloat16)).astype(jnp.float32)
    mixture = jnp.einsum(
        "rght,rtgd->rghd",
        weights.astype(jnp.bfloat16),
        kv_cache[..., head_size:],
        preferred_element_type=jnp.float32,
    )
    mixture = (
        mixture
        + own_low[..., None] * fresh_key_value[..., head_size:].astype(jnp.float32)[:, :, None, :]
    )
    return (mixture / denominator[..., None]).astype(jnp.bfloat16).reshape(count_req, -1)


def token_rows(hidden, routes, gates, experts):
    combine = gates / jnp.sum(gates, axis=1, keepdims=True)
    named = routes[:, :, None] == jnp.arange(experts, dtype=jnp.int32)[None, None, :]
    share = jnp.sum(jnp.where(named, combine[:, :, None], 0.0), axis=1)
    terms = []
    for _ in range(3):
        term = lax.reduce_precision(share, 8, 7)
        terms.append(term.astype(jnp.bfloat16))
        share = share - term
    fill = jnp.zeros((hidden.shape[0], EXTRA - 3 * experts), jnp.bfloat16)
    return jnp.concatenate([hidden, *terms, fill], axis=1)


def experts_on(rows, picks, weights):
    width = rows.shape[1] - EXTRA
    share = jnp.sum(
        jnp.where(picks, rows[:, width:].astype(jnp.float32), 0.0), axis=1, keepdims=True
    )
    total = None
    for gate_up, down in weights:
        inner = down.shape[0]
        projected = jnp.dot(rows[:, :width], gate_up, preferred_element_type=jnp.float32)
        act = (jax.nn.silu(projected[:, :inner]) * projected[:, inner:]).astype(jnp.bfloat16)
        part = jnp.dot(act, down, preferred_element_type=jnp.float32)
        total = part if total is None else total + part
    return (total * share).astype(jnp.bfloat16)


def per_device(
    query, fresh_key_value, kv_cache, cache_lengths, hidden, routes, gates, w_gate_up, w_down
):
    sections = lax.axis_size("sec")
    section = lax.axis_index("sec")
    experts = lax.axis_size("dev") // 2
    expert = lax.axis_index("dev") // 2
    expert_side = section == sections - 1
    count = hidden.shape[0]
    f32 = jnp.float32

    gate_up, down = w_gate_up[0], w_down[0]
    weights = ((gate_up, down), (other_core(gate_up), other_core(down)))

    packed = token_rows(hidden, routes, gates, experts)
    block = jnp.concatenate([step_sec(packed, sections - 1 - s) for s in range(sections - 1)], axis=0)

    group = jnp.concatenate([block, step_u(block, 1), step_u(block, -1), step_u(block, 2)], axis=0)
    before, after = step_v(group, 1), step_v(group, -1)
    half = group.shape[0] // 2
    across = jnp.concatenate([step_v(before[:half], 1), step_v(after[half:], -1)], axis=0)

    attention_out = attention_block(query, fresh_key_value, kv_cache, cache_lengths)
    attention_out = jnp.where(expert_side, jnp.zeros_like(attention_out), attention_out)

    column = lax.broadcasted_iota(jnp.int32, (1, EXTRA), 1)
    picks = (column % experts == expert) & (column < 3 * experts)
    size = group.shape[0]
    y_one = experts_on(jnp.concatenate([group, before], axis=0), picks, weights)
    y_two = experts_on(jnp.concatenate([after, across], axis=0), picks, weights)
    y_own, y_before, y_after, y_across = y_one[:size], y_one[size:], y_two[:size], y_two[size:]

    to_after, to_before = step_v(y_across[:half], 1), step_v(y_across[half:], -1)
    y_after = jnp.concatenate(
        [(y_after[:half].astype(f32) + to_after.astype(f32)).astype(jnp.bfloat16), y_after[half:]], axis=0
    )
    y_before = jnp.concatenate(
        [y_before[:half], (y_before[half:].astype(f32) + to_before.astype(f32)).astype(jnp.bfloat16)], axis=0
    )
    summed = y_own.astype(f32) + step_v(y_after, 1).astype(f32) + step_v(y_before, -1).astype(f32)
    held = sections * count - count
    low = summed.astype(jnp.bfloat16)
    total = (
        summed[:held]
        + step_u(low[held : 2 * held], -1).astype(f32)
        + step_u(low[2 * held : 3 * held], 1).astype(f32)
        + step_u(low[3 * held :], 2).astype(f32)
    ).astype(jnp.bfloat16)

    result = jnp.zeros((count, total.shape[1]), jnp.bfloat16)
    for s in range(sections - 1):
        back = step_sec(total[s * count : (s + 1) * count], s + 1)
        result = jnp.where(section == s, back, result)
    return attention_out, result


def solution(mesh):
    return jax.shard_map(
        per_device,
        mesh=mesh,
        in_specs=(
            P(("sec", "dev"), None),
            P(("sec", "dev"), None, None),
            P(("sec", "dev"), None, None, None),
            P(("sec", "dev")),
            P(("sec", "dev"), None),
            P(("sec", "dev"), None),
            P(("sec", "dev"), None),
            P(("sec", "dev"), None, None),
            P(("sec", "dev"), None, None),
        ),
        out_specs=(P(("sec", "dev"), None), P(("sec", "dev"), None)),
        check_vma=False,
    )
```

time: 550 us -> 184 us (0.33)
  waiting for transfers between devices: 456 us -> 55.1 us
  matrix products: 7.41 us -> 43.7 us
  starting transfers between devices: 14.9 us -> 28.8 us
  between operations: 14.2 us -> 1.08 us
    psum x1 -> x0, waiting for transfers between devices: 182 us -> none  [spread_2(): return lax.psum(block, axis)]
    all_to_all x2 -> x0, waiting for transfers between devices: 167 us -> none  [the longest x1 119 us: per_device(): lax.all_to_all(collected[:sections - 1], 'dev', split_axis=1, concat_axis...]
    all_gather x1 -> x0, waiting for transfers between devices: 94.6 us -> none  [per_device(): collected = lax.all_gather(outgoing[None], 'sec', axis=0, tiled=True)]
    ppermute x1 -> x22, waiting for transfers between devices: 11.6 us -> 55.1 us  [the longest x8 23 us: step_v(): return lax.ppermute(block, 'dev', along(False, distance))]
    dot_general x4 -> x8, matrix products: 6.07 us -> 42.3 us  [the longest x4 25.3 us: experts_on(): jnp.dot(rows[:, :width], gate_up, preferred_element_type=jnp.float32)]
    concatenate x0 -> x4, local copies, waits for them, and re-layouts: none -> 33.4 us  [the longest x1 18.3 us: per_device(): y_one = experts_on(jnp.concatenate([group, before], axis=0), picks, weights)]
    ppermute x1 -> x22, starting transfers between devices: 0.01 us -> 28.8 us  [the longest x8 13 us: step_v(): return lax.ppermute(block, 'dev', along(False, distance))]
    all_to_all x2 -> x0, starting transfers between devices: 14.8 us -> none  [the longest x1 7.5 us: per_device(): lax.all_to_all(mine, 'dev', split_axis=0, concat_axis=0, tiled=True)]
  transfers between devices with their start and end apart: 5 -> 22, of which waited for: 5 -> 14; matrix products, arithmetic and copies ran while one was open for 1% -> 46% of each run, Pallas kernels for 0% -> 0%
where the time goes in v1:
time: 184 us; the launch traced here: 182 us
  waiting for transfers between devices  55.1 us (30%)
  local copies, waits for them, and re-layouts  45.4 us (25%)
  matrix products  43.7 us (24%)
  starting transfers between devices  28.8 us (16%)
  other arithmetic  7.66 us (4%)
    dot_general x4, matrix products, experts_on(): jnp.dot(rows[:, :width], gate_up, preferred_element_type=jnp.float32)  25.3 us
    ppermute x8, waiting for transfers between devices, step_v(): return lax.ppermute(block, 'dev', along(False, distance))  23 us
    concatenate x1, local copies, waits for them, and re-layouts, per_device(): y_one = experts_on(jnp.concatenate([group, before], axis=0), picks, weights)  18.3 us
    ppermute x6, waiting for transfers between devices, step_u(): return lax.ppermute(block, 'dev', along(True, distance))  18.3 us
    dot_general x4, matrix products, experts_on(): part = jnp.dot(act, down, preferred_element_type=jnp.float32)  17 us
    ppermute x6, waiting for transfers between devices, step_sec(): lax.ppermute(block, 'sec', [(i, (i + distance) % SIDE) for i in range(SID...  13.8 us
    ppermute x8, starting transfers between devices, step_v(): return lax.ppermute(block, 'dev', along(False, distance))  13 us
    concatenate x1, local copies, waits for them, and re-layouts, per_device(): jnp.concatenate([block, step_u(block, 1), step_u(block, -1), step_u(block...  12.8 us
  transfers between devices with their start and end apart: 22, of which 14 were waited for; matrix products, arithmetic and copies ran while one was open for 46% of the time, Pallas kernels for 0%

profile of v1, /device:TPU:0, one launch (start us, length us, event | category | flops | bytes accessed | tf_op | source)
XLA Modules:
  0.0 181.7 jit_solution(10628557356812162053)
XLA Ops:
  4.1 3.1 %collective-permute-start = (bf16[12,4224]{1,0:T(8,128)(2,1)S(1)}, bf16[12,4224]{1,0:T(8,128)(2,1)S(1)}, u32[]{:S(2)}, u32[]{:S(2)}) collective-permute-start(bf16[12,4224]{1,0:T(8,128)(2,1)S(1)} %concatenate.23), channel_id=1, source_target_pairs={{0,96},{32,0},{64,32},{96,64},{1,97},{33,1},{65,33},{97,65},{2,98}... | collective-permute-start | bytes 304136 | tf_op jit(solution)/shard_map/ppermute | solution.py:31
  8.8 4.8 %collective-permute-done = bf16[12,4224]{1,0:T(8,128)(2,1)S(1)} collective-permute-done((bf16[12,4224]{1,0:T(8,128)(2,1)S(1)}, bf16[12,4224]{1,0:T(8,128)(2,1)S(1)}, u32[]{:S(2)}, u32[]{:S(2)}) %collective-permute-start) | collective-permute-done | bytes 101408 | tf_op jit(solution)/shard_map/ppermute | solution.py:31
  22.6 3.3 %collective-permute-done.3 = bf16[36,4224]{1,0:T(8,128)(2,1)S(1)} collective-permute-done((bf16[36,4224]{1,0:T(8,128)(2,1)S(1)}, bf16[36,4224]{1,0:T(8,128)(2,1)S(1)}, u32[]{:S(2)}, u32[]{:S(2)}) %collective-permute-start.3) | collective-permute-done | bytes 304160 | tf_op jit(solution)/shard_map/ppermute | solution.py:23
  25.9 3.2 %collective-permute-done.4 = bf16[36,4224]{1,0:T(8,128)(2,1)S(1)} collective-permute-done((bf16[36,4224]{1,0:T(8,128)(2,1)S(1)}, bf16[36,4224]{1,0:T(8,128)(2,1)S(1)}, u32[]{:S(2)}, u32[]{:S(2)}) %collective-permute-start.4) | collective-permute-done | bytes 304160 | tf_op jit(solution)/shard_map/ppermute | solution.py:23
  30.5 12.8 %concatenate.25 = bf16[144,4224]{1,0:T(8,128)(2,1)} concatenate(bf16[12,4224]{1,0:T(8,128)(2,1)S(1)} %collective-permute-done, bf16[12,4224]{1,0:T(8,128)(2,1)S(1)} %collective-permute-done.1, bf16[12,4224]{1,0:T(8,128)(2,1)S(1)} %collective-permute-done.2, bf16[36,4224]{1,0:T(8,128)(2,1)S(1)} %collective-permute-done.3, bf16[36,4224]{1,0:T(8,128)(2,1)S(1)} %collective-permute-done.4, ...), dimensions={0} | concatenate | bytes 2433024 | tf_op jit(solution)/shard_map/concatenate | solution.py:128
  45.3 2.2 %collective-permute-start.9 = (bf16[144,4224]{1,0:T(8,128)(2,1)}, bf16[144,4224]{1,0:T(8,128)(2,1)S(1)}, u32[]{:S(2)}, u32[]{:S(2)}) collective-permute-start(bf16[144,4224]{1,0:T(8,128)(2,1)} %concatenate.25), channel_id=1, source_target_pairs={{0,24},{1,7},{2,26},{3,1},{4,28},{5,3},{6,30},{7,5},{8,0},{9,15},{... | collective-permute-start | bytes 3649544 | tf_op jit(solution)/shard_map/ppermute | solution.py:27
  47.5 14.7 %collective-permute-done.6 = bf16[144,4224]{1,0:T(8,128)(2,1)S(1)} collective-permute-done((bf16[144,4224]{1,0:T(8,128)(2,1)}, bf16[144,4224]{1,0:T(8,128)(2,1)S(1)}, u32[]{:S(2)}, u32[]{:S(2)}) %collective-permute-start.6) | collective-permute-done | bytes 1216544 | tf_op jit(solution)/shard_map/ppermute | solution.py:27
  64.0 3.2 %collective-permute-start.11 = (bf16[72,4224]{1,0:T(8,128)(2,1)}, bf16[72,4224]{1,0:T(8,128)(2,1)}, u32[]{:S(2)}, u32[]{:S(2)}) collective-permute-start(bf16[72,4224]{1,0:T(8,128)(2,1)} %slice.147), channel_id=1, source_target_pairs={{0,24},{1,7},{2,26},{3,1},{4,28},{5,3},{6,30},{7,5},{8,0},{9,15},{... | collective-permute-start | bytes 1824776 | tf_op jit(solution)/shard_map/ppermute | solution.py:27
  67.2 18.3 %concatenate.26 = bf16[288,4224]{1,0:T(8,128)(2,1)} concatenate(bf16[12,4224]{1,0:T(8,128)(2,1)} %copy-done.4, bf16[12,4224]{1,0:T(8,128)(2,1)} %copy-done.5, bf16[12,4224]{1,0:T(8,128)(2,1)} %copy-done.6, bf16[36,4224]{1,0:T(8,128)(2,1)S(1)} %collective-permute-done.3, bf16[36,4224]{1,0:T(8,128)(2,1)S(1)} %collective-permute-done.4, ...), dimensions={0} | concatenate | bytes 4866048 | tf_op jit(solution)/shard_map/concatenate | solution.py:139
  85.5 7.6 %fusion.14 = f32[288,1536]{1,0:T(8,128)S(1)} fusion(bf16[288,4224]{1,0:T(8,128)(2,1)} %concatenate.26, bf16[1,4096,1536]{2,1,0:T(8,128)(2,1)} %param.16), kind=kOutput, calls=%fused_computation.17 | convolution fusion | flops 3623878656 | bytes 16711680 | tf_op jit(solution)/shard_map/dot_general | solution.py:104
  93.2 5.0 %fusion.43 = f32[288,4096]{1,0:T(8,128)S(1)} fusion(f32[288,1536]{1,0:T(8,128)S(1)} %fusion.14, bf16[1,768,4096]{2,1,0:T(8,128)(2,1)} %param.17), kind=kOutput, calls=%fused_computation.44 | convolution fusion | flops 1813266432 | bytes 12779520 | tf_op jit(solution)/shard_map/dot_general | solution.py:106
  101.1 3.9 %fusion.10 = f32[288,1536]{1,0:T(8,128)S(1)} fusion(bf16[288,4224]{1,0:T(8,128)(2,1)S(1)} %constant_dynamic-update-slice_fusion, bf16[1,4096,1536]{2,1,0:T(8,128)(2,1)S(1)} %bitcast.37), kind=kOutput, calls=%fused_computation.13 | convolution fusion | flops 3623878656 | bytes 16711680 | tf_op jit(solution)/shard_map/dot_general | solution.py:104
  107.2 6.9 %fusion.8 = f32[288,1536]{1,0:T(8,128)S(1)} fusion(bf16[4096,1536]{1,0:T(8,128)(2,1)} %collective-permute-done.7, bf16[288,4224]{1,0:T(8,128)(2,1)S(1)} %constant_dynamic-update-slice_fusion), kind=kOutput, calls=%fused_computation.11 | convolution fusion | flops 3623878656 | bytes 16711680 | tf_op jit(solution)/shard_map/dot_general | solution.py:104
  114.1 5.0 %fusion.3 = bf16[288,4096]{1,0:T(8,128)(2,1)S(1)} fusion(f32[288,4096]{1,0:T(8,128)S(1)} %fusion.46, bf16[768,4096]{1,0:T(8,128)(2,1)} %collective-permute-done.8, f32[288]{0:T(512)S(1)} %get-tuple-element.3, f32[288,1536]{1,0:T(8,128)S(1)} %fusion.8), kind=kOutput, calls=%fused_computation.5 | convolution fusion | flops 1816805376 | bytes 15139968 | tf_op jit(solution)/shard_map/dot_general | solution.py:106
  119.3 3.2 %collective-permute-start.14 = (bf16[72,4096]{1,0:T(8,128)(2,1)S(1)}, bf16[72,4096]{1,0:T(8,128)(2,1)S(1)}, u32[]{:S(2)}, u32[]{:S(2)}) collective-permute-start(bf16[72,4096]{1,0:T(8,128)(2,1)S(1)} %get-tuple-element.9), channel_id=1, source_target_pairs={{0,24},{1,7},{2,26},{3,1},{4,28},{5,3},{6,30},{7,5},{8,0},{9,15},{... | collective-permute-start | bytes 1769480 | tf_op jit(solution)/shard_map/ppermute | solution.py:27
  122.6 6.9 %fusion.12 = f32[288,1536]{1,0:T(8,128)S(1)} fusion(bf16[4096,1536]{1,0:T(8,128)(2,1)} %collective-permute-done.7, bf16[288,4224]{1,0:T(8,128)(2,1)S(1)} %copy-done), kind=kOutput, calls=%fused_computation.15 | convolution fusion | flops 3623878656 | bytes 16711680 | tf_op jit(solution)/shard_map/dot_general | solution.py:104
  129.4 5.0 %fusion.2 = bf16[288,4096]{1,0:T(8,128)(2,1)S(1)} fusion(f32[288,4096]{1,0:T(8,128)S(1)} %fusion.43, bf16[768,4096]{1,0:T(8,128)(2,1)} %collective-permute-done.8, f32[288]{0:T(512)S(1)} %get-tuple-element.2, f32[288,1536]{1,0:T(8,128)S(1)} %fusion.12), kind=kOutput, calls=%fused_computation.4 | convolution fusion | flops 1816805376 | bytes 15139968 | tf_op jit(solution)/shard_map/dot_general | solution.py:106
  137.1 2.2 %collective-permute-start.15 = (bf16[144,4096]{1,0:T(8,128)(2,1)}, bf16[144,4096]{1,0:T(8,128)(2,1)}, u32[]{:S(2)}, u32[]{:S(2)}) collective-permute-start(bf16[144,4096]{1,0:T(8,128)(2,1)} %pad_maximum_fusion.1), channel_id=1, source_target_pairs={{0,24},{1,7},{2,26},{3,1},{4,28},{5,3},{6,30},{7,5},{8,0},{9,15},{... | collective-permute-start | bytes 3538952 | tf_op jit(solution)/shard_map/ppermute | solution.py:27
  139.6 4.0 %fusion.70 = (bf16[2,1024,4,128]{3,2,1,0:T(4,128)(2,1)S(1)}, bf16[2,1024,4,128]{3,2,1,0:T(4,128)(2,1)}) fusion(bf16[2,1024,4,256]{3,2,1,0:T(4,128)(2,1)} %param.11), kind=kLoop, calls=%fused_computation.88 | loop fusion | bytes 8388608 | tf_op jit(solution)/shard_map/slice | solution.py:49
  144.3 8.0 %collective-permute-done.13 = bf16[144,4096]{1,0:T(8,128)(2,1)S(1)} collective-permute-done((bf16[144,4096]{1,0:T(8,128)(2,1)S(1)}, bf16[144,4096]{1,0:T(8,128)(2,1)S(1)}, u32[]{:S(2)}, u32[]{:S(2)}) %collective-permute-start.13) | collective-permute-done | bytes 1179680 | tf_op jit(solution)/shard_map/ppermute | solution.py:27
  153.6 2.2 %fusion.69 = (bf16[144,4096]{1,0:T(8,128)(2,1)S(1)}, f32[144,4096]{1,0:T(8,128)S(1)}) fusion(bf16[144,4096]{1,0:T(8,128)(2,1)} %collective-permute-done.15, bf16[144,4096]{1,0:T(8,128)(2,1)} %copy-done.7, bf16[288,4096]{1,0:T(8,128)(2,1)S(1)} %copy-done.2), kind=kLoop, calls=%fused_computation.87 | loop fusion | flops 3538944 | bytes 7077888 | tf_op jit(solution)/shard_map/convert_element_type | solution.py:152
  156.8 2.3 %collective-permute-start.16 = (bf16[36,4096]{1,0:T(8,128)(2,1)}, bf16[36,4096]{1,0:T(8,128)(2,1)S(1)}, u32[]{:S(2)}, u32[]{:S(2)}) collective-permute-start(bf16[36,4096]{1,0:T(8,128)(2,1)} %get-tuple-element.11), channel_id=1, source_target_pairs={{0,6},{1,25},{2,0},{3,27},{4,2},{5,29},{6,4},{7,31},{8,14},{9,1},{... | collective-permute-start | bytes 884744 | tf_op jit(solution)/shard_map/ppermute | solution.py:23
  160.9 3.3 %collective-permute-done.16 = bf16[36,4096]{1,0:T(8,128)(2,1)S(1)} collective-permute-done((bf16[36,4096]{1,0:T(8,128)(2,1)}, bf16[36,4096]{1,0:T(8,128)(2,1)S(1)}, u32[]{:S(2)}, u32[]{:S(2)}) %collective-permute-start.16) | collective-permute-done | bytes 294944 | tf_op jit(solution)/shard_map/ppermute | solution.py:23
  164.1 7.1 %collective-permute-done.17 = bf16[36,4096]{1,0:T(8,128)(2,1)} collective-permute-done((bf16[36,4096]{1,0:T(8,128)(2,1)}, bf16[36,4096]{1,0:T(8,128)(2,1)}, u32[]{:S(2)}, u32[]{:S(2)}) %collective-permute-start.17) | collective-permute-done | bytes 294944 | tf_op jit(solution)/shard_map/ppermute | solution.py:23
  (103 shorter events, 42.4 us)
Async XLA Ops:
  0.6 46.9 %copy-start.9 = (bf16[2,4,256]{2,1,0:T(4,128)(2,1)S(1)}, bf16[2,4,256]{2,1,0:T(4,128)(2,1)}, u32[]{:S(2)}) copy-start(bf16[2,4,256]{2,1,0:T(4,128)(2,1)} %param.10) | copy-start | bytes 12292
  0.6 106.5 %collective-permute-start.7 = (bf16[4096,1536]{1,0:T(8,128)(2,1)}, bf16[4096,1536]{1,0:T(8,128)(2,1)}, u32[]{:S(2)}, u32[]{:S(2)}) collective-permute-start(bf16[4096,1536]{1,0:T(8,128)(2,1)} %bitcast.35), channel_id=1, source_target_pairs={{0,1},{1,0},{2,3},{3,2},{4,5},{5,4},{6,7},{7,6},{8,9},{9,8},{10,11... | collective-permute-start | bytes 37748744 | tf_op jit(solution)/shard_map/ppermute | solution.py:35
  4.1 9.5 %collective-permute-start = (bf16[12,4224]{1,0:T(8,128)(2,1)S(1)}, bf16[12,4224]{1,0:T(8,128)(2,1)S(1)}, u32[]{:S(2)}, u32[]{:S(2)}) collective-permute-start(bf16[12,4224]{1,0:T(8,128)(2,1)S(1)} %concatenate.23), channel_id=1, source_target_pairs={{0,96},{32,0},{64,32},{96,64},{1,97},{33,1},{65,33},{97,65},{2,98}... | collective-permute-start | bytes 304136 | tf_op jit(solution)/shard_map/ppermute | solution.py:31
  7.2 8.0 %collective-permute-start.1 = (bf16[12,4224]{1,0:T(8,128)(2,1)S(1)}, bf16[12,4224]{1,0:T(8,128)(2,1)S(1)}, u32[]{:S(2)}, u32[]{:S(2)}) collective-permute-start(bf16[12,4224]{1,0:T(8,128)(2,1)S(1)} %concatenate.23), channel_id=1, source_target_pairs={{0,64},{32,96},{64,0},{96,32},{1,65},{33,97},{65,1},{97,33},{2,66}... | collective-permute-start | bytes 304136 | tf_op jit(solution)/shard_map/ppermute | solution.py:31
  7.9 9.5 %collective-permute-start.2 = (bf16[12,4224]{1,0:T(8,128)(2,1)S(1)}, bf16[12,4224]{1,0:T(8,128)(2,1)S(1)}, u32[]{:S(2)}, u32[]{:S(2)}) collective-permute-start(bf16[12,4224]{1,0:T(8,128)(2,1)S(1)} %concatenate.23), channel_id=1, source_target_pairs={{0,32},{32,64},{64,96},{96,0},{1,33},{33,65},{65,97},{97,1},{2,34}... | collective-permute-start | bytes 304136 | tf_op jit(solution)/shard_map/ppermute | solution.py:31
  13.6 29.7 %copy-start.4 = (bf16[12,4224]{1,0:T(8,128)(2,1)}, bf16[12,4224]{1,0:T(8,128)(2,1)S(1)}, u32[]{:S(2)}) copy-start(bf16[12,4224]{1,0:T(8,128)(2,1)S(1)} %collective-permute-done) | copy-start | bytes 304132
  17.4 8.5 %collective-permute-start.3 = (bf16[36,4224]{1,0:T(8,128)(2,1)S(1)}, bf16[36,4224]{1,0:T(8,128)(2,1)S(1)}, u32[]{:S(2)}, u32[]{:S(2)}) collective-permute-start(bf16[36,4224]{1,0:T(8,128)(2,1)S(1)} %pad_maximum_fusion.2), channel_id=1, source_target_pairs={{0,2},{1,9},{2,4},{3,11},{4,6},{5,13},{6,0},{7,15},{8,10},{9,17},{... | collective-permute-start | bytes 912392 | tf_op jit(solution)/shard_map/ppermute | solution.py:23
  19.0 10.1 %collective-permute-start.4 = (bf16[36,4224]{1,0:T(8,128)(2,1)S(1)}, bf16[36,4224]{1,0:T(8,128)(2,1)S(1)}, u32[]{:S(2)}, u32[]{:S(2)}) collective-permute-start(bf16[36,4224]{1,0:T(8,128)(2,1)S(1)} %pad_maximum_fusion.2), channel_id=1, source_target_pairs={{0,6},{1,25},{2,0},{3,27},{4,2},{5,29},{6,4},{7,31},{8,14},{9,1},{... | collective-permute-start | bytes 912392 | tf_op jit(solution)/shard_map/ppermute | solution.py:23
  20.7 9.8 %collective-permute-start.5 = (bf16[36,4224]{1,0:T(8,128)(2,1)S(1)}, bf16[36,4224]{1,0:T(8,128)(2,1)S(1)}, u32[]{:S(2)}, u32[]{:S(2)}) collective-permute-start(bf16[36,4224]{1,0:T(8,128)(2,1)S(1)} %pad_maximum_fusion.2), channel_id=1, source_target_pairs={{0,4},{1,17},{2,6},{3,19},{4,0},{5,21},{6,2},{7,23},{8,12},{9,25},... | collective-permute-start | bytes 912392 | tf_op jit(solution)/shard_map/ppermute | solution.py:23
  43.3 18.9 %collective-permute-start.6 = (bf16[144,4224]{1,0:T(8,128)(2,1)}, bf16[144,4224]{1,0:T(8,128)(2,1)S(1)}, u32[]{:S(2)}, u32[]{:S(2)}) collective-permute-start(bf16[144,4224]{1,0:T(8,128)(2,1)} %concatenate.25), channel_id=1, source_target_pairs={{0,8},{1,3},{2,10},{3,5},{4,12},{5,7},{6,14},{7,1},{8,16},{9,11},{... | collective-permute-start | bytes 3649544 | tf_op jit(solution)/shard_map/ppermute | solution.py:27
  45.3 17.8 %collective-permute-start.9 = (bf16[144,4224]{1,0:T(8,128)(2,1)}, bf16[144,4224]{1,0:T(8,128)(2,1)S(1)}, u32[]{:S(2)}, u32[]{:S(2)}) collective-permute-start(bf16[144,4224]{1,0:T(8,128)(2,1)} %concatenate.25), channel_id=1, source_target_pairs={{0,24},{1,7},{2,26},{3,1},{4,28},{5,3},{6,30},{7,5},{8,0},{9,15},{... | collective-permute-start | bytes 3649544 | tf_op jit(solution)/shard_map/ppermute | solution.py:27
  47.5 66.6 %collective-permute-start.8 = (bf16[768,4096]{1,0:T(8,128)(2,1)}, bf16[768,4096]{1,0:T(8,128)(2,1)}, u32[]{:S(2)}, u32[]{:S(2)}) collective-permute-start(bf16[768,4096]{1,0:T(8,128)(2,1)} %bitcast.38), channel_id=1, source_target_pairs={{0,1},{1,0},{2,3},{3,2},{4,5},{5,4},{6,7},{7,6},{8,9},{9,8},{10,11... | collective-permute-start | bytes 18874376 | tf_op jit(solution)/shard_map/ppermute | solution.py:35
  63.1 35.3 %collective-permute-start.10 = (bf16[72,4224]{1,0:T(8,128)(2,1)}, bf16[72,4224]{1,0:T(8,128)(2,1)}, u32[]{:S(2)}, u32[]{:S(2)}) collective-permute-start(bf16[72,4224]{1,0:T(8,128)(2,1)} %slice.146), channel_id=1, source_target_pairs={{0,8},{1,3},{2,10},{3,5},{4,12},{5,7},{6,14},{7,1},{8,16},{9,11},{... | collective-permute-start | bytes 1824776 | tf_op jit(solution)/shard_map/ppermute | solution.py:27
  64.0 35.7 %collective-permute-start.11 = (bf16[72,4224]{1,0:T(8,128)(2,1)}, bf16[72,4224]{1,0:T(8,128)(2,1)}, u32[]{:S(2)}, u32[]{:S(2)}) collective-permute-start(bf16[72,4224]{1,0:T(8,128)(2,1)} %slice.147), channel_id=1, source_target_pairs={{0,24},{1,7},{2,26},{3,1},{4,28},{5,3},{6,30},{7,5},{8,0},{9,15},{... | collective-permute-start | bytes 1824776 | tf_op jit(solution)/shard_map/ppermute | solution.py:27
  119.3 15.2 %collective-permute-start.12 = (bf16[72,4096]{1,0:T(8,128)(2,1)S(1)}, bf16[72,4096]{1,0:T(8,128)(2,1)S(1)}, u32[]{:S(2)}, u32[]{:S(2)}) collective-permute-start(bf16[72,4096]{1,0:T(8,128)(2,1)S(1)} %get-tuple-element.8), channel_id=1, source_target_pairs={{0,8},{1,3},{2,10},{3,5},{4,12},{5,7},{6,14},{7,1},{8,16},{9,11},{... | collective-permute-start | bytes 1769480 | tf_op jit(solution)/shard_map/ppermute | solution.py:27
  119.3 15.5 %collective-permute-start.14 = (bf16[72,4096]{1,0:T(8,128)(2,1)S(1)}, bf16[72,4096]{1,0:T(8,128)(2,1)S(1)}, u32[]{:S(2)}, u32[]{:S(2)}) collective-permute-start(bf16[72,4096]{1,0:T(8,128)(2,1)S(1)} %get-tuple-element.9), channel_id=1, source_target_pairs={{0,24},{1,7},{2,26},{3,1},{4,28},{5,3},{6,30},{7,5},{8,0},{9,15},{... | collective-permute-start | bytes 1769480 | tf_op jit(solution)/shard_map/ppermute | solution.py:27
  134.8 17.5 %collective-permute-start.13 = (bf16[144,4096]{1,0:T(8,128)(2,1)S(1)}, bf16[144,4096]{1,0:T(8,128)(2,1)S(1)}, u32[]{:S(2)}, u32[]{:S(2)}) collective-permute-start(bf16[144,4096]{1,0:T(8,128)(2,1)S(1)} %pad_maximum_fusion), channel_id=1, source_target_pairs={{0,8},{1,3},{2,10},{3,5},{4,12},{5,7},{6,14},{7,1},{8,16},{9,11},{... | collective-permute-start | bytes 3538952 | tf_op jit(solution)/shard_map/ppermute | solution.py:27
  137.1 16.5 %collective-permute-start.15 = (bf16[144,4096]{1,0:T(8,128)(2,1)}, bf16[144,4096]{1,0:T(8,128)(2,1)}, u32[]{:S(2)}, u32[]{:S(2)}) collective-permute-start(bf16[144,4096]{1,0:T(8,128)(2,1)} %pad_maximum_fusion.1), channel_id=1, source_target_pairs={{0,24},{1,7},{2,26},{3,1},{4,28},{5,3},{6,30},{7,5},{8,0},{9,15},{... | collective-permute-start | bytes 3538952 | tf_op jit(solution)/shard_map/ppermute | solution.py:27
  156.8 7.3 %collective-permute-start.16 = (bf16[36,4096]{1,0:T(8,128)(2,1)}, bf16[36,4096]{1,0:T(8,128)(2,1)S(1)}, u32[]{:S(2)}, u32[]{:S(2)}) collective-permute-start(bf16[36,4096]{1,0:T(8,128)(2,1)} %get-tuple-element.11), channel_id=1, source_target_pairs={{0,6},{1,25},{2,0},{3,27},{4,2},{5,29},{6,4},{7,31},{8,14},{9,1},{... | collective-permute-start | bytes 884744 | tf_op jit(solution)/shard_map/ppermute | solution.py:23
  159.1 12.1 %collective-permute-start.17 = (bf16[36,4096]{1,0:T(8,128)(2,1)}, bf16[36,4096]{1,0:T(8,128)(2,1)}, u32[]{:S(2)}, u32[]{:S(2)}) collective-permute-start(bf16[36,4096]{1,0:T(8,128)(2,1)} %get-tuple-element.13), channel_id=1, source_target_pairs={{0,2},{1,9},{2,4},{3,11},{4,6},{5,13},{6,0},{7,15},{8,10},{9,17},{... | collective-permute-start | bytes 884744 | tf_op jit(solution)/shard_map/ppermute | solution.py:23
  159.1 12.1 %collective-permute-start.18 = (bf16[36,4096]{1,0:T(8,128)(2,1)S(1)}, bf16[36,4096]{1,0:T(8,128)(2,1)}, u32[]{:S(2)}, u32[]{:S(2)}) collective-permute-start(bf16[36,4096]{1,0:T(8,128)(2,1)S(1)} %get-tuple-element.12), channel_id=1, source_target_pairs={{0,4},{1,17},{2,6},{3,19},{4,0},{5,21},{6,2},{7,23},{8,12},{9,25},... | collective-permute-start | bytes 884744 | tf_op jit(solution)/shard_map/ppermute | solution.py:23
  172.5 5.0 %collective-permute-start.19 = (bf16[12,4096]{1,0:T(8,128)(2,1)S(1)}, bf16[12,4096]{1,0:T(8,128)(2,1)S(1)}, u32[]{:S(2)}, u32[]{:S(2)}) collective-permute-start(bf16[12,4096]{1,0:T(8,128)(2,1)S(1)} %get-tuple-element.16), channel_id=1, source_target_pairs={{0,96},{32,0},{64,32},{96,64},{1,97},{33,1},{65,33},{97,65},{2,98}... | collective-permute-start | bytes 294920 | tf_op jit(solution)/shard_map/ppermute | solution.py:31
  173.2 6.6 %collective-permute-start.20 = (bf16[12,4096]{1,0:T(8,128)(2,1)S(1)}, bf16[12,4096]{1,0:T(8,128)(2,1)S(1)}, u32[]{:S(2)}, u32[]{:S(2)}) collective-permute-start(bf16[12,4096]{1,0:T(8,128)(2,1)S(1)} %get-tuple-element.15), channel_id=1, source_target_pairs={{0,64},{32,96},{64,0},{96,32},{1,65},{33,97},{65,1},{97,33},{2,66}... | collective-permute-start | bytes 294920 | tf_op jit(solution)/shard_map/ppermute | solution.py:31
  173.8 7.3 %collective-permute-start.21 = (bf16[12,4096]{1,0:T(8,128)(2,1)S(1)}, bf16[12,4096]{1,0:T(8,128)(2,1)S(1)}, u32[]{:S(2)}, u32[]{:S(2)}) collective-permute-start(bf16[12,4096]{1,0:T(8,128)(2,1)S(1)} %get-tuple-element.14), channel_id=1, source_target_pairs={{0,32},{32,64},{64,96},{96,0},{1,33},{33,65},{65,97},{97,1},{2,34}... | collective-permute-start | bytes 294920 | tf_op jit(solution)/shard_map/ppermute | solution.py:31
  (14 other events, 140.8 us)

commit v2 on v1

--- a/solution.py
+++ b/solution.py
@@ -1,6 +1,10 @@
+import functools
+
 import jax
 import jax.numpy as jnp
 from jax import lax
+from jax.experimental import pallas as pl
+from jax.experimental.pallas import tpu as pltpu
 from jax.sharding import PartitionSpec as P
 
 SIDE = 4
@@ -27,8 +31,19 @@
     return lax.ppermute(block, "dev", along(False, distance))
 
 
-def step_sec(block, distance):
-    return lax.ppermute(block, "sec", [(i, (i + distance) % SIDE) for i in range(SIDE)])
+def to_section(block, source, target):
+    return lax.ppermute(block, "sec", [(source, target)])
+
+
+def stacked(blocks):
+    rows = sum(block.shape[0] for block in blocks)
+    start, total = 0, None
+    for block in blocks:
+        size = block.shape[0]
+        padded = jnp.pad(block, ((start, rows - start - size), (0, 0)))
+        total = padded if total is None else total + padded
+        start += size
+    return total
 
 
 def other_core(block):
@@ -93,19 +108,93 @@
     return jnp.concatenate([hidden, *terms, fill], axis=1)
 
 
-def experts_on(rows, picks, weights):
-    width = rows.shape[1] - EXTRA
-    share = jnp.sum(
-        jnp.where(picks, rows[:, width:].astype(jnp.float32), 0.0), axis=1, keepdims=True
-    )
-    total = None
-    for gate_up, down in weights:
-        inner = down.shape[0]
-        projected = jnp.dot(rows[:, :width], gate_up, preferred_element_type=jnp.float32)
-        act = (jax.nn.silu(projected[:, :inner]) * projected[:, inner:]).astype(jnp.bfloat16)
-        part = jnp.dot(act, down, preferred_element_type=jnp.float32)
-        total = part if total is None else total + part
-    return (total * share).astype(jnp.bfloat16)
+def expert_kernel(pieces, inner, *refs):
+    pick = refs[0]
+    rows_in = refs[1 : 1 + len(pieces)]
+    gate_own, up_own, gate_other, up_other, down_own, down_other = refs[1 + len(pieces) : 7 + len(pieces)]
+    outs = refs[7 + len(pieces) : -3]
+    rows, act, share = refs[-3:]
+    width = gate_own.shape[0]
+    block = gate_own.shape[1]
+    steps = inner // block
+    step = pl.program_id(0)
+
+    @pl.when(step == 0)
+    def _():
+        start = 0
+        for ref, (first, size) in zip(rows_in, pieces):
+            taken = slice(first, first + size)
+            rows[start : start + size, :] = ref[taken, :width]
+            share[start : start + size, :] = jnp.sum(
+                ref[taken, width:].astype(jnp.float32) * pick[...], axis=1, keepdims=True
+            )
+            start += size
+
+    def hidden_block(gate, up):
+        left = jnp.dot(rows[...], gate[...], preferred_element_type=jnp.float32)
+        right = jnp.dot(rows[...], up[...], preferred_element_type=jnp.float32)
+        act[:, pl.ds(pl.multiple_of(step * block, block), block)] = (jax.nn.silu(left) * right).astype(
+            jnp.bfloat16
+        )
+
+    @pl.when(step < steps)
+    def _():
+        hidden_block(gate_own, up_own)
+
+    @pl.when((step >= steps) & (step < 2 * steps))
+    def _():
+        hidden_block(gate_other, up_other)
+
+    @pl.when(step >= 2 * steps)
+    def _():
+        total = jnp.dot(act[:, :inner], down_own[...], preferred_element_type=jnp.float32)
+        total += jnp.dot(act[:, inner:], down_other[...], preferred_element_type=jnp.float32)
+        total = (total * share[...]).astype(jnp.bfloat16)
+        start = 0
+        for out in outs:
+            out[...] = total[start : start + out.shape[0], :]
+            start += out.shape[0]
+
+
+def experts_on(parts, sizes, pick, weights):
+    (gate_up, down), (gate_up_other, down_other) = weights
+    width, inner = gate_up.shape[0], down.shape[0]
+    block, columns = 256, 512
+    steps = inner // block
+    count = sum(sizes)
+    pieces = [piece for piece, _, _ in parts]
+    taken = tuple((first, size) for _, first, size in parts)
+
+    def part(first, offset):
+        return pl.BlockSpec(
+            (width, block), lambda i: (0, offset + jnp.clip(i - first, 0, steps - 1))
+        )
+
+    def column(i):
+        return (0, jnp.maximum(i - 2 * steps, 0))
+
+    whole = pl.BlockSpec(memory_space=pltpu.VMEM)
+    held = (gate_up, gate_up, gate_up_other, gate_up_other, down, down_other)
+    return pl.pallas_call(
+        functools.partial(expert_kernel, taken, inner),
+        grid=(2 * steps + width // columns,),
+        in_specs=[whole] * (1 + len(pieces))
+        + [part(0, 0), part(0, steps), part(steps, 0), part(steps, steps)]
+        + [pl.BlockSpec((inner, columns), column)] * 2,
+        out_specs=[pl.BlockSpec((size, columns), column) for size in sizes],
+        out_shape=[jax.ShapeDtypeStruct((size, width), jnp.bfloat16) for size in sizes],
+        scratch_shapes=[
+            pltpu.VMEM((count, width), jnp.bfloat16),
+            pltpu.VMEM((count, 2 * inner), jnp.bfloat16),
+            pltpu.VMEM((count, 1), jnp.float32),
+        ],
+        compiler_params=pltpu.CompilerParams(vmem_limit_bytes=40 << 20),
+        cost_estimate=pl.CostEstimate(
+            flops=12 * count * width * inner,
+            bytes_accessed=12 * width * inner + 4 * count * width,
+            transcendentals=2 * count * inner,
+        ),
+    )(pick, *pieces, *(pltpu.with_memory_space_constraint(w, pltpu.HBM) for w in held))
 
 
 def per_device(
@@ -123,32 +212,38 @@
     weights = ((gate_up, down), (other_core(gate_up), other_core(down)))
 
     packed = token_rows(hidden, routes, gates, experts)
-    block = jnp.concatenate([step_sec(packed, sections - 1 - s) for s in range(sections - 1)], axis=0)
-
-    group = jnp.concatenate([block, step_u(block, 1), step_u(block, -1), step_u(block, 2)], axis=0)
+    block = jnp.concatenate([to_section(packed, s, sections - 1) for s in range(sections - 1)], axis=0)
+
+    group = stacked([block, step_u(block, 1), step_u(block, -1), step_u(block, 2)])
+    size = group.shape[0]
+    cut = 16 * ((size // 2 + 15) // 16)
     before, after = step_v(group, 1), step_v(group, -1)
-    half = group.shape[0] // 2
-    across = jnp.concatenate([step_v(before[:half], 1), step_v(after[half:], -1)], axis=0)
+    across_a, across_b = step_v(before[:cut], 1), step_v(after[cut:], -1)
 
     attention_out = attention_block(query, fresh_key_value, kv_cache, cache_lengths)
     attention_out = jnp.where(expert_side, jnp.zeros_like(attention_out), attention_out)
 
     column = lax.broadcasted_iota(jnp.int32, (1, EXTRA), 1)
-    picks = (column % experts == expert) & (column < 3 * experts)
-    size = group.shape[0]
-    y_one = experts_on(jnp.concatenate([group, before], axis=0), picks, weights)
-    y_two = experts_on(jnp.concatenate([after, across], axis=0), picks, weights)
-    y_own, y_before, y_after, y_across = y_one[:size], y_one[size:], y_two[:size], y_two[size:]
-
-    to_after, to_before = step_v(y_across[:half], 1), step_v(y_across[half:], -1)
-    y_after = jnp.concatenate(
-        [(y_after[:half].astype(f32) + to_after.astype(f32)).astype(jnp.bfloat16), y_after[half:]], axis=0
-    )
-    y_before = jnp.concatenate(
-        [y_before[:half], (y_before[half:].astype(f32) + to_before.astype(f32)).astype(jnp.bfloat16)], axis=0
-    )
-    summed = y_own.astype(f32) + step_v(y_after, 1).astype(f32) + step_v(y_before, -1).astype(f32)
-    held = sections * count - count
+    pick = ((column % experts == expert) & (column < 3 * experts)).astype(f32)
+    rest = size - cut
+    cross_a, cross_b, after_b, before_a = experts_on(
+        [(across_a, 0, cut), (across_b, 0, rest), (after, cut, rest), (before, 0, cut)],
+        (cut, rest, rest, cut),
+        pick,
+        weights,
+    )
+    own_a, own_b, after_a, before_b = experts_on(
+        [(group, 0, size), (after, 0, cut), (before, cut, rest)], (cut, rest, cut, rest), pick, weights
+    )
+
+    from_cross_a, from_cross_b = step_v(cross_a, 1), step_v(cross_b, -1)
+    from_after_b, from_before_a = step_v(after_b, 1), step_v(before_a, -1)
+    from_after_a = step_v((after_a.astype(f32) + from_cross_a.astype(f32)).astype(jnp.bfloat16), 1)
+    from_before_b = step_v((before_b.astype(f32) + from_cross_b.astype(f32)).astype(jnp.bfloat16), -1)
+    sum_a = own_a.astype(f32) + from_after_a.astype(f32) + from_before_a.astype(f32)
+    sum_b = own_b.astype(f32) + from_after_b.astype(f32) + from_before_b.astype(f32)
+    held = size // SIDE
+    summed = jnp.concatenate([sum_a, sum_b], axis=0)
     low = summed.astype(jnp.bfloat16)
     total = (
         summed[:held]
@@ -157,10 +252,10 @@
         + step_u(low[3 * held :], 2).astype(f32)
     ).astype(jnp.bfloat16)
 
-    result = jnp.zeros((count, total.shape[1]), jnp.bfloat16)
+    result = None
     for s in range(sections - 1):
-        back = step_sec(total[s * count : (s + 1) * count], s + 1)
-        result = jnp.where(section == s, back, result)
+        back = to_section(total[s * count : (s + 1) * count], sections - 1, s)
+        result = back if result is None else result + back
     return attention_out, result
 
 

time: 184 us -> 162 us (0.88)
  Pallas kernels: 0 us -> 47.5 us
  matrix products: 43.7 us -> 2.92 us
  local copies, waits for them, and re-layouts: 45.4 us -> 7.91 us
  waiting for transfers between devices: 55.1 us -> 61 us
  starting transfers between devices: 28.8 us -> 34.6 us
    pallas_call x0 -> x2, Pallas kernels: none -> 47.5 us  [experts_on(): pl.pallas_call(functools.partial(expert_kernel, taken, inner), grid=(2 *...]
    dot_general x8 -> x0, matrix products: 42.3 us -> none  [the longest x4 25.3 us: experts_on(): jnp.dot(rows[:, :width], gate_up, preferred_element_type=jnp.float32)]
    concatenate x3 -> x0, local copies, waits for them, and re-layouts: 32.4 us -> none  [the longest x1 18.3 us: per_device(): y_one = experts_on(jnp.concatenate([group, before], axis=0), picks, weights)]
    ppermute x8 -> x10, waiting for transfers between devices: 23 us -> 34.1 us  [step_v(): return lax.ppermute(block, 'dev', along(False, distance))]
    ppermute x6, waiting for transfers between devices: 13.8 us -> 8.94 us  [to_section(): return lax.ppermute(block, 'sec', [(source, target)])]
    unnamed x37 -> x15, local copies, waits for them, and re-layouts: 4.91 us -> 1.47 us
    convert_element_type x3, other arithmetic: 2.49 us -> 0.3 us  [the longest x1 0.16 us: per_device(): (after_a.astype(f32) + from_cross_a.astype(f32)).astype(jnp.bfloat16)]
    ppermute x6, starting transfers between devices: 6.84 us -> 8.97 us  [to_section(): return lax.ppermute(block, 'sec', [(source, target)])]
  transfers between devices with their start and end apart: 22 -> 24, of which waited for: 14 -> 12; matrix products, arithmetic and copies ran while one was open for 46% -> 9% of each run, Pallas kernels for 0% -> 15%
where the time goes in v2:
time: 162 us; the launch traced here: 161 us
  waiting for transfers between devices  61 us (38%)
  Pallas kernels  47.5 us (29%)
  starting transfers between devices  34.6 us (21%)
  local copies, waits for them, and re-layouts  7.91 us (5%)
  other arithmetic  5.86 us (4%)
  matrix products  2.92 us (2%)
    pallas_call x2, Pallas kernels, experts_on(): pl.pallas_call(functools.partial(expert_kernel, taken, inner), grid=(2 *...  47.5 us
    ppermute x10, waiting for transfers between devices, step_v(): return lax.ppermute(block, 'dev', along(False, distance))  34.1 us
    ppermute x6, waiting for transfers between devices, step_u(): return lax.ppermute(block, 'dev', along(True, distance))  17.9 us
    ppermute x10, starting transfers between devices, step_v(): return lax.ppermute(block, 'dev', along(False, distance))  15 us
    ppermute x6, starting transfers between devices, step_u(): return lax.ppermute(block, 'dev', along(True, distance))  9.97 us
    ppermute x6, starting transfers between devices, to_section(): return lax.ppermute(block, 'sec', [(source, target)])  8.97 us
    ppermute x6, waiting for transfers between devices, to_section(): return lax.ppermute(block, 'sec', [(source, target)])  8.94 us
    slice x1, local copies, waits for them, and re-layouts, attention_block(): kv_cache[..., :head_size]  4.32 us
  transfers between devices with their start and end apart: 24, of which 12 were waited for; matrix products, arithmetic and copies ran while one was open for 9% of the time, Pallas kernels for 15%

profile of v2, /device:TPU:0, one launch (start us, length us, event | category | flops | bytes accessed | tf_op | source)
XLA Modules:
  0.0 160.6 jit_solution(15536050068653527287)
XLA Ops:
  4.6 5.0 %collective-permute-start = (bf16[12,4224]{1,0:T(8,128)(2,1)S(1)}, bf16[12,4224]{1,0:T(8,128)(2,1)S(1)}, u32[]{:S(2)}, u32[]{:S(2)}) collective-permute-start(bf16[12,4224]{1,0:T(8,128)(2,1)S(1)} %concatenate.10), channel_id=1, source_target_pairs={{0,96},{1,97},{2,98},{3,99},{4,100},{5,101},{6,102},{7,103},{8,104... | collective-permute-start | bytes 304136 | tf_op jit(solution)/shard_map/ppermute | solution.py:35
  11.0 4.7 %collective-permute-done = bf16[12,4224]{1,0:T(8,128)(2,1)S(1)} collective-permute-done((bf16[12,4224]{1,0:T(8,128)(2,1)S(1)}, bf16[12,4224]{1,0:T(8,128)(2,1)S(1)}, u32[]{:S(2)}, u32[]{:S(2)}) %collective-permute-start) | collective-permute-done | bytes 101408 | tf_op jit(solution)/shard_map/ppermute | solution.py:35
  19.0 1.8 %collective-permute-start.5 = (bf16[36,4224]{1,0:T(8,128)(2,1)S(1)}, bf16[36,4224]{1,0:T(8,128)(2,1)S(1)}, u32[]{:S(2)}, u32[]{:S(2)}) collective-permute-start(bf16[36,4224]{1,0:T(8,128)(2,1)S(1)} %pad_maximum_fusion), channel_id=1, source_target_pairs={{0,4},{1,17},{2,6},{3,19},{4,0},{5,21},{6,2},{7,23},{8,12},{9,25},... | collective-permute-start | bytes 912392 | tf_op jit(solution)/shard_map/ppermute | solution.py:27
  20.9 3.3 %collective-permute-done.3 = bf16[36,4224]{1,0:T(8,128)(2,1)S(1)} collective-permute-done((bf16[36,4224]{1,0:T(8,128)(2,1)S(1)}, bf16[36,4224]{1,0:T(8,128)(2,1)S(1)}, u32[]{:S(2)}, u32[]{:S(2)}) %collective-permute-start.3) | collective-permute-done | bytes 304160 | tf_op jit(solution)/shard_map/ppermute | solution.py:27
  24.2 3.2 %collective-permute-done.4 = bf16[36,4224]{1,0:T(8,128)(2,1)S(1)} collective-permute-done((bf16[36,4224]{1,0:T(8,128)(2,1)S(1)}, bf16[36,4224]{1,0:T(8,128)(2,1)S(1)}, u32[]{:S(2)}, u32[]{:S(2)}) %collective-permute-start.4) | collective-permute-done | bytes 304160 | tf_op jit(solution)/shard_map/ppermute | solution.py:27
  30.0 1.9 %collective-permute-start.7 = (bf16[144,4224]{1,0:T(8,128)(2,1)}, bf16[144,4224]{1,0:T(8,128)(2,1)S(1)}, u32[]{:S(2)}, u32[]{:S(2)}) collective-permute-start(bf16[144,4224]{1,0:T(8,128)(2,1)} %pad_add_fusion.refs_1_), channel_id=1, source_target_pairs={{0,8},{1,3},{2,10},{3,5},{4,12},{5,7},{6,14},{7,1},{8,16},{9,11},{... | collective-permute-start | bytes 3649544 | tf_op jit(solution)/shard_map/ppermute | solution.py:31
  32.0 2.2 %collective-permute-start.6 = (bf16[144,4224]{1,0:T(8,128)(2,1)}, bf16[144,4224]{1,0:T(8,128)(2,1)S(1)}, u32[]{:S(2)}, u32[]{:S(2)}) collective-permute-start(bf16[144,4224]{1,0:T(8,128)(2,1)} %pad_add_fusion.refs_1_), channel_id=1, source_target_pairs={{0,24},{1,7},{2,26},{3,1},{4,28},{5,3},{6,30},{7,5},{8,0},{9,15},{... | collective-permute-start | bytes 3649544 | tf_op jit(solution)/shard_map/ppermute | solution.py:31
  34.3 4.3 %fusion.36 = (bf16[2,1024,4,128]{3,2,1,0:T(4,128)(2,1)}, bf16[2,1024,4,128]{3,2,1,0:T(4,128)(2,1)}) fusion(bf16[2,1024,4,256]{3,2,1,0:T(4,128)(2,1)} %param.11), kind=kLoop, calls=%fused_computation.48 | loop fusion | bytes 8388608 | tf_op jit(solution)/shard_map/slice | solution.py:64
  38.6 10.3 %collective-permute-done.7.refs_3_.refs_4_ = bf16[144,4224]{1,0:T(8,128)(2,1)S(1)} collective-permute-done((bf16[144,4224]{1,0:T(8,128)(2,1)}, bf16[144,4224]{1,0:T(8,128)(2,1)S(1)}, u32[]{:S(2)}, u32[]{:S(2)}) %collective-permute-start.7) | collective-permute-done | bytes 1216544 | tf_op jit(solution)/shard_map/ppermute | solution.py:31
  50.0 3.3 %collective-permute-start.11 = (bf16[64,4224]{1,0:T(8,128)(2,1)S(1)}, bf16[64,4224]{1,0:T(8,128)(2,1)S(1)}, u32[]{:S(2)}, u32[]{:S(2)}) collective-permute-start(bf16[64,4224]{1,0:T(8,128)(2,1)S(1)} %slice.55), channel_id=1, source_target_pairs={{0,24},{1,7},{2,26},{3,1},{4,28},{5,3},{6,30},{7,5},{8,0},{9,15},{... | collective-permute-start | bytes 1622024 | tf_op jit(solution)/shard_map/ppermute | solution.py:31
  53.3 2.3 %fusion.39 = (f32[2,4,16]{2,1,0:T(4,128)S(1)}, f32[2,4,16,1024]{3,2,1,0:T(8,128)S(1)}) fusion(bf16[2,4,16,128]{3,2,1,0:T(8,128)(2,1)S(1)} %bitcast.25, bf16[2,1024,4,128]{3,2,1,0:T(4,128)(2,1)} %get-tuple-element.20, pred[2,1024]{1,0:T(4,128)(4,1)S(1)} %iota_compare_fusion.1), kind=kOutput, calls=%fused_computation.51 | convolution fusion | flops 33947520 | bytes 2656768 | tf_op jit(solution)/shard_map/rghd,rtgd->rght/dot_general | solution.py:61
  55.7 4.5 %collective-permute-done.11.refs_2_ = bf16[64,4224]{1,0:T(8,128)(2,1)S(1)} collective-permute-done((bf16[64,4224]{1,0:T(8,128)(2,1)S(1)}, bf16[64,4224]{1,0:T(8,128)(2,1)S(1)}, u32[]{:S(2)}, u32[]{:S(2)}) %collective-permute-start.11) | collective-permute-done | bytes 540704 | tf_op jit(solution)/shard_map/ppermute | solution.py:31
  60.2 1.9 %collective-permute-done.10.refs_1_ = bf16[80,4224]{1,0:T(8,128)(2,1)S(1)} collective-permute-done((bf16[80,4224]{1,0:T(8,128)(2,1)}, bf16[80,4224]{1,0:T(8,128)(2,1)S(1)}, u32[]{:S(2)}, u32[]{:S(2)}) %collective-permute-start.10) | collective-permute-done | bytes 675872 | tf_op jit(solution)/shard_map/ppermute | solution.py:31
  62.1 23.2 %shard_map.105 = (bf16[80,4096]{1,0:T(8,128)(2,1)S(1)}, bf16[64,4096]{1,0:T(8,128)(2,1)S(1)}, bf16[64,4096]{1,0:T(8,128)(2,1)S(1)}, bf16[80,4096]{1,0:T(8,128)(2,1)S(1)}) custom-call(f32[1,128]{1,0:T(1,128)S(1)} %and_convert_fusion.refs_0_, bf16[80,4224]{1,0:T(8,128)(2,1)S(1)} %collective-permute-done.10.refs_1_, ...), custom_call_target="tpu_custom_call" | custom-call | flops 10871635968 | bytes 42467328 | tf_op jit(solution)/shard_map/pallas_call | solution.py:178
  85.3 1.9 %collective-permute-start.17 = (bf16[64,4096]{1,0:T(8,128)(2,1)S(1)}, bf16[64,4096]{1,0:T(8,128)(2,1)S(1)}, u32[]{:S(2)}, u32[]{:S(2)}) collective-permute-start(bf16[64,4096]{1,0:T(8,128)(2,1)S(1)} %get-tuple-element.17), channel_id=1, source_target_pairs={{0,24},{1,7},{2,26},{3,1},{4,28},{5,3},{6,30},{7,5},{8,0},{9,15},{... | collective-permute-start | bytes 1572872 | tf_op jit(solution)/shard_map/ppermute | solution.py:31
  87.4 3.2 %collective-permute-start.14 = (bf16[80,4096]{1,0:T(8,128)(2,1)S(1)}, bf16[80,4096]{1,0:T(8,128)(2,1)S(1)}, u32[]{:S(2)}, u32[]{:S(2)}) collective-permute-start(bf16[80,4096]{1,0:T(8,128)(2,1)S(1)} %get-tuple-element.13), channel_id=1, source_target_pairs={{0,24},{1,7},{2,26},{3,1},{4,28},{5,3},{6,30},{7,5},{8,0},{9,15},{... | collective-permute-start | bytes 1966088 | tf_op jit(solution)/shard_map/ppermute | solution.py:31
  90.6 24.3 %shard_map.104 = (bf16[80,4096]{1,0:T(8,128)(2,1)S(1)}, bf16[64,4096]{1,0:T(8,128)(2,1)S(1)}, bf16[80,4096]{1,0:T(8,128)(2,1)S(1)}, bf16[64,4096]{1,0:T(8,128)(2,1)S(1)}) custom-call(f32[1,128]{1,0:T(1,128)S(1)} %and_convert_fusion.refs_0_, bf16[144,4224]{1,0:T(8,128)(2,1)} %pad_add_fusion.refs_1_, ...), custom_call_target="tpu_custom_call" | custom-call | flops 10871635968 | bytes 42467328 | tf_op jit(solution)/shard_map/pallas_call | solution.py:178
  115.1 2.1 %collective-permute-start.18 = (bf16[64,4096]{1,0:T(8,128)(2,1)S(1)}, bf16[64,4096]{1,0:T(8,128)(2,1)S(1)}, u32[]{:S(2)}, u32[]{:S(2)}) collective-permute-start(bf16[64,4096]{1,0:T(8,128)(2,1)S(1)} %add_convert_fusion.2), channel_id=1, source_target_pairs={{0,24},{1,7},{2,26},{3,1},{4,28},{5,3},{6,30},{7,5},{8,0},{9,15},{... | collective-permute-start | bytes 1572872 | tf_op jit(solution)/shard_map/ppermute | solution.py:31
  117.6 7.8 %collective-permute-done.18 = bf16[64,4096]{1,0:T(8,128)(2,1)S(1)} collective-permute-done((bf16[64,4096]{1,0:T(8,128)(2,1)S(1)}, bf16[64,4096]{1,0:T(8,128)(2,1)S(1)}, u32[]{:S(2)}, u32[]{:S(2)}) %collective-permute-start.18) | collective-permute-done | bytes 524320 | tf_op jit(solution)/shard_map/ppermute | solution.py:31
  125.6 9.5 %collective-permute-done.13 = bf16[80,4096]{1,0:T(8,128)(2,1)S(1)} collective-permute-done((bf16[80,4096]{1,0:T(8,128)(2,1)S(1)}, bf16[80,4096]{1,0:T(8,128)(2,1)S(1)}, u32[]{:S(2)}, u32[]{:S(2)}) %collective-permute-start.13) | collective-permute-done | bytes 655392 | tf_op jit(solution)/shard_map/ppermute | solution.py:31
  135.6 3.3 %collective-permute-start.15 = (bf16[36,4096]{1,0:T(8,128)(2,1)S(1)}, bf16[36,4096]{1,0:T(8,128)(2,1)S(1)}, u32[]{:S(2)}, u32[]{:S(2)}) collective-permute-start(bf16[36,4096]{1,0:T(8,128)(2,1)S(1)} %get-tuple-element.22), channel_id=1, source_target_pairs={{0,6},{1,25},{2,0},{3,27},{4,2},{5,29},{6,4},{7,31},{8,14},{9,1},{... | collective-permute-start | bytes 884744 | tf_op jit(solution)/shard_map/ppermute | solution.py:27
  140.7 2.8 %collective-permute-done.15 = bf16[36,4096]{1,0:T(8,128)(2,1)S(1)} collective-permute-done((bf16[36,4096]{1,0:T(8,128)(2,1)S(1)}, bf16[36,4096]{1,0:T(8,128)(2,1)S(1)}, u32[]{:S(2)}, u32[]{:S(2)}) %collective-permute-start.15) | collective-permute-done | bytes 294944 | tf_op jit(solution)/shard_map/ppermute | solution.py:27
  143.5 7.2 %collective-permute-done.19 = bf16[36,4096]{1,0:T(8,128)(2,1)S(1)} collective-permute-done((bf16[36,4096]{1,0:T(8,128)(2,1)S(1)}, bf16[36,4096]{1,0:T(8,128)(2,1)S(1)}, u32[]{:S(2)}, u32[]{:S(2)}) %collective-permute-start.19) | collective-permute-done | bytes 294944 | tf_op jit(solution)/shard_map/ppermute | solution.py:27
  155.7 4.3 %collective-permute-done.21 = bf16[12,4096]{1,0:T(8,128)(2,1)S(1)} collective-permute-done((bf16[12,4096]{1,0:T(8,128)(2,1)S(1)}, bf16[12,4096]{1,0:T(8,128)(2,1)S(1)}, u32[]{:S(2)}, u32[]{:S(2)}) %collective-permute-start.21) | collective-permute-done | bytes 98336 | tf_op jit(solution)/shard_map/ppermute | solution.py:35
  (71 shorter events, 21.4 us)
Async XLA Ops:
  0.6 61.4 %collective-permute-start.8 = (bf16[4096,1536]{1,0:T(8,128)(2,1)}, bf16[4096,1536]{1,0:T(8,128)(2,1)}, u32[]{:S(2)}, u32[]{:S(2)}) collective-permute-start(bf16[4096,1536]{1,0:T(8,128)(2,1)} %bitcast.16), channel_id=1, source_target_pairs={{0,1},{1,0},{2,3},{3,2},{4,5},{5,4},{6,7},{7,6},{8,9},{9,8},{10,11... | collective-permute-start | bytes 37748744 | tf_op jit(solution)/shard_map/ppermute | solution.py:50
  0.7 61.3 %collective-permute-start.9 = (bf16[768,4096]{1,0:T(8,128)(2,1)}, bf16[768,4096]{1,0:T(8,128)(2,1)}, u32[]{:S(2)}, u32[]{:S(2)}) collective-permute-start(bf16[768,4096]{1,0:T(8,128)(2,1)} %bitcast.21), channel_id=1, source_target_pairs={{0,1},{1,0},{2,3},{3,2},{4,5},{5,4},{6,7},{7,6},{8,9},{9,8},{10,11... | collective-permute-start | bytes 18874376 | tf_op jit(solution)/shard_map/ppermute | solution.py:50
  4.6 11.0 %collective-permute-start = (bf16[12,4224]{1,0:T(8,128)(2,1)S(1)}, bf16[12,4224]{1,0:T(8,128)(2,1)S(1)}, u32[]{:S(2)}, u32[]{:S(2)}) collective-permute-start(bf16[12,4224]{1,0:T(8,128)(2,1)S(1)} %concatenate.10), channel_id=1, source_target_pairs={{0,96},{1,97},{2,98},{3,99},{4,100},{5,101},{6,102},{7,103},{8,104... | collective-permute-start | bytes 304136 | tf_op jit(solution)/shard_map/ppermute | solution.py:35
  9.6 6.0 %collective-permute-start.1 = (bf16[12,4224]{1,0:T(8,128)(2,1)S(1)}, bf16[12,4224]{1,0:T(8,128)(2,1)S(1)}, u32[]{:S(2)}, u32[]{:S(2)}) collective-permute-start(bf16[12,4224]{1,0:T(8,128)(2,1)S(1)} %concatenate.10), channel_id=1, source_target_pairs={{32,96},{33,97},{34,98},{35,99},{36,100},{37,101},{38,102},{39,103... | collective-permute-start | bytes 304136 | tf_op jit(solution)/shard_map/ppermute | solution.py:35
  10.3 5.3 %collective-permute-start.2 = (bf16[12,4224]{1,0:T(8,128)(2,1)S(1)}, bf16[12,4224]{1,0:T(8,128)(2,1)S(1)}, u32[]{:S(2)}, u32[]{:S(2)}) collective-permute-start(bf16[12,4224]{1,0:T(8,128)(2,1)S(1)} %concatenate.10), channel_id=1, source_target_pairs={{64,96},{65,97},{66,98},{67,99},{68,100},{69,101},{70,102},{71,103... | collective-permute-start | bytes 304136 | tf_op jit(solution)/shard_map/ppermute | solution.py:35
  15.7 8.5 %collective-permute-start.3 = (bf16[36,4224]{1,0:T(8,128)(2,1)S(1)}, bf16[36,4224]{1,0:T(8,128)(2,1)S(1)}, u32[]{:S(2)}, u32[]{:S(2)}) collective-permute-start(bf16[36,4224]{1,0:T(8,128)(2,1)S(1)} %pad_maximum_fusion), channel_id=1, source_target_pairs={{0,2},{1,9},{2,4},{3,11},{4,6},{5,13},{6,0},{7,15},{8,10},{9,17},{... | collective-permute-start | bytes 912392 | tf_op jit(solution)/shard_map/ppermute | solution.py:27
  17.3 10.1 %collective-permute-start.4 = (bf16[36,4224]{1,0:T(8,128)(2,1)S(1)}, bf16[36,4224]{1,0:T(8,128)(2,1)S(1)}, u32[]{:S(2)}, u32[]{:S(2)}) collective-permute-start(bf16[36,4224]{1,0:T(8,128)(2,1)S(1)} %pad_maximum_fusion), channel_id=1, source_target_pairs={{0,6},{1,25},{2,0},{3,27},{4,2},{5,29},{6,4},{7,31},{8,14},{9,1},{... | collective-permute-start | bytes 912392 | tf_op jit(solution)/shard_map/ppermute | solution.py:27
  19.0 9.8 %collective-permute-start.5 = (bf16[36,4224]{1,0:T(8,128)(2,1)S(1)}, bf16[36,4224]{1,0:T(8,128)(2,1)S(1)}, u32[]{:S(2)}, u32[]{:S(2)}) collective-permute-start(bf16[36,4224]{1,0:T(8,128)(2,1)S(1)} %pad_maximum_fusion), channel_id=1, source_target_pairs={{0,4},{1,17},{2,6},{3,19},{4,0},{5,21},{6,2},{7,23},{8,12},{9,25},... | collective-permute-start | bytes 912392 | tf_op jit(solution)/shard_map/ppermute | solution.py:27
  30.0 18.9 %collective-permute-start.7 = (bf16[144,4224]{1,0:T(8,128)(2,1)}, bf16[144,4224]{1,0:T(8,128)(2,1)S(1)}, u32[]{:S(2)}, u32[]{:S(2)}) collective-permute-start(bf16[144,4224]{1,0:T(8,128)(2,1)} %pad_add_fusion.refs_1_), channel_id=1, source_target_pairs={{0,8},{1,3},{2,10},{3,5},{4,12},{5,7},{6,14},{7,1},{8,16},{9,11},{... | collective-permute-start | bytes 3649544 | tf_op jit(solution)/shard_map/ppermute | solution.py:31
  32.0 18.0 %collective-permute-start.6 = (bf16[144,4224]{1,0:T(8,128)(2,1)}, bf16[144,4224]{1,0:T(8,128)(2,1)S(1)}, u32[]{:S(2)}, u32[]{:S(2)}) collective-permute-start(bf16[144,4224]{1,0:T(8,128)(2,1)} %pad_add_fusion.refs_1_), channel_id=1, source_target_pairs={{0,24},{1,7},{2,26},{3,1},{4,28},{5,3},{6,30},{7,5},{8,0},{9,15},{... | collective-permute-start | bytes 3649544 | tf_op jit(solution)/shard_map/ppermute | solution.py:31
  49.9 12.2 %collective-permute-start.10 = (bf16[80,4224]{1,0:T(8,128)(2,1)}, bf16[80,4224]{1,0:T(8,128)(2,1)S(1)}, u32[]{:S(2)}, u32[]{:S(2)}) collective-permute-start(bf16[80,4224]{1,0:T(8,128)(2,1)} %slice.54), channel_id=1, source_target_pairs={{0,8},{1,3},{2,10},{3,5},{4,12},{5,7},{6,14},{7,1},{8,16},{9,11},{... | collective-permute-start | bytes 2027528 | tf_op jit(solution)/shard_map/ppermute | solution.py:31
  50.0 10.2 %collective-permute-start.11 = (bf16[64,4224]{1,0:T(8,128)(2,1)S(1)}, bf16[64,4224]{1,0:T(8,128)(2,1)S(1)}, u32[]{:S(2)}, u32[]{:S(2)}) collective-permute-start(bf16[64,4224]{1,0:T(8,128)(2,1)S(1)} %slice.55), channel_id=1, source_target_pairs={{0,24},{1,7},{2,26},{3,1},{4,28},{5,3},{6,30},{7,5},{8,0},{9,15},{... | collective-permute-start | bytes 1622024 | tf_op jit(solution)/shard_map/ppermute | solution.py:31
  85.3 29.6 %collective-permute-start.17 = (bf16[64,4096]{1,0:T(8,128)(2,1)S(1)}, bf16[64,4096]{1,0:T(8,128)(2,1)S(1)}, u32[]{:S(2)}, u32[]{:S(2)}) collective-permute-start(bf16[64,4096]{1,0:T(8,128)(2,1)S(1)} %get-tuple-element.17), channel_id=1, source_target_pairs={{0,24},{1,7},{2,26},{3,1},{4,28},{5,3},{6,30},{7,5},{8,0},{9,15},{... | collective-permute-start | bytes 1572872 | tf_op jit(solution)/shard_map/ppermute | solution.py:31
  87.2 30.4 %collective-permute-start.16 = (bf16[64,4096]{1,0:T(8,128)(2,1)S(1)}, bf16[64,4096]{1,0:T(8,128)(2,1)S(1)}, u32[]{:S(2)}, u32[]{:S(2)}) collective-permute-start(bf16[64,4096]{1,0:T(8,128)(2,1)S(1)} %get-tuple-element.15), channel_id=1, source_target_pairs={{0,8},{1,3},{2,10},{3,5},{4,12},{5,7},{6,14},{7,1},{8,16},{9,11},{... | collective-permute-start | bytes 1572872 | tf_op jit(solution)/shard_map/ppermute | solution.py:31
  87.4 29.7 %collective-permute-start.12 = (bf16[80,4096]{1,0:T(8,128)(2,1)S(1)}, bf16[80,4096]{1,0:T(8,128)(2,1)S(1)}, u32[]{:S(2)}, u32[]{:S(2)}) collective-permute-start(bf16[80,4096]{1,0:T(8,128)(2,1)S(1)} %get-tuple-element.12), channel_id=1, source_target_pairs={{0,8},{1,3},{2,10},{3,5},{4,12},{5,7},{6,14},{7,1},{8,16},{9,11},{... | collective-permute-start | bytes 1966088 | tf_op jit(solution)/shard_map/ppermute | solution.py:31
  87.4 38.2 %collective-permute-start.14 = (bf16[80,4096]{1,0:T(8,128)(2,1)S(1)}, bf16[80,4096]{1,0:T(8,128)(2,1)S(1)}, u32[]{:S(2)}, u32[]{:S(2)}) collective-permute-start(bf16[80,4096]{1,0:T(8,128)(2,1)S(1)} %get-tuple-element.13), channel_id=1, source_target_pairs={{0,24},{1,7},{2,26},{3,1},{4,28},{5,3},{6,30},{7,5},{8,0},{9,15},{... | collective-permute-start | bytes 1966088 | tf_op jit(solution)/shard_map/ppermute | solution.py:31
  115.1 10.4 %collective-permute-start.18 = (bf16[64,4096]{1,0:T(8,128)(2,1)S(1)}, bf16[64,4096]{1,0:T(8,128)(2,1)S(1)}, u32[]{:S(2)}, u32[]{:S(2)}) collective-permute-start(bf16[64,4096]{1,0:T(8,128)(2,1)S(1)} %add_convert_fusion.2), channel_id=1, source_target_pairs={{0,24},{1,7},{2,26},{3,1},{4,28},{5,3},{6,30},{7,5},{8,0},{9,15},{... | collective-permute-start | bytes 1572872 | tf_op jit(solution)/shard_map/ppermute | solution.py:31
  117.3 17.9 %collective-permute-start.13 = (bf16[80,4096]{1,0:T(8,128)(2,1)S(1)}, bf16[80,4096]{1,0:T(8,128)(2,1)S(1)}, u32[]{:S(2)}, u32[]{:S(2)}) collective-permute-start(bf16[80,4096]{1,0:T(8,128)(2,1)S(1)} %add_convert_fusion), channel_id=1, source_target_pairs={{0,8},{1,3},{2,10},{3,5},{4,12},{5,7},{6,14},{7,1},{8,16},{9,11},{... | collective-permute-start | bytes 1966088 | tf_op jit(solution)/shard_map/ppermute | solution.py:31
  135.6 7.9 %collective-permute-start.15 = (bf16[36,4096]{1,0:T(8,128)(2,1)S(1)}, bf16[36,4096]{1,0:T(8,128)(2,1)S(1)}, u32[]{:S(2)}, u32[]{:S(2)}) collective-permute-start(bf16[36,4096]{1,0:T(8,128)(2,1)S(1)} %get-tuple-element.22), channel_id=1, source_target_pairs={{0,6},{1,25},{2,0},{3,27},{4,2},{5,29},{6,4},{7,31},{8,14},{9,1},{... | collective-permute-start | bytes 884744 | tf_op jit(solution)/shard_map/ppermute | solution.py:27
  138.9 11.8 %collective-permute-start.19 = (bf16[36,4096]{1,0:T(8,128)(2,1)S(1)}, bf16[36,4096]{1,0:T(8,128)(2,1)S(1)}, u32[]{:S(2)}, u32[]{:S(2)}) collective-permute-start(bf16[36,4096]{1,0:T(8,128)(2,1)S(1)} %get-tuple-element.23), channel_id=1, source_target_pairs={{0,2},{1,9},{2,4},{3,11},{4,6},{5,13},{6,0},{7,15},{8,10},{9,17},{... | collective-permute-start | bytes 884744 | tf_op jit(solution)/shard_map/ppermute | solution.py:27
  138.9 11.8 %collective-permute-start.20 = (bf16[36,4096]{1,0:T(8,128)(2,1)S(1)}, bf16[36,4096]{1,0:T(8,128)(2,1)}, u32[]{:S(2)}, u32[]{:S(2)}) collective-permute-start(bf16[36,4096]{1,0:T(8,128)(2,1)S(1)} %get-tuple-element.24), channel_id=1, source_target_pairs={{0,4},{1,17},{2,6},{3,19},{4,0},{5,21},{6,2},{7,23},{8,12},{9,25},... | collective-permute-start | bytes 884744 | tf_op jit(solution)/shard_map/ppermute | solution.py:27
  151.9 8.1 %collective-permute-start.21 = (bf16[12,4096]{1,0:T(8,128)(2,1)S(1)}, bf16[12,4096]{1,0:T(8,128)(2,1)S(1)}, u32[]{:S(2)}, u32[]{:S(2)}) collective-permute-start(bf16[12,4096]{1,0:T(8,128)(2,1)S(1)} %get-tuple-element.27), channel_id=1, source_target_pairs={{96,0},{97,1},{98,2},{99,3},{100,4},{101,5},{102,6},{103,7},{104,8... | collective-permute-start | bytes 294920 | tf_op jit(solution)/shard_map/ppermute | solution.py:35
  153.2 6.8 %collective-permute-start.22 = (bf16[12,4096]{1,0:T(8,128)(2,1)S(1)}, bf16[12,4096]{1,0:T(8,128)(2,1)S(1)}, u32[]{:S(2)}, u32[]{:S(2)}) collective-permute-start(bf16[12,4096]{1,0:T(8,128)(2,1)S(1)} %get-tuple-element.25), channel_id=1, source_target_pairs={{96,32},{97,33},{98,34},{99,35},{100,36},{101,37},{102,38},{103,39... | collective-permute-start | bytes 294920 | tf_op jit(solution)/shard_map/ppermute | solution.py:35
  153.8 6.1 %collective-permute-start.23 = (bf16[12,4096]{1,0:T(8,128)(2,1)S(1)}, bf16[12,4096]{1,0:T(8,128)(2,1)S(1)}, u32[]{:S(2)}, u32[]{:S(2)}) collective-permute-start(bf16[12,4096]{1,0:T(8,128)(2,1)S(1)} %get-tuple-element.26), channel_id=1, source_target_pairs={{96,64},{97,65},{98,66},{99,67},{100,68},{101,69},{102,70},{103,71... | collective-permute-start | bytes 294920 | tf_op jit(solution)/shard_map/ppermute | solution.py:35
  (6 other events, 195.0 us)

commit v3 on v2

--- a/solution.py
+++ b/solution.py
@@ -9,6 +9,7 @@
 
 SIDE = 4
 EXTRA = 128
+VMEM_LIMIT = 6 << 20
 
 
 def along(first, distance):
@@ -108,93 +109,92 @@
     return jnp.concatenate([hidden, *terms, fill], axis=1)
 
 
-def expert_kernel(pieces, inner, *refs):
-    pick = refs[0]
-    rows_in = refs[1 : 1 + len(pieces)]
-    gate_own, up_own, gate_other, up_other, down_own, down_other = refs[1 + len(pieces) : 7 + len(pieces)]
-    outs = refs[7 + len(pieces) : -3]
-    rows, act, share = refs[-3:]
-    width = gate_own.shape[0]
-    block = gate_own.shape[1]
-    steps = inner // block
-    step = pl.program_id(0)
-
-    @pl.when(step == 0)
-    def _():
-        start = 0
-        for ref, (first, size) in zip(rows_in, pieces):
-            taken = slice(first, first + size)
-            rows[start : start + size, :] = ref[taken, :width]
-            share[start : start + size, :] = jnp.sum(
-                ref[taken, width:].astype(jnp.float32) * pick[...], axis=1, keepdims=True
-            )
-            start += size
-
-    def hidden_block(gate, up):
+def expert_kernel(parts, outputs, columns, load, *refs):
+    refs = list(refs)
+    pick = refs.pop(0)
+    rows_in = [refs.pop(0) for _ in parts]
+    weights = [refs.pop(0) for _ in range(4 if load else 6)]
+    outs = [refs.pop(0) for _ in range(outputs)]
+    copies = []
+    if load:
+        (gate_up, down, gate_up_other, down_other), weights = weights, [refs.pop(0) for _ in range(6)]
+        sems = refs.pop()
+        sources = []
+        for both in (gate_up, gate_up_other):
+            inner = both.shape[1] // 2
+            sources += [both.at[:, :inner], both.at[:, inner:]]
+        sources += [down, down_other]
+        for i, (source, kept) in enumerate(zip(sources, weights)):
+            copies.append(pltpu.make_async_copy(source, kept, sems.at[i]))
+            copies[-1].start()
+    rows, act, share = refs
+    gate_ups, (down_own, down_other) = (weights[:2], weights[2:4]), weights[4:]
+    inner, width = down_own.shape
+
+    def arrived(index):
+        if load:
+            copies[index].wait()
+
+    start = 0
+    for ref, (first, size) in zip(rows_in, parts):
+        taken = slice(first, first + size)
+        rows[start : start + size, :] = ref[taken, :width]
+        share[start : start + size, :] = jnp.sum(
+            ref[taken, width:].astype(jnp.float32) * pick[...], axis=1, keepdims=True
+        )
+        start += size
+
+    for half, (gate, up) in enumerate(gate_ups):
+        arrived(2 * half)
         left = jnp.dot(rows[...], gate[...], preferred_element_type=jnp.float32)
+        arrived(2 * half + 1)
         right = jnp.dot(rows[...], up[...], preferred_element_type=jnp.float32)
-        act[:, pl.ds(pl.multiple_of(step * block, block), block)] = (jax.nn.silu(left) * right).astype(
-            jnp.bfloat16
-        )
-
-    @pl.when(step < steps)
-    def _():
-        hidden_block(gate_own, up_own)
-
-    @pl.when((step >= steps) & (step < 2 * steps))
-    def _():
-        hidden_block(gate_other, up_other)
-
-    @pl.when(step >= 2 * steps)
-    def _():
-        total = jnp.dot(act[:, :inner], down_own[...], preferred_element_type=jnp.float32)
-        total += jnp.dot(act[:, inner:], down_other[...], preferred_element_type=jnp.float32)
+        act[:, half * inner : (half + 1) * inner] = (jax.nn.silu(left) * right).astype(jnp.bfloat16)
+    arrived(4)
+    arrived(5)
+
+    @pl.loop(0, width // columns)
+    def _(n):
+        at = pl.ds(pl.multiple_of(n * columns, columns), columns)
+        total = jnp.dot(act[:, :inner], down_own[:, at], preferred_element_type=jnp.float32)
+        total += jnp.dot(act[:, inner:], down_other[:, at], preferred_element_type=jnp.float32)
         total = (total * share[...]).astype(jnp.bfloat16)
         start = 0
         for out in outs:
-            out[...] = total[start : start + out.shape[0], :]
+            out[:, at] = total[start : start + out.shape[0], :]
             start += out.shape[0]
 
 
-def experts_on(parts, sizes, pick, weights):
-    (gate_up, down), (gate_up_other, down_other) = weights
-    width, inner = gate_up.shape[0], down.shape[0]
-    block, columns = 256, 512
-    steps = inner // block
+def experts_on(parts, sizes, pick, weights, load=False):
+    inner, width = weights[-1].shape
     count = sum(sizes)
     pieces = [piece for piece, _, _ in parts]
     taken = tuple((first, size) for _, first, size in parts)
-
-    def part(first, offset):
-        return pl.BlockSpec(
-            (width, block), lambda i: (0, offset + jnp.clip(i - first, 0, steps - 1))
-        )
-
-    def column(i):
-        return (0, jnp.maximum(i - 2 * steps, 0))
-
+    space = pltpu.HBM if load else pltpu.VMEM
+    held = [pltpu.with_memory_space_constraint(w, space) for w in weights]
     whole = pl.BlockSpec(memory_space=pltpu.VMEM)
-    held = (gate_up, gate_up, gate_up_other, gate_up_other, down, down_other)
-    return pl.pallas_call(
-        functools.partial(expert_kernel, taken, inner),
-        grid=(2 * steps + width // columns,),
-        in_specs=[whole] * (1 + len(pieces))
-        + [part(0, 0), part(0, steps), part(steps, 0), part(steps, steps)]
-        + [pl.BlockSpec((inner, columns), column)] * 2,
-        out_specs=[pl.BlockSpec((size, columns), column) for size in sizes],
-        out_shape=[jax.ShapeDtypeStruct((size, width), jnp.bfloat16) for size in sizes],
+    there = pl.BlockSpec(memory_space=pl.ANY) if load else whole
+    kept = [(width, inner)] * 4 + [(inner, width)] * 2 if load else []
+    kept = [pltpu.VMEM(shape, jnp.bfloat16) for shape in kept]
+    outs = pl.pallas_call(
+        functools.partial(expert_kernel, taken, len(sizes), 1024, load),
+        in_specs=[whole] * (1 + len(pieces)) + [there] * len(weights),
+        out_specs=[whole] * (len(sizes) + len(kept)),
+        out_shape=[jax.ShapeDtypeStruct((size, width), jnp.bfloat16) for size in sizes] + kept,
         scratch_shapes=[
             pltpu.VMEM((count, width), jnp.bfloat16),
             pltpu.VMEM((count, 2 * inner), jnp.bfloat16),
             pltpu.VMEM((count, 1), jnp.float32),
-        ],
-        compiler_params=pltpu.CompilerParams(vmem_limit_bytes=40 << 20),
+        ]
+        + ([pltpu.SemaphoreType.DMA((6,))] if load else []),
+        compiler_params=pltpu.CompilerParams(vmem_limit_bytes=VMEM_LIMIT),
         cost_estimate=pl.CostEstimate(
             flops=12 * count * width * inner,
-            bytes_accessed=12 * width * inner + 4 * count * width,
+            bytes_accessed=12 * width * inner if load else 4 * count * width,
             transcendentals=2 * count * inner,
         ),
-    )(pick, *pieces, *(pltpu.with_memory_space_constraint(w, pltpu.HBM) for w in held))
+    )(pick, *pieces, *held)
+    return outs[: len(sizes)], outs[len(sizes) :]
 
 
 def per_device(
@@ -209,7 +209,7 @@
     f32 = jnp.float32
 
     gate_up, down = w_gate_up[0], w_down[0]
-    weights = ((gate_up, down), (other_core(gate_up), other_core(down)))
+    weights = (gate_up, down, other_core(gate_up), other_core(down))
 
     packed = token_rows(hidden, routes, gates, experts)
     block = jnp.concatenate([to_section(packed, s, sections - 1) for s in range(sections - 1)], axis=0)
@@ -217,24 +217,24 @@
     group = stacked([block, step_u(block, 1), step_u(block, -1), step_u(block, 2)])
     size = group.shape[0]
     cut = 16 * ((size // 2 + 15) // 16)
+    rest = size - cut
     before, after = step_v(group, 1), step_v(group, -1)
+    column = lax.broadcasted_iota(jnp.int32, (1, EXTRA), 1)
+    pick = ((column % experts == expert) & (column < 3 * experts)).astype(f32)
+    (own_a, own_b), kept = experts_on([(group, 0, size)], (cut, rest), pick, weights, load=True)
+
+    before, after, own_a, own_b = lax.optimization_barrier((before, after, own_a, own_b))
     across_a, across_b = step_v(before[:cut], 1), step_v(after[cut:], -1)
+    (after_a, after_b, before_a, before_b), _ = experts_on(
+        [(after, 0, size), (before, 0, size)], (cut, rest, cut, rest), pick, kept
+    )
+    across_a, across_b, after_a, after_b, before_a, before_b = lax.optimization_barrier(
+        (across_a, across_b, after_a, after_b, before_a, before_b)
+    )
+    (cross_a, cross_b), _ = experts_on([(across_a, 0, cut), (across_b, 0, rest)], (cut, rest), pick, kept)
 
     attention_out = attention_block(query, fresh_key_value, kv_cache, cache_lengths)
     attention_out = jnp.where(expert_side, jnp.zeros_like(attention_out), attention_out)
-
-    column = lax.broadcasted_iota(jnp.int32, (1, EXTRA), 1)
-    pick = ((column % experts == expert) & (column < 3 * experts)).astype(f32)
-    rest = size - cut
-    cross_a, cross_b, after_b, before_a = experts_on(
-        [(across_a, 0, cut), (across_b, 0, rest), (after, cut, rest), (before, 0, cut)],
-        (cut, rest, rest, cut),
-        pick,
-        weights,
-    )
-    own_a, own_b, after_a, before_b = experts_on(
-        [(group, 0, size), (after, 0, cut), (before, cut, rest)], (cut, rest, cut, rest), pick, weights
-    )
 
     from_cross_a, from_cross_b = step_v(cross_a, 1), step_v(cross_b, -1)
     from_after_b, from_before_a = step_v(after_b, 1), step_v(before_a, -1)

time: 162 us -> 139 us (0.86)
  Pallas kernels: 47.5 us -> 32.9 us
  waiting for transfers between devices: 61 us -> 49.6 us
  starting transfers between devices: 34.6 us -> 39.7 us
    pallas_call x2 -> x3, Pallas kernels: 47.5 us -> 32.9 us  [experts_on(): pl.pallas_call(functools.partial(expert_kernel, taken, len(sizes), 1024,...]
    ppermute x10, waiting for transfers between devices: 34.1 us -> 24.2 us  [step_v(): return lax.ppermute(block, 'dev', along(False, distance))]
    ppermute x6, starting transfers between devices: 9.97 us -> 14.2 us  [step_u(): return lax.ppermute(block, 'dev', along(True, distance))]
  transfers between devices with their start and end apart: 24 -> 24, of which waited for: 12 -> 11; matrix products, arithmetic and copies ran while one was open for 9% -> 9% of each run, Pallas kernels for 15% -> 19%
where the time goes in v3:
time: 139 us; the launch traced here: 137 us
  waiting for transfers between devices  49.6 us (36%)
  starting transfers between devices  39.7 us (29%)
  Pallas kernels  32.9 us (24%)
  local copies, waits for them, and re-layouts  7.4 us (5%)
  other arithmetic  5.51 us (4%)
    pallas_call x3, Pallas kernels, experts_on(): pl.pallas_call(functools.partial(expert_kernel, taken, len(sizes), 1024,...  32.9 us
    ppermute x10, waiting for transfers between devices, step_v(): return lax.ppermute(block, 'dev', along(False, distance))  24.2 us
    ppermute x6, waiting for transfers between devices, step_u(): return lax.ppermute(block, 'dev', along(True, distance))  16.5 us
    ppermute x10, starting transfers between devices, step_v(): return lax.ppermute(block, 'dev', along(False, distance))  15.9 us
    ppermute x6, starting transfers between devices, step_u(): return lax.ppermute(block, 'dev', along(True, distance))  14.2 us
    ppermute x6, starting transfers between devices, to_section(): return lax.ppermute(block, 'sec', [(source, target)])  8.97 us
    ppermute x6, waiting for transfers between devices, to_section(): return lax.ppermute(block, 'sec', [(source, target)])  8.95 us
    slice x1, local copies, waits for them, and re-layouts, attention_block(): kv_cache[..., :head_size]  3.98 us
  transfers between devices with their start and end apart: 24, of which 11 were waited for; matrix products, arithmetic and copies ran while one was open for 9% of the time, Pallas kernels for 19%

profile of v3, /device:TPU:0, one launch (start us, length us, event | category | flops | bytes accessed | tf_op | source)
XLA Modules:
  0.0 137.4 jit_solution(17214455437620080949)
XLA Ops:
  4.6 5.0 %collective-permute-start = (bf16[12,4224]{1,0:T(8,128)(2,1)S(1)}, bf16[12,4224]{1,0:T(8,128)(2,1)S(1)}, u32[]{:S(2)}, u32[]{:S(2)}) collective-permute-start(bf16[12,4224]{1,0:T(8,128)(2,1)S(1)} %concatenate.10), channel_id=1, source_target_pairs={{0,96},{1,97},{2,98},{3,99},{4,100},{5,101},{6,102},{7,103},{8,104... | collective-permute-start | bytes 304136 | tf_op jit(solution)/shard_map/ppermute | solution.py:36
  11.0 4.7 %collective-permute-done = bf16[12,4224]{1,0:T(8,128)(2,1)S(1)} collective-permute-done((bf16[12,4224]{1,0:T(8,128)(2,1)S(1)}, bf16[12,4224]{1,0:T(8,128)(2,1)S(1)}, u32[]{:S(2)}, u32[]{:S(2)}) %collective-permute-start) | collective-permute-done | bytes 101408 | tf_op jit(solution)/shard_map/ppermute | solution.py:36
  15.7 1.6 %collective-permute-start.3 = (bf16[36,4224]{1,0:T(8,128)(2,1)S(1)}, bf16[36,4224]{1,0:T(8,128)(2,1)S(1)}, u32[]{:S(2)}, u32[]{:S(2)}) collective-permute-start(bf16[36,4224]{1,0:T(8,128)(2,1)S(1)} %pad_maximum_fusion), channel_id=1, source_target_pairs={{0,2},{1,9},{2,4},{3,11},{4,6},{5,13},{6,0},{7,15},{8,10},{9,17},{... | collective-permute-start | bytes 912392 | tf_op jit(solution)/shard_map/ppermute | solution.py:28
  17.3 1.7 %collective-permute-start.4 = (bf16[36,4224]{1,0:T(8,128)(2,1)S(1)}, bf16[36,4224]{1,0:T(8,128)(2,1)S(1)}, u32[]{:S(2)}, u32[]{:S(2)}) collective-permute-start(bf16[36,4224]{1,0:T(8,128)(2,1)S(1)} %pad_maximum_fusion), channel_id=1, source_target_pairs={{0,6},{1,25},{2,0},{3,27},{4,2},{5,29},{6,4},{7,31},{8,14},{9,1},{... | collective-permute-start | bytes 912392 | tf_op jit(solution)/shard_map/ppermute | solution.py:28
  19.0 1.8 %collective-permute-start.5 = (bf16[36,4224]{1,0:T(8,128)(2,1)S(1)}, bf16[36,4224]{1,0:T(8,128)(2,1)S(1)}, u32[]{:S(2)}, u32[]{:S(2)}) collective-permute-start(bf16[36,4224]{1,0:T(8,128)(2,1)S(1)} %pad_maximum_fusion), channel_id=1, source_target_pairs={{0,4},{1,17},{2,6},{3,19},{4,0},{5,21},{6,2},{7,23},{8,12},{9,25},... | collective-permute-start | bytes 912392 | tf_op jit(solution)/shard_map/ppermute | solution.py:28
  22.3 1.9 %collective-permute-done.3 = bf16[36,4224]{1,0:T(8,128)(2,1)S(1)} collective-permute-done((bf16[36,4224]{1,0:T(8,128)(2,1)S(1)}, bf16[36,4224]{1,0:T(8,128)(2,1)S(1)}, u32[]{:S(2)}, u32[]{:S(2)}) %collective-permute-start.3) | collective-permute-done | bytes 304160 | tf_op jit(solution)/shard_map/ppermute | solution.py:28
  24.2 3.2 %collective-permute-done.4 = bf16[36,4224]{1,0:T(8,128)(2,1)S(1)} collective-permute-done((bf16[36,4224]{1,0:T(8,128)(2,1)S(1)}, bf16[36,4224]{1,0:T(8,128)(2,1)S(1)}, u32[]{:S(2)}, u32[]{:S(2)}) %collective-permute-start.4) | collective-permute-done | bytes 304160 | tf_op jit(solution)/shard_map/ppermute | solution.py:28
  29.0 2.0 %collective-permute-start.6 = (bf16[144,4224]{1,0:T(8,128)(2,1)S(1)}, bf16[144,4224]{1,0:T(8,128)(2,1)S(1)}, u32[]{:S(2)}, u32[]{:S(2)}) collective-permute-start(bf16[144,4224]{1,0:T(8,128)(2,1)S(1)} %pad_add_fusion.refs_1_), channel_id=1, source_target_pairs={{0,8},{1,3},{2,10},{3,5},{4,12},{5,7},{6,14},{7,1},{8,16},{9,11},{... | collective-permute-start | bytes 3649544 | tf_op jit(solution)/shard_map/ppermute | solution.py:32
  31.0 2.6 %collective-permute-start.7 = (bf16[144,4224]{1,0:T(8,128)(2,1)S(1)}, bf16[144,4224]{1,0:T(8,128)(2,1)S(1)}, u32[]{:S(2)}, u32[]{:S(2)}) collective-permute-start(bf16[144,4224]{1,0:T(8,128)(2,1)S(1)} %pad_add_fusion.refs_1_), channel_id=1, source_target_pairs={{0,24},{1,7},{2,26},{3,1},{4,28},{5,3},{6,30},{7,5},{8,0},{9,15},{... | collective-permute-start | bytes 3649544 | tf_op jit(solution)/shard_map/ppermute | solution.py:32
  33.7 4.0 %fusion.36 = (bf16[2,1024,4,128]{3,2,1,0:T(4,128)(2,1)S(1)}, bf16[2,1024,4,128]{3,2,1,0:T(4,128)(2,1)}) fusion(bf16[2,1024,4,256]{3,2,1,0:T(4,128)(2,1)} %param.11), kind=kLoop, calls=%fused_computation.48 | loop fusion | bytes 8388608 | tf_op jit(solution)/shard_map/slice | solution.py:65
  37.7 14.4 %shard_map.104 = (bf16[80,4096]{1,0:T(8,128)(2,1)S(1)}, bf16[64,4096]{1,0:T(8,128)(2,1)S(1)}, bf16[4096,768]{1,0:T(8,128)(2,1)S(1)}, bf16[4096,768]{1,0:T(8,128)...) custom-call(f32[1,128]{1,0:T(1,128)S(1)} %and_convert_fusion.refs_0_, ...), custom_call_target="tpu_custom_call" | custom-call | flops 5435817984 | bytes 37748736 | tf_op jit(solution)/shard_map/pallas_call | solution.py:179
  53.4 2.5 %collective-permute-start.11 = (bf16[64,4224]{1,0:T(8,128)(2,1)S(1)}, bf16[64,4224]{1,0:T(8,128)(2,1)S(1)}, u32[]{:S(2)}, u32[]{:S(2)}) collective-permute-start(bf16[64,4224]{1,0:T(8,128)(2,1)S(1)} %slice.46), channel_id=1, source_target_pairs={{0,24},{1,7},{2,26},{3,1},{4,28},{5,3},{6,30},{7,5},{8,0},{9,15},{... | collective-permute-start | bytes 1622024 | tf_op jit(solution)/shard_map/ppermute | solution.py:32
  55.8 11.9 %shard_map.105 = (bf16[80,4096]{1,0:T(8,128)(2,1)S(1)}, bf16[64,4096]{1,0:T(8,128)(2,1)S(1)}, bf16[80,4096]{1,0:T(8,128)(2,1)S(1)}, bf16[64,4096]{1,0:T(8,128)(2,1)S(1)}) custom-call(f32[1,128]{1,0:T(1,128)S(1)} %and_convert_fusion.refs_0_, bf16[144,4224]{1,0:T(8,128)(2,1)S(1)} %collective-permute-done.7.refs_1_, ...), custom_call_target="tpu_custom_call" | custom-call | flops 10871635968 | bytes 4718592 | tf_op jit(solution)/shard_map/pallas_call | solution.py:179
  67.8 6.6 %shard_map.106 = (bf16[80,4096]{1,0:T(8,128)(2,1)S(1)}, bf16[64,4096]{1,0:T(8,128)(2,1)S(1)}) custom-call(f32[1,128]{1,0:T(1,128)S(1)} %and_convert_fusion.refs_0_, bf16[80,4224]{1,0:T(8,128)(2,1)S(1)} %collective-permute-done.10.refs_1_, bf16[64,4224]{1,0:T(8,128)(2,1)S(1)} %collective-permute-done.11.refs_2_, ...), custom_call_target="tpu_custom_call" | custom-call | flops 5435817984 | bytes 2359296 | tf_op jit(solution)/shard_map/pallas_call | solution.py:179
  77.4 3.2 %collective-permute-start.14 = (bf16[80,4096]{1,0:T(8,128)(2,1)S(1)}, bf16[80,4096]{1,0:T(8,128)(2,1)S(1)}, u32[]{:S(2)}, u32[]{:S(2)}) collective-permute-start(bf16[80,4096]{1,0:T(8,128)(2,1)S(1)} %get-tuple-element.45), channel_id=1, source_target_pairs={{0,24},{1,7},{2,26},{3,1},{4,28},{5,3},{6,30},{7,5},{8,0},{9,15},{... | collective-permute-start | bytes 1966088 | tf_op jit(solution)/shard_map/ppermute | solution.py:32
  80.6 3.0 %collective-permute-done.17 = bf16[64,4096]{1,0:T(8,128)(2,1)S(1)} collective-permute-done((bf16[64,4096]{1,0:T(8,128)(2,1)S(1)}, bf16[64,4096]{1,0:T(8,128)(2,1)S(1)}, u32[]{:S(2)}, u32[]{:S(2)}) %collective-permute-start.17) | collective-permute-done | bytes 524320 | tf_op jit(solution)/shard_map/ppermute | solution.py:32
  83.7 2.2 %collective-permute-start.18 = (bf16[64,4096]{1,0:T(8,128)(2,1)S(1)}, bf16[64,4096]{1,0:T(8,128)(2,1)S(1)}, u32[]{:S(2)}, u32[]{:S(2)}) collective-permute-start(bf16[64,4096]{1,0:T(8,128)(2,1)S(1)} %add_convert_fusion.2), channel_id=1, source_target_pairs={{0,24},{1,7},{2,26},{3,1},{4,28},{5,3},{6,30},{7,5},{8,0},{9,15},{... | collective-permute-start | bytes 1572872 | tf_op jit(solution)/shard_map/ppermute | solution.py:32
  86.0 7.5 %collective-permute-done.12 = bf16[80,4096]{1,0:T(8,128)(2,1)S(1)} collective-permute-done((bf16[80,4096]{1,0:T(8,128)(2,1)S(1)}, bf16[80,4096]{1,0:T(8,128)(2,1)S(1)}, u32[]{:S(2)}, u32[]{:S(2)}) %collective-permute-start.12) | collective-permute-done | bytes 655392 | tf_op jit(solution)/shard_map/ppermute | solution.py:32
  93.8 2.5 %collective-permute-done.18 = bf16[64,4096]{1,0:T(8,128)(2,1)S(1)} collective-permute-done((bf16[64,4096]{1,0:T(8,128)(2,1)S(1)}, bf16[64,4096]{1,0:T(8,128)(2,1)S(1)}, u32[]{:S(2)}, u32[]{:S(2)}) %collective-permute-start.18) | collective-permute-done | bytes 524320 | tf_op jit(solution)/shard_map/ppermute | solution.py:32
  96.5 11.2 %collective-permute-done.13 = bf16[80,4096]{1,0:T(8,128)(2,1)S(1)} collective-permute-done((bf16[80,4096]{1,0:T(8,128)(2,1)S(1)}, bf16[80,4096]{1,0:T(8,128)(2,1)S(1)}, u32[]{:S(2)}, u32[]{:S(2)}) %collective-permute-start.13) | collective-permute-done | bytes 655392 | tf_op jit(solution)/shard_map/ppermute | solution.py:32
  108.1 7.6 %collective-permute-start.15 = (bf16[36,4096]{1,0:T(8,128)(2,1)S(1)}, bf16[36,4096]{1,0:T(8,128)(2,1)S(1)}, u32[]{:S(2)}, u32[]{:S(2)}) collective-permute-start(bf16[36,4096]{1,0:T(8,128)(2,1)S(1)} %get-tuple-element.54), channel_id=1, source_target_pairs={{0,6},{1,25},{2,0},{3,27},{4,2},{5,29},{6,4},{7,31},{8,14},{9,1},{... | collective-permute-start | bytes 884744 | tf_op jit(solution)/shard_map/ppermute | solution.py:28
  117.5 2.8 %collective-permute-done.15 = bf16[36,4096]{1,0:T(8,128)(2,1)S(1)} collective-permute-done((bf16[36,4096]{1,0:T(8,128)(2,1)S(1)}, bf16[36,4096]{1,0:T(8,128)(2,1)S(1)}, u32[]{:S(2)}, u32[]{:S(2)}) %collective-permute-start.15) | collective-permute-done | bytes 294944 | tf_op jit(solution)/shard_map/ppermute | solution.py:28
  120.2 7.2 %collective-permute-done.19 = bf16[36,4096]{1,0:T(8,128)(2,1)S(1)} collective-permute-done((bf16[36,4096]{1,0:T(8,128)(2,1)S(1)}, bf16[36,4096]{1,0:T(8,128)(2,1)S(1)}, u32[]{:S(2)}, u32[]{:S(2)}) %collective-permute-start.19) | collective-permute-done | bytes 294944 | tf_op jit(solution)/shard_map/ppermute | solution.py:28
  132.4 4.3 %collective-permute-done.21 = bf16[12,4096]{1,0:T(8,128)(2,1)S(1)} collective-permute-done((bf16[12,4096]{1,0:T(8,128)(2,1)S(1)}, bf16[12,4096]{1,0:T(8,128)(2,1)S(1)}, u32[]{:S(2)}, u32[]{:S(2)}) %collective-permute-start.21) | collective-permute-done | bytes 98336 | tf_op jit(solution)/shard_map/ppermute | solution.py:36
  (64 shorter events, 21.3 us)
Async XLA Ops:
  0.6 37.1 %collective-permute-start.8 = (bf16[4096,1536]{1,0:T(8,128)(2,1)}, bf16[4096,1536]{1,0:T(8,128)(2,1)}, u32[]{:S(2)}, u32[]{:S(2)}) collective-permute-start(bf16[4096,1536]{1,0:T(8,128)(2,1)} %bitcast.16), channel_id=1, source_target_pairs={{0,1},{1,0},{2,3},{3,2},{4,5},{5,4},{6,7},{7,6},{8,9},{9,8},{10,11... | collective-permute-start | bytes 37748744 | tf_op jit(solution)/shard_map/ppermute | solution.py:51
  0.7 37.0 %collective-permute-start.9 = (bf16[768,4096]{1,0:T(8,128)(2,1)}, bf16[768,4096]{1,0:T(8,128)(2,1)}, u32[]{:S(2)}, u32[]{:S(2)}) collective-permute-start(bf16[768,4096]{1,0:T(8,128)(2,1)} %bitcast.18), channel_id=1, source_target_pairs={{0,1},{1,0},{2,3},{3,2},{4,5},{5,4},{6,7},{7,6},{8,9},{9,8},{10,11... | collective-permute-start | bytes 18874376 | tf_op jit(solution)/shard_map/ppermute | solution.py:51
  4.6 11.0 %collective-permute-start = (bf16[12,4224]{1,0:T(8,128)(2,1)S(1)}, bf16[12,4224]{1,0:T(8,128)(2,1)S(1)}, u32[]{:S(2)}, u32[]{:S(2)}) collective-permute-start(bf16[12,4224]{1,0:T(8,128)(2,1)S(1)} %concatenate.10), channel_id=1, source_target_pairs={{0,96},{1,97},{2,98},{3,99},{4,100},{5,101},{6,102},{7,103},{8,104... | collective-permute-start | bytes 304136 | tf_op jit(solution)/shard_map/ppermute | solution.py:36
  9.6 6.0 %collective-permute-start.1 = (bf16[12,4224]{1,0:T(8,128)(2,1)S(1)}, bf16[12,4224]{1,0:T(8,128)(2,1)S(1)}, u32[]{:S(2)}, u32[]{:S(2)}) collective-permute-start(bf16[12,4224]{1,0:T(8,128)(2,1)S(1)} %concatenate.10), channel_id=1, source_target_pairs={{32,96},{33,97},{34,98},{35,99},{36,100},{37,101},{38,102},{39,103... | collective-permute-start | bytes 304136 | tf_op jit(solution)/shard_map/ppermute | solution.py:36
  10.3 5.3 %collective-permute-start.2 = (bf16[12,4224]{1,0:T(8,128)(2,1)S(1)}, bf16[12,4224]{1,0:T(8,128)(2,1)S(1)}, u32[]{:S(2)}, u32[]{:S(2)}) collective-permute-start(bf16[12,4224]{1,0:T(8,128)(2,1)S(1)} %concatenate.10), channel_id=1, source_target_pairs={{64,96},{65,97},{66,98},{67,99},{68,100},{69,101},{70,102},{71,103... | collective-permute-start | bytes 304136 | tf_op jit(solution)/shard_map/ppermute | solution.py:36
  15.7 8.5 %collective-permute-start.3 = (bf16[36,4224]{1,0:T(8,128)(2,1)S(1)}, bf16[36,4224]{1,0:T(8,128)(2,1)S(1)}, u32[]{:S(2)}, u32[]{:S(2)}) collective-permute-start(bf16[36,4224]{1,0:T(8,128)(2,1)S(1)} %pad_maximum_fusion), channel_id=1, source_target_pairs={{0,2},{1,9},{2,4},{3,11},{4,6},{5,13},{6,0},{7,15},{8,10},{9,17},{... | collective-permute-start | bytes 912392 | tf_op jit(solution)/shard_map/ppermute | solution.py:28
  17.3 10.1 %collective-permute-start.4 = (bf16[36,4224]{1,0:T(8,128)(2,1)S(1)}, bf16[36,4224]{1,0:T(8,128)(2,1)S(1)}, u32[]{:S(2)}, u32[]{:S(2)}) collective-permute-start(bf16[36,4224]{1,0:T(8,128)(2,1)S(1)} %pad_maximum_fusion), channel_id=1, source_target_pairs={{0,6},{1,25},{2,0},{3,27},{4,2},{5,29},{6,4},{7,31},{8,14},{9,1},{... | collective-permute-start | bytes 912392 | tf_op jit(solution)/shard_map/ppermute | solution.py:28
  19.0 9.8 %collective-permute-start.5 = (bf16[36,4224]{1,0:T(8,128)(2,1)S(1)}, bf16[36,4224]{1,0:T(8,128)(2,1)S(1)}, u32[]{:S(2)}, u32[]{:S(2)}) collective-permute-start(bf16[36,4224]{1,0:T(8,128)(2,1)S(1)} %pad_maximum_fusion), channel_id=1, source_target_pairs={{0,4},{1,17},{2,6},{3,19},{4,0},{5,21},{6,2},{7,23},{8,12},{9,25},... | collective-permute-start | bytes 912392 | tf_op jit(solution)/shard_map/ppermute | solution.py:28
  29.0 23.2 %collective-permute-start.6 = (bf16[144,4224]{1,0:T(8,128)(2,1)S(1)}, bf16[144,4224]{1,0:T(8,128)(2,1)S(1)}, u32[]{:S(2)}, u32[]{:S(2)}) collective-permute-start(bf16[144,4224]{1,0:T(8,128)(2,1)S(1)} %pad_add_fusion.refs_1_), channel_id=1, source_target_pairs={{0,8},{1,3},{2,10},{3,5},{4,12},{5,7},{6,14},{7,1},{8,16},{9,11},{... | collective-permute-start | bytes 3649544 | tf_op jit(solution)/shard_map/ppermute | solution.py:32
  31.0 21.2 %collective-permute-start.7 = (bf16[144,4224]{1,0:T(8,128)(2,1)S(1)}, bf16[144,4224]{1,0:T(8,128)(2,1)S(1)}, u32[]{:S(2)}, u32[]{:S(2)}) collective-permute-start(bf16[144,4224]{1,0:T(8,128)(2,1)S(1)} %pad_add_fusion.refs_1_), channel_id=1, source_target_pairs={{0,24},{1,7},{2,26},{3,1},{4,28},{5,3},{6,30},{7,5},{8,0},{9,15},{... | collective-permute-start | bytes 3649544 | tf_op jit(solution)/shard_map/ppermute | solution.py:32
  52.2 15.5 %collective-permute-start.10 = (bf16[80,4224]{1,0:T(8,128)(2,1)S(1)}, bf16[80,4224]{1,0:T(8,128)(2,1)S(1)}, u32[]{:S(2)}, u32[]{:S(2)}) collective-permute-start(bf16[80,4224]{1,0:T(8,128)(2,1)S(1)} %slice.45), channel_id=1, source_target_pairs={{0,8},{1,3},{2,10},{3,5},{4,12},{5,7},{6,14},{7,1},{8,16},{9,11},{... | collective-permute-start | bytes 2027528 | tf_op jit(solution)/shard_map/ppermute | solution.py:32
  53.4 14.4 %collective-permute-start.11 = (bf16[64,4224]{1,0:T(8,128)(2,1)S(1)}, bf16[64,4224]{1,0:T(8,128)(2,1)S(1)}, u32[]{:S(2)}, u32[]{:S(2)}) collective-permute-start(bf16[64,4224]{1,0:T(8,128)(2,1)S(1)} %slice.46), channel_id=1, source_target_pairs={{0,24},{1,7},{2,26},{3,1},{4,28},{5,3},{6,30},{7,5},{8,0},{9,15},{... | collective-permute-start | bytes 1622024 | tf_op jit(solution)/shard_map/ppermute | solution.py:32
  74.4 9.3 %collective-permute-start.17 = (bf16[64,4096]{1,0:T(8,128)(2,1)S(1)}, bf16[64,4096]{1,0:T(8,128)(2,1)S(1)}, u32[]{:S(2)}, u32[]{:S(2)}) collective-permute-start(bf16[64,4096]{1,0:T(8,128)(2,1)S(1)} %get-tuple-element.49), channel_id=1, source_target_pairs={{0,24},{1,7},{2,26},{3,1},{4,28},{5,3},{6,30},{7,5},{8,0},{9,15},{... | collective-permute-start | bytes 1572872 | tf_op jit(solution)/shard_map/ppermute | solution.py:32
  76.0 17.8 %collective-permute-start.16 = (bf16[64,4096]{1,0:T(8,128)(2,1)S(1)}, bf16[64,4096]{1,0:T(8,128)(2,1)S(1)}, u32[]{:S(2)}, u32[]{:S(2)}) collective-permute-start(bf16[64,4096]{1,0:T(8,128)(2,1)S(1)} %get-tuple-element.47), channel_id=1, source_target_pairs={{0,8},{1,3},{2,10},{3,5},{4,12},{5,7},{6,14},{7,1},{8,16},{9,11},{... | collective-permute-start | bytes 1572872 | tf_op jit(solution)/shard_map/ppermute | solution.py:32
  77.3 16.1 %collective-permute-start.12 = (bf16[80,4096]{1,0:T(8,128)(2,1)S(1)}, bf16[80,4096]{1,0:T(8,128)(2,1)S(1)}, u32[]{:S(2)}, u32[]{:S(2)}) collective-permute-start(bf16[80,4096]{1,0:T(8,128)(2,1)S(1)} %get-tuple-element.44), channel_id=1, source_target_pairs={{0,8},{1,3},{2,10},{3,5},{4,12},{5,7},{6,14},{7,1},{8,16},{9,11},{... | collective-permute-start | bytes 1966088 | tf_op jit(solution)/shard_map/ppermute | solution.py:32
  77.4 19.0 %collective-permute-start.14 = (bf16[80,4096]{1,0:T(8,128)(2,1)S(1)}, bf16[80,4096]{1,0:T(8,128)(2,1)S(1)}, u32[]{:S(2)}, u32[]{:S(2)}) collective-permute-start(bf16[80,4096]{1,0:T(8,128)(2,1)S(1)} %get-tuple-element.45), channel_id=1, source_target_pairs={{0,24},{1,7},{2,26},{3,1},{4,28},{5,3},{6,30},{7,5},{8,0},{9,15},{... | collective-permute-start | bytes 1966088 | tf_op jit(solution)/shard_map/ppermute | solution.py:32
  83.7 12.5 %collective-permute-start.18 = (bf16[64,4096]{1,0:T(8,128)(2,1)S(1)}, bf16[64,4096]{1,0:T(8,128)(2,1)S(1)}, u32[]{:S(2)}, u32[]{:S(2)}) collective-permute-start(bf16[64,4096]{1,0:T(8,128)(2,1)S(1)} %add_convert_fusion.2), channel_id=1, source_target_pairs={{0,24},{1,7},{2,26},{3,1},{4,28},{5,3},{6,30},{7,5},{8,0},{9,15},{... | collective-permute-start | bytes 1572872 | tf_op jit(solution)/shard_map/ppermute | solution.py:32
  93.6 14.0 %collective-permute-start.13 = (bf16[80,4096]{1,0:T(8,128)(2,1)S(1)}, bf16[80,4096]{1,0:T(8,128)(2,1)S(1)}, u32[]{:S(2)}, u32[]{:S(2)}) collective-permute-start(bf16[80,4096]{1,0:T(8,128)(2,1)S(1)} %add_convert_fusion), channel_id=1, source_target_pairs={{0,8},{1,3},{2,10},{3,5},{4,12},{5,7},{6,14},{7,1},{8,16},{9,11},{... | collective-permute-start | bytes 1966088 | tf_op jit(solution)/shard_map/ppermute | solution.py:32
  108.1 12.2 %collective-permute-start.15 = (bf16[36,4096]{1,0:T(8,128)(2,1)S(1)}, bf16[36,4096]{1,0:T(8,128)(2,1)S(1)}, u32[]{:S(2)}, u32[]{:S(2)}) collective-permute-start(bf16[36,4096]{1,0:T(8,128)(2,1)S(1)} %get-tuple-element.54), channel_id=1, source_target_pairs={{0,6},{1,25},{2,0},{3,27},{4,2},{5,29},{6,4},{7,31},{8,14},{9,1},{... | collective-permute-start | bytes 884744 | tf_op jit(solution)/shard_map/ppermute | solution.py:28
  115.6 11.8 %collective-permute-start.19 = (bf16[36,4096]{1,0:T(8,128)(2,1)S(1)}, bf16[36,4096]{1,0:T(8,128)(2,1)S(1)}, u32[]{:S(2)}, u32[]{:S(2)}) collective-permute-start(bf16[36,4096]{1,0:T(8,128)(2,1)S(1)} %get-tuple-element.55), channel_id=1, source_target_pairs={{0,2},{1,9},{2,4},{3,11},{4,6},{5,13},{6,0},{7,15},{8,10},{9,17},{... | collective-permute-start | bytes 884744 | tf_op jit(solution)/shard_map/ppermute | solution.py:28
  115.6 11.8 %collective-permute-start.20 = (bf16[36,4096]{1,0:T(8,128)(2,1)S(1)}, bf16[36,4096]{1,0:T(8,128)(2,1)}, u32[]{:S(2)}, u32[]{:S(2)}) collective-permute-start(bf16[36,4096]{1,0:T(8,128)(2,1)S(1)} %get-tuple-element.56), channel_id=1, source_target_pairs={{0,4},{1,17},{2,6},{3,19},{4,0},{5,21},{6,2},{7,23},{8,12},{9,25},... | collective-permute-start | bytes 884744 | tf_op jit(solution)/shard_map/ppermute | solution.py:28
  128.6 8.1 %collective-permute-start.21 = (bf16[12,4096]{1,0:T(8,128)(2,1)S(1)}, bf16[12,4096]{1,0:T(8,128)(2,1)S(1)}, u32[]{:S(2)}, u32[]{:S(2)}) collective-permute-start(bf16[12,4096]{1,0:T(8,128)(2,1)S(1)} %get-tuple-element.59), channel_id=1, source_target_pairs={{96,0},{97,1},{98,2},{99,3},{100,4},{101,5},{102,6},{103,7},{104,8... | collective-permute-start | bytes 294920 | tf_op jit(solution)/shard_map/ppermute | solution.py:36
  129.9 6.8 %collective-permute-start.22 = (bf16[12,4096]{1,0:T(8,128)(2,1)S(1)}, bf16[12,4096]{1,0:T(8,128)(2,1)S(1)}, u32[]{:S(2)}, u32[]{:S(2)}) collective-permute-start(bf16[12,4096]{1,0:T(8,128)(2,1)S(1)} %get-tuple-element.57), channel_id=1, source_target_pairs={{96,32},{97,33},{98,34},{99,35},{100,36},{101,37},{102,38},{103,39... | collective-permute-start | bytes 294920 | tf_op jit(solution)/shard_map/ppermute | solution.py:36
  130.6 6.1 %collective-permute-start.23 = (bf16[12,4096]{1,0:T(8,128)(2,1)S(1)}, bf16[12,4096]{1,0:T(8,128)(2,1)S(1)}, u32[]{:S(2)}, u32[]{:S(2)}) collective-permute-start(bf16[12,4096]{1,0:T(8,128)(2,1)S(1)} %get-tuple-element.58), channel_id=1, source_target_pairs={{96,64},{97,65},{98,66},{99,67},{100,68},{101,69},{102,70},{103,71... | collective-permute-start | bytes 294920 | tf_op jit(solution)/shard_map/ppermute | solution.py:36
  (2 other events, 21.2 us)

commit v4 on v3

--- a/solution.py
+++ b/solution.py
@@ -96,17 +96,43 @@
     return (mixture / denominator[..., None]).astype(jnp.bfloat16).reshape(count_req, -1)
 
 
-def token_rows(hidden, routes, gates, experts):
-    combine = gates / jnp.sum(gates, axis=1, keepdims=True)
-    named = routes[:, :, None] == jnp.arange(experts, dtype=jnp.int32)[None, None, :]
-    share = jnp.sum(jnp.where(named, combine[:, :, None], 0.0), axis=1)
+def pack_kernel(experts, hidden, routes, gates, out):
+    count, width = hidden.shape
+    out[:, :width] = hidden[...]
+    combine = gates[...] / jnp.sum(gates[...], axis=0, keepdims=True)
+    place = lax.broadcasted_iota(jnp.int32, (EXTRA, count), 0)
+    share = jnp.zeros((EXTRA, count), jnp.float32)
+    for k in range(routes.shape[0]):
+        named = routes[k : k + 1, :] == place % experts
+        share += jnp.where(named, combine[k : k + 1, :], 0.0)
     terms = []
     for _ in range(3):
-        term = lax.reduce_precision(share, 8, 7)
-        terms.append(term.astype(jnp.bfloat16))
-        share = share - term
-    fill = jnp.zeros((hidden.shape[0], EXTRA - 3 * experts), jnp.bfloat16)
-    return jnp.concatenate([hidden, *terms, fill], axis=1)
+        terms.append(share.astype(jnp.bfloat16).astype(jnp.float32))
+        share = share - terms[-1]
+    packed = jnp.where(place < experts, terms[0], jnp.where(place < 2 * experts, terms[1], terms[2]))
+    packed = jnp.where(place < 3 * experts, packed, 0.0).astype(jnp.bfloat16)
+    same = lax.broadcasted_iota(jnp.int32, (count, count), 0) == lax.broadcasted_iota(
+        jnp.int32, (count, count), 1
+    )
+    turned = lax.dot_general(
+        same.astype(jnp.float32).astype(jnp.bfloat16),
+        packed,
+        (((1,), (1,)), ((), ())),
+        preferred_element_type=jnp.float32,
+    )
+    out[:, width:] = turned.astype(jnp.bfloat16)
+
+
+def token_rows(hidden, routes, gates, experts):
+    count, width = hidden.shape
+    whole = pl.BlockSpec(memory_space=pltpu.VMEM)
+    return pl.pallas_call(
+        functools.partial(pack_kernel, experts),
+        in_specs=[whole] * 3,
+        out_specs=whole,
+        out_shape=jax.ShapeDtypeStruct((count, width + EXTRA), hidden.dtype),
+        compiler_params=pltpu.CompilerParams(vmem_limit_bytes=VMEM_LIMIT),
+    )(hidden, routes.T, gates.T)
 
 
 def expert_kernel(parts, outputs, columns, load, *refs):
@@ -231,25 +257,40 @@
     across_a, across_b, after_a, after_b, before_a, before_b = lax.optimization_barrier(
         (across_a, across_b, after_a, after_b, before_a, before_b)
     )
+    from_after_b, from_before_a = step_v(after_b, 1), step_v(before_a, -1)
     (cross_a, cross_b), _ = experts_on([(across_a, 0, cut), (across_b, 0, rest)], (cut, rest), pick, kept)
-
-    attention_out = attention_block(query, fresh_key_value, kv_cache, cache_lengths)
-    attention_out = jnp.where(expert_side, jnp.zeros_like(attention_out), attention_out)
-
+    from_after_b, from_before_a, cross_a, cross_b = lax.optimization_barrier(
+        (from_after_b, from_before_a, cross_a, cross_b)
+    )
     from_cross_a, from_cross_b = step_v(cross_a, 1), step_v(cross_b, -1)
-    from_after_b, from_before_a = step_v(after_b, 1), step_v(before_a, -1)
+
+    query, _ = lax.optimization_barrier((query, cross_a))
+    attention_out = lax.cond(
+        expert_side,
+        lambda query, *_: jnp.zeros_like(query),
+        attention_block,
+        query,
+        fresh_key_value,
+        kv_cache,
+        cache_lengths,
+    )
+
+    from_before_b = step_v((before_b.astype(f32) + from_cross_b.astype(f32)).astype(jnp.bfloat16), -1)
     from_after_a = step_v((after_a.astype(f32) + from_cross_a.astype(f32)).astype(jnp.bfloat16), 1)
-    from_before_b = step_v((before_b.astype(f32) + from_cross_b.astype(f32)).astype(jnp.bfloat16), -1)
+    held = size // SIDE
+    near = 2 * held - (cut - held)
+    sum_b = own_b.astype(f32) + from_after_b.astype(f32) + from_before_b.astype(f32)
+    far = sum_b[near:].astype(jnp.bfloat16)
+    part = held // 2
+    from_far_a, from_far_b = step_u(far[:part], 1), step_u(far[part:], -1)
     sum_a = own_a.astype(f32) + from_after_a.astype(f32) + from_before_a.astype(f32)
-    sum_b = own_b.astype(f32) + from_after_b.astype(f32) + from_before_b.astype(f32)
-    held = size // SIDE
-    summed = jnp.concatenate([sum_a, sum_b], axis=0)
-    low = summed.astype(jnp.bfloat16)
+    ahead = jnp.concatenate([sum_a[2 * held :], sum_b[:near]], axis=0)
+    ahead = ahead + jnp.pad(from_far_a.astype(f32), ((0, held - part), (0, 0)))
+    behind = sum_a[held : 2 * held] + jnp.pad(from_far_b.astype(f32), ((part, 0), (0, 0)))
     total = (
-        summed[:held]
-        + step_u(low[held : 2 * held], -1).astype(f32)
-        + step_u(low[2 * held : 3 * held], 1).astype(f32)
-        + step_u(low[3 * held :], 2).astype(f32)
+        sum_a[:held]
+        + step_u(ahead.astype(jnp.bfloat16), 1).astype(f32)
+        + step_u(behind.astype(jnp.bfloat16), -1).astype(f32)
     ).astype(jnp.bfloat16)
 
     result = None

time: 139 us -> 126 us (0.906)
  waiting for transfers between devices: 49.6 us -> 42.8 us
  other arithmetic: 5.51 us -> 2.3 us
  starting transfers between devices: 39.7 us -> 36.7 us
  Pallas kernels: 32.9 us -> 34.7 us
    slice x1 -> x3, local copies, waits for them, and re-layouts: 3.98 us -> 0.13 us  [the longest x1 0.09 us: per_device(): from_far_a, from_far_b = (step_u(far[:part], 1), step_u(far[part:], -1))]
    ppermute x6, waiting for transfers between devices: 8.95 us -> 5.51 us  [to_section(): return lax.ppermute(block, 'sec', [(source, target)])]
    another operation x0 -> x1, local copies, waits for them, and re-layouts: none -> 2.74 us
    ppermute x6 -> x7, starting transfers between devices: 14.2 us -> 11.9 us  [step_u(): return lax.ppermute(block, 'dev', along(True, distance))]
    ppermute x6 -> x7, waiting for transfers between devices: 16.5 us -> 14.3 us  [step_u(): return lax.ppermute(block, 'dev', along(True, distance))]
    pallas_call x3, Pallas kernels: 32.9 us -> 34.6 us  [experts_on(): pl.pallas_call(functools.partial(expert_kernel, taken, len(sizes), 1024,...]
  transfers between devices with their start and end apart: 24 -> 25, of which waited for: 11 -> 13; matrix products, arithmetic and copies ran while one was open for 9% -> 5% of each run, Pallas kernels for 19% -> 28%
where the time goes in v4:
time: 126 us; the launch traced here: 125 us
  waiting for transfers between devices  42.8 us (34%)
  starting transfers between devices  36.7 us (29%)
  Pallas kernels  34.7 us (28%)
  local copies, waits for them, and re-layouts  6.39 us (5%)
  other arithmetic  2.3 us (2%)
  matrix products  1.33 us (1%)
    pallas_call x3, Pallas kernels, experts_on(): pl.pallas_call(functools.partial(expert_kernel, taken, len(sizes), 1024,...  34.6 us
    ppermute x10, waiting for transfers between devices, step_v(): return lax.ppermute(block, 'dev', along(False, distance))  23 us
    ppermute x10, starting transfers between devices, step_v(): return lax.ppermute(block, 'dev', along(False, distance))  15.2 us
    ppermute x7, waiting for transfers between devices, step_u(): return lax.ppermute(block, 'dev', along(True, distance))  14.3 us
    ppermute x7, starting transfers between devices, step_u(): return lax.ppermute(block, 'dev', along(True, distance))  11.9 us
    ppermute x6, starting transfers between devices, to_section(): return lax.ppermute(block, 'sec', [(source, target)])  8.97 us
    ppermute x6, waiting for transfers between devices, to_section(): return lax.ppermute(block, 'sec', [(source, target)])  5.51 us
    another operation x1, local copies, waits for them, and re-layouts  2.74 us
  transfers between devices with their start and end apart: 25, of which 13 were waited for; matrix products, arithmetic and copies ran while one was open for 5% of the time, Pallas kernels for 28%

profile of v4, /device:TPU:0, one launch (start us, length us, event | category | flops | bytes accessed | tf_op | source)
XLA Modules:
  0.0 125.2 jit_solution(2174298412725976404)
XLA Ops:
  3.7 5.0 %collective-permute-start = (bf16[12,4224]{1,0:T(8,128)(2,1)S(1)}, bf16[12,4224]{1,0:T(8,128)(2,1)S(1)}, u32[]{:S(2)}, u32[]{:S(2)}) collective-permute-start(bf16[12,4224]{1,0:T(8,128)(2,1)S(1)} %shard_map.107), channel_id=1, source_target_pairs={{0,96},{1,97},{2,98},{3,99},{4,100},{5,101},{6,102},{7,103},{8,104... | collective-permute-start | bytes 304136 | tf_op jit(solution)/shard_map/ppermute | solution.py:36
  10.0 4.7 %collective-permute-done = bf16[12,4224]{1,0:T(8,128)(2,1)S(1)} collective-permute-done((bf16[12,4224]{1,0:T(8,128)(2,1)S(1)}, bf16[12,4224]{1,0:T(8,128)(2,1)S(1)}, u32[]{:S(2)}, u32[]{:S(2)}) %collective-permute-start) | collective-permute-done | bytes 101408 | tf_op jit(solution)/shard_map/ppermute | solution.py:36
  14.8 1.6 %collective-permute-start.3 = (bf16[36,4224]{1,0:T(8,128)(2,1)S(1)}, bf16[36,4224]{1,0:T(8,128)(2,1)S(1)}, u32[]{:S(2)}, u32[]{:S(2)}) collective-permute-start(bf16[36,4224]{1,0:T(8,128)(2,1)S(1)} %pad_maximum_fusion), channel_id=1, source_target_pairs={{0,2},{1,9},{2,4},{3,11},{4,6},{5,13},{6,0},{7,15},{8,10},{9,17},{... | collective-permute-start | bytes 912392 | tf_op jit(solution)/shard_map/ppermute | solution.py:28
  16.3 1.7 %collective-permute-start.4 = (bf16[36,4224]{1,0:T(8,128)(2,1)S(1)}, bf16[36,4224]{1,0:T(8,128)(2,1)S(1)}, u32[]{:S(2)}, u32[]{:S(2)}) collective-permute-start(bf16[36,4224]{1,0:T(8,128)(2,1)S(1)} %pad_maximum_fusion), channel_id=1, source_target_pairs={{0,6},{1,25},{2,0},{3,27},{4,2},{5,29},{6,4},{7,31},{8,14},{9,1},{... | collective-permute-start | bytes 912392 | tf_op jit(solution)/shard_map/ppermute | solution.py:28
  18.1 1.8 %collective-permute-start.5 = (bf16[36,4224]{1,0:T(8,128)(2,1)S(1)}, bf16[36,4224]{1,0:T(8,128)(2,1)S(1)}, u32[]{:S(2)}, u32[]{:S(2)}) collective-permute-start(bf16[36,4224]{1,0:T(8,128)(2,1)S(1)} %pad_maximum_fusion), channel_id=1, source_target_pairs={{0,4},{1,17},{2,6},{3,19},{4,0},{5,21},{6,2},{7,23},{8,12},{9,25},... | collective-permute-start | bytes 912392 | tf_op jit(solution)/shard_map/ppermute | solution.py:28
  19.9 3.3 %collective-permute-done.3 = bf16[36,4224]{1,0:T(8,128)(2,1)S(1)} collective-permute-done((bf16[36,4224]{1,0:T(8,128)(2,1)S(1)}, bf16[36,4224]{1,0:T(8,128)(2,1)S(1)}, u32[]{:S(2)}, u32[]{:S(2)}) %collective-permute-start.3) | collective-permute-done | bytes 304160 | tf_op jit(solution)/shard_map/ppermute | solution.py:28
  23.2 3.2 %collective-permute-done.4 = bf16[36,4224]{1,0:T(8,128)(2,1)S(1)} collective-permute-done((bf16[36,4224]{1,0:T(8,128)(2,1)S(1)}, bf16[36,4224]{1,0:T(8,128)(2,1)S(1)}, u32[]{:S(2)}, u32[]{:S(2)}) %collective-permute-start.4) | collective-permute-done | bytes 304160 | tf_op jit(solution)/shard_map/ppermute | solution.py:28
  28.1 2.0 %collective-permute-start.6 = (bf16[144,4224]{1,0:T(8,128)(2,1)S(1)}, bf16[144,4224]{1,0:T(8,128)(2,1)S(1)}, u32[]{:S(2)}, u32[]{:S(2)}) collective-permute-start(bf16[144,4224]{1,0:T(8,128)(2,1)S(1)} %pad_add_fusion.refs_1_), channel_id=1, source_target_pairs={{0,8},{1,3},{2,10},{3,5},{4,12},{5,7},{6,14},{7,1},{8,16},{9,11},{... | collective-permute-start | bytes 3649544 | tf_op jit(solution)/shard_map/ppermute | solution.py:32
  30.1 2.6 %collective-permute-start.7 = (bf16[144,4224]{1,0:T(8,128)(2,1)S(1)}, bf16[144,4224]{1,0:T(8,128)(2,1)}, u32[]{:S(2)}, u32[]{:S(2)}) collective-permute-start(bf16[144,4224]{1,0:T(8,128)(2,1)S(1)} %pad_add_fusion.refs_1_), channel_id=1, source_target_pairs={{0,24},{1,7},{2,26},{3,1},{4,28},{5,3},{6,30},{7,5},{8,0},{9,15},{... | collective-permute-start | bytes 3649544 | tf_op jit(solution)/shard_map/ppermute | solution.py:32
  32.7 14.6 %shard_map.108 = (bf16[80,4096]{1,0:T(8,128)(2,1)S(1)}, bf16[64,4096]{1,0:T(8,128)(2,1)S(1)}, bf16[4096,768]{1,0:T(8,128)(2,1)S(1)}, bf16[4096,768]{1,0:T(8,128)...) custom-call(f32[1,128]{1,0:T(1,128)S(1)} %and_convert_fusion.refs_0_, ...), custom_call_target="tpu_custom_call" | custom-call | flops 5435817984 | bytes 37748736 | tf_op jit(solution)/shard_map/pallas_call | solution.py:205
  48.4 2.1 %collective-permute-start.10 = (bf16[80,4224]{1,0:T(8,128)(2,1)S(1)}, bf16[80,4224]{1,0:T(8,128)(2,1)S(1)}, u32[]{:S(2)}, u32[]{:S(2)}) collective-permute-start(bf16[80,4224]{1,0:T(8,128)(2,1)S(1)} %slice.49), channel_id=1, source_target_pairs={{0,8},{1,3},{2,10},{3,5},{4,12},{5,7},{6,14},{7,1},{8,16},{9,11},{... | collective-permute-start | bytes 2027528 | tf_op jit(solution)/shard_map/ppermute | solution.py:32
  53.0 13.4 %shard_map.109 = (bf16[80,4096]{1,0:T(8,128)(2,1)S(1)}, bf16[64,4096]{1,0:T(8,128)(2,1)S(1)}, bf16[80,4096]{1,0:T(8,128)(2,1)S(1)}, bf16[64,4096]{1,0:T(8,128)(2,1)S(1)}) custom-call(f32[1,128]{1,0:T(1,128)S(1)} %and_convert_fusion.refs_0_, bf16[144,4224]{1,0:T(8,128)(2,1)} %collective-permute-done.7.refs_1_, ...), custom_call_target="tpu_custom_call" | custom-call | flops 10871635968 | bytes 4718592 | tf_op jit(solution)/shard_map/pallas_call | solution.py:205
  68.6 6.6 %shard_map.110 = (bf16[80,4096]{1,0:T(8,128)(2,1)S(1)}, bf16[64,4096]{1,0:T(8,128)(2,1)S(1)}) custom-call(f32[1,128]{1,0:T(1,128)S(1)} %and_convert_fusion.refs_0_, bf16[80,4224]{1,0:T(8,128)(2,1)S(1)} %collective-permute-done.10.refs_1_, bf16[64,4224]{1,0:T(8,128)(2,1)S(1)} %collective-permute-done.11.refs_2_, ...), custom_call_target="tpu_custom_call" | custom-call | flops 5435817984 | bytes 2359296 | tf_op jit(solution)/shard_map/pallas_call | solution.py:205
  75.2 2.8 %collective-permute-done.12 = bf16[64,4096]{1,0:T(8,128)(2,1)S(1)} collective-permute-done((bf16[64,4096]{1,0:T(8,128)(2,1)S(1)}, bf16[64,4096]{1,0:T(8,128)(2,1)S(1)}, u32[]{:S(2)}, u32[]{:S(2)}) %collective-permute-start.12) | collective-permute-done | bytes 524320 | tf_op jit(solution)/shard_map/ppermute | solution.py:32
  80.0 7.2 %collective-permute-done.16 = bf16[64,4096]{1,0:T(8,128)(2,1)S(1)} collective-permute-done((bf16[64,4096]{1,0:T(8,128)(2,1)S(1)}, bf16[64,4096]{1,0:T(8,128)(2,1)S(1)}, u32[]{:S(2)}, u32[]{:S(2)}) %collective-permute-start.16) | collective-permute-done | bytes 524320 | tf_op jit(solution)/shard_map/ppermute | solution.py:32
  87.2 2.7 %collective-permute-start.17 = (bf16[64,4096]{1,0:T(8,128)(2,1)S(1)}, bf16[64,4096]{1,0:T(8,128)(2,1)S(1)}, u32[]{:S(2)}, u32[]{:S(2)}) collective-permute-start(bf16[64,4096]{1,0:T(8,128)(2,1)S(1)} %add_convert_fusion.1), channel_id=1, source_target_pairs={{0,24},{1,7},{2,26},{3,1},{4,28},{5,3},{6,30},{7,5},{8,0},{9,15},{... | collective-permute-start | bytes 1572872 | tf_op jit(solution)/shard_map/ppermute | solution.py:32
  91.6 7.2 %collective-permute-done.17 = bf16[64,4096]{1,0:T(8,128)(2,1)S(1)} collective-permute-done((bf16[64,4096]{1,0:T(8,128)(2,1)S(1)}, bf16[64,4096]{1,0:T(8,128)(2,1)S(1)}, u32[]{:S(2)}, u32[]{:S(2)}) %collective-permute-start.17) | collective-permute-done | bytes 524320 | tf_op jit(solution)/shard_map/ppermute | solution.py:32
  99.1 1.8 %collective-permute-start.18 = (bf16[18,4096]{1,0:T(8,128)(2,1)S(1)}, bf16[18,4096]{1,0:T(8,128)(2,1)S(1)}, u32[]{:S(2)}, u32[]{:S(2)}) collective-permute-start(bf16[18,4096]{1,0:T(8,128)(2,1)S(1)} %get-tuple-element.93), channel_id=1, source_target_pairs={{0,2},{1,9},{2,4},{3,11},{4,6},{5,13},{6,0},{7,15},{8,10},{9,17},{... | collective-permute-start | bytes 442376 | tf_op jit(solution)/shard_map/ppermute | solution.py:28
  100.9 1.6 %collective-permute-start.20 = (bf16[18,4096]{1,0:T(8,128)(2,1)S(1)}, bf16[18,4096]{1,0:T(8,128)(2,1)S(1)}, u32[]{:S(2)}, u32[]{:S(2)}) collective-permute-start(bf16[18,4096]{1,0:T(8,128)(2,1)S(1)} %get-tuple-element.94), channel_id=1, source_target_pairs={{0,6},{1,25},{2,0},{3,27},{4,2},{5,29},{6,4},{7,31},{8,14},{9,1},{... | collective-permute-start | bytes 442376 | tf_op jit(solution)/shard_map/ppermute | solution.py:28
  102.5 3.6 %collective-permute-done.15 = bf16[80,4096]{1,0:T(8,128)(2,1)S(1)} collective-permute-done((bf16[80,4096]{1,0:T(8,128)(2,1)S(1)}, bf16[80,4096]{1,0:T(8,128)(2,1)S(1)}, u32[]{:S(2)}, u32[]{:S(2)}) %collective-permute-start.15) | collective-permute-done | bytes 655392 | tf_op jit(solution)/shard_map/ppermute | solution.py:32
  106.4 2.6 %collective-permute-start.19 = (bf16[36,4096]{1,0:T(8,128)(2,1)S(1)}, bf16[36,4096]{1,0:T(8,128)(2,1)S(1)}, u32[]{:S(2)}, u32[]{:S(2)}) collective-permute-start(bf16[36,4096]{1,0:T(8,128)(2,1)S(1)} %fusion.30), channel_id=1, source_target_pairs={{0,2},{1,9},{2,4},{3,11},{4,6},{5,13},{6,0},{7,15},{8,10},{9,17},{... | collective-permute-start | bytes 884744 | tf_op jit(solution)/shard_map/ppermute | solution.py:28
  109.9 4.9 %collective-permute-done.19 = bf16[36,4096]{1,0:T(8,128)(2,1)S(1)} collective-permute-done((bf16[36,4096]{1,0:T(8,128)(2,1)S(1)}, bf16[36,4096]{1,0:T(8,128)(2,1)S(1)}, u32[]{:S(2)}, u32[]{:S(2)}) %collective-permute-start.19) | collective-permute-done | bytes 294944 | tf_op jit(solution)/shard_map/ppermute | solution.py:28
  119.1 4.5 %conditional.1 = (bf16[2,8192]{1,0:T(2,128)(2,1)S(1)}) conditional(s32[]{:T(128)} %convert_element_type.87, (s32[2]{0:T(128)S(1)}, bf16[2,8192]{1,0:T(2,128)(2,1)S(1)}, bf16[2,1024,4,256]{3,2,1,0:T(4,128)(2,1)}, bf16[2,4,256]{2,1,0:T(4,128)(2,1)S(1)}) %tuple.37, () %tuple.23), branch_computations={%region_0.3_spmd, %region_3.4_spmd} | conditional | flops 68128512 | bytes 14426640 | solution.py:268
  119.2 2.7 %copy.14 = bf16[2,1024,4,256]{3,1,2,0:T(8,128)(2,1)S(1)} copy(bf16[2,1024,4,256]{3,2,1,0:T(4,128)(2,1)} %get-tuple-element.83) | data formatting | bytes 8388608 | tf_op jit(solution)/shard_map
  (74 shorter events, 24.7 us)
Async XLA Ops:
  0.6 32.0 %collective-permute-start.8 = (bf16[4096,1536]{1,0:T(8,128)(2,1)}, bf16[4096,1536]{1,0:T(8,128)(2,1)}, u32[]{:S(2)}, u32[]{:S(2)}) collective-permute-start(bf16[4096,1536]{1,0:T(8,128)(2,1)} %bitcast.20), channel_id=1, source_target_pairs={{0,1},{1,0},{2,3},{3,2},{4,5},{5,4},{6,7},{7,6},{8,9},{9,8},{10,11... | collective-permute-start | bytes 37748744 | tf_op jit(solution)/shard_map/ppermute | solution.py:51
  0.7 31.9 %collective-permute-start.9 = (bf16[768,4096]{1,0:T(8,128)(2,1)}, bf16[768,4096]{1,0:T(8,128)(2,1)}, u32[]{:S(2)}, u32[]{:S(2)}) collective-permute-start(bf16[768,4096]{1,0:T(8,128)(2,1)} %bitcast.22), channel_id=1, source_target_pairs={{0,1},{1,0},{2,3},{3,2},{4,5},{5,4},{6,7},{7,6},{8,9},{9,8},{10,11... | collective-permute-start | bytes 18874376 | tf_op jit(solution)/shard_map/ppermute | solution.py:51
  3.7 11.0 %collective-permute-start = (bf16[12,4224]{1,0:T(8,128)(2,1)S(1)}, bf16[12,4224]{1,0:T(8,128)(2,1)S(1)}, u32[]{:S(2)}, u32[]{:S(2)}) collective-permute-start(bf16[12,4224]{1,0:T(8,128)(2,1)S(1)} %shard_map.107), channel_id=1, source_target_pairs={{0,96},{1,97},{2,98},{3,99},{4,100},{5,101},{6,102},{7,103},{8,104... | collective-permute-start | bytes 304136 | tf_op jit(solution)/shard_map/ppermute | solution.py:36
  8.7 6.0 %collective-permute-start.1 = (bf16[12,4224]{1,0:T(8,128)(2,1)S(1)}, bf16[12,4224]{1,0:T(8,128)(2,1)S(1)}, u32[]{:S(2)}, u32[]{:S(2)}) collective-permute-start(bf16[12,4224]{1,0:T(8,128)(2,1)S(1)} %shard_map.107), channel_id=1, source_target_pairs={{32,96},{33,97},{34,98},{35,99},{36,100},{37,101},{38,102},{39,103... | collective-permute-start | bytes 304136 | tf_op jit(solution)/shard_map/ppermute | solution.py:36
  14.8 8.5 %collective-permute-start.3 = (bf16[36,4224]{1,0:T(8,128)(2,1)S(1)}, bf16[36,4224]{1,0:T(8,128)(2,1)S(1)}, u32[]{:S(2)}, u32[]{:S(2)}) collective-permute-start(bf16[36,4224]{1,0:T(8,128)(2,1)S(1)} %pad_maximum_fusion), channel_id=1, source_target_pairs={{0,2},{1,9},{2,4},{3,11},{4,6},{5,13},{6,0},{7,15},{8,10},{9,17},{... | collective-permute-start | bytes 912392 | tf_op jit(solution)/shard_map/ppermute | solution.py:28
  16.3 10.1 %collective-permute-start.4 = (bf16[36,4224]{1,0:T(8,128)(2,1)S(1)}, bf16[36,4224]{1,0:T(8,128)(2,1)S(1)}, u32[]{:S(2)}, u32[]{:S(2)}) collective-permute-start(bf16[36,4224]{1,0:T(8,128)(2,1)S(1)} %pad_maximum_fusion), channel_id=1, source_target_pairs={{0,6},{1,25},{2,0},{3,27},{4,2},{5,29},{6,4},{7,31},{8,14},{9,1},{... | collective-permute-start | bytes 912392 | tf_op jit(solution)/shard_map/ppermute | solution.py:28
  18.1 9.8 %collective-permute-start.5 = (bf16[36,4224]{1,0:T(8,128)(2,1)S(1)}, bf16[36,4224]{1,0:T(8,128)(2,1)S(1)}, u32[]{:S(2)}, u32[]{:S(2)}) collective-permute-start(bf16[36,4224]{1,0:T(8,128)(2,1)S(1)} %pad_maximum_fusion), channel_id=1, source_target_pairs={{0,4},{1,17},{2,6},{3,19},{4,0},{5,21},{6,2},{7,23},{8,12},{9,25},... | collective-permute-start | bytes 912392 | tf_op jit(solution)/shard_map/ppermute | solution.py:28
  28.1 19.2 %collective-permute-start.6 = (bf16[144,4224]{1,0:T(8,128)(2,1)S(1)}, bf16[144,4224]{1,0:T(8,128)(2,1)S(1)}, u32[]{:S(2)}, u32[]{:S(2)}) collective-permute-start(bf16[144,4224]{1,0:T(8,128)(2,1)S(1)} %pad_add_fusion.refs_1_), channel_id=1, source_target_pairs={{0,8},{1,3},{2,10},{3,5},{4,12},{5,7},{6,14},{7,1},{8,16},{9,11},{... | collective-permute-start | bytes 3649544 | tf_op jit(solution)/shard_map/ppermute | solution.py:32
  30.1 18.3 %collective-permute-start.7 = (bf16[144,4224]{1,0:T(8,128)(2,1)S(1)}, bf16[144,4224]{1,0:T(8,128)(2,1)}, u32[]{:S(2)}, u32[]{:S(2)}) collective-permute-start(bf16[144,4224]{1,0:T(8,128)(2,1)S(1)} %pad_add_fusion.refs_1_), channel_id=1, source_target_pairs={{0,24},{1,7},{2,26},{3,1},{4,28},{5,3},{6,30},{7,5},{8,0},{9,15},{... | collective-permute-start | bytes 3649544 | tf_op jit(solution)/shard_map/ppermute | solution.py:32
  48.4 18.1 %collective-permute-start.10 = (bf16[80,4224]{1,0:T(8,128)(2,1)S(1)}, bf16[80,4224]{1,0:T(8,128)(2,1)S(1)}, u32[]{:S(2)}, u32[]{:S(2)}) collective-permute-start(bf16[80,4224]{1,0:T(8,128)(2,1)S(1)} %slice.49), channel_id=1, source_target_pairs={{0,8},{1,3},{2,10},{3,5},{4,12},{5,7},{6,14},{7,1},{8,16},{9,11},{... | collective-permute-start | bytes 2027528 | tf_op jit(solution)/shard_map/ppermute | solution.py:32
  51.6 14.9 %collective-permute-start.11 = (bf16[64,4224]{1,0:T(8,128)(2,1)S(1)}, bf16[64,4224]{1,0:T(8,128)(2,1)S(1)}, u32[]{:S(2)}, u32[]{:S(2)}) collective-permute-start(bf16[64,4224]{1,0:T(8,128)(2,1)S(1)} %slice.50), channel_id=1, source_target_pairs={{0,24},{1,7},{2,26},{3,1},{4,28},{5,3},{6,30},{7,5},{8,0},{9,15},{... | collective-permute-start | bytes 1622024 | tf_op jit(solution)/shard_map/ppermute | solution.py:32
  66.5 11.5 %collective-permute-start.13 = (bf16[80,4096]{1,0:T(8,128)(2,1)S(1)}, bf16[80,4096]{1,0:T(8,128)(2,1)S(1)}, u32[]{:S(2)}, u32[]{:S(2)}) collective-permute-start(bf16[80,4096]{1,0:T(8,128)(2,1)S(1)} %get-tuple-element.61), channel_id=1, source_target_pairs={{0,24},{1,7},{2,26},{3,1},{4,28},{5,3},{6,30},{7,5},{8,0},{9,15},{... | collective-permute-start | bytes 1966088 | tf_op jit(solution)/shard_map/ppermute | solution.py:32
  67.5 10.4 %collective-permute-start.12 = (bf16[64,4096]{1,0:T(8,128)(2,1)S(1)}, bf16[64,4096]{1,0:T(8,128)(2,1)S(1)}, u32[]{:S(2)}, u32[]{:S(2)}) collective-permute-start(bf16[64,4096]{1,0:T(8,128)(2,1)S(1)} %get-tuple-element.60), channel_id=1, source_target_pairs={{0,8},{1,3},{2,10},{3,5},{4,12},{5,7},{6,14},{7,1},{8,16},{9,11},{... | collective-permute-start | bytes 1572872 | tf_op jit(solution)/shard_map/ppermute | solution.py:32
  77.9 9.2 %collective-permute-start.16 = (bf16[64,4096]{1,0:T(8,128)(2,1)S(1)}, bf16[64,4096]{1,0:T(8,128)(2,1)S(1)}, u32[]{:S(2)}, u32[]{:S(2)}) collective-permute-start(bf16[64,4096]{1,0:T(8,128)(2,1)S(1)} %get-tuple-element.74), channel_id=1, source_target_pairs={{0,24},{1,7},{2,26},{3,1},{4,28},{5,3},{6,30},{7,5},{8,0},{9,15},{... | collective-permute-start | bytes 1572872 | tf_op jit(solution)/shard_map/ppermute | solution.py:32
  79.3 11.8 %collective-permute-start.14 = (bf16[80,4096]{1,0:T(8,128)(2,1)S(1)}, bf16[80,4096]{1,0:T(8,128)(2,1)S(1)}, u32[]{:S(2)}, u32[]{:S(2)}) collective-permute-start(bf16[80,4096]{1,0:T(8,128)(2,1)S(1)} %get-tuple-element.66), channel_id=1, source_target_pairs={{0,8},{1,3},{2,10},{3,5},{4,12},{5,7},{6,14},{7,1},{8,16},{9,11},{... | collective-permute-start | bytes 1966088 | tf_op jit(solution)/shard_map/ppermute | solution.py:32
  87.2 11.5 %collective-permute-start.17 = (bf16[64,4096]{1,0:T(8,128)(2,1)S(1)}, bf16[64,4096]{1,0:T(8,128)(2,1)S(1)}, u32[]{:S(2)}, u32[]{:S(2)}) collective-permute-start(bf16[64,4096]{1,0:T(8,128)(2,1)S(1)} %add_convert_fusion.1), channel_id=1, source_target_pairs={{0,24},{1,7},{2,26},{3,1},{4,28},{5,3},{6,30},{7,5},{8,0},{9,15},{... | collective-permute-start | bytes 1572872 | tf_op jit(solution)/shard_map/ppermute | solution.py:32
  91.3 14.8 %collective-permute-start.15 = (bf16[80,4096]{1,0:T(8,128)(2,1)S(1)}, bf16[80,4096]{1,0:T(8,128)(2,1)S(1)}, u32[]{:S(2)}, u32[]{:S(2)}) collective-permute-start(bf16[80,4096]{1,0:T(8,128)(2,1)S(1)} %add_convert_fusion), channel_id=1, source_target_pairs={{0,8},{1,3},{2,10},{3,5},{4,12},{5,7},{6,14},{7,1},{8,16},{9,11},{... | collective-permute-start | bytes 1966088 | tf_op jit(solution)/shard_map/ppermute | solution.py:32
  99.1 7.3 %collective-permute-start.18 = (bf16[18,4096]{1,0:T(8,128)(2,1)S(1)}, bf16[18,4096]{1,0:T(8,128)(2,1)S(1)}, u32[]{:S(2)}, u32[]{:S(2)}) collective-permute-start(bf16[18,4096]{1,0:T(8,128)(2,1)S(1)} %get-tuple-element.93), channel_id=1, source_target_pairs={{0,2},{1,9},{2,4},{3,11},{4,6},{5,13},{6,0},{7,15},{8,10},{9,17},{... | collective-permute-start | bytes 442376 | tf_op jit(solution)/shard_map/ppermute | solution.py:28
  100.9 8.2 %collective-permute-start.20 = (bf16[18,4096]{1,0:T(8,128)(2,1)S(1)}, bf16[18,4096]{1,0:T(8,128)(2,1)S(1)}, u32[]{:S(2)}, u32[]{:S(2)}) collective-permute-start(bf16[18,4096]{1,0:T(8,128)(2,1)S(1)} %get-tuple-element.94), channel_id=1, source_target_pairs={{0,6},{1,25},{2,0},{3,27},{4,2},{5,29},{6,4},{7,31},{8,14},{9,1},{... | collective-permute-start | bytes 442376 | tf_op jit(solution)/shard_map/ppermute | solution.py:28
  106.4 8.4 %collective-permute-start.19 = (bf16[36,4096]{1,0:T(8,128)(2,1)S(1)}, bf16[36,4096]{1,0:T(8,128)(2,1)S(1)}, u32[]{:S(2)}, u32[]{:S(2)}) collective-permute-start(bf16[36,4096]{1,0:T(8,128)(2,1)S(1)} %fusion.30), channel_id=1, source_target_pairs={{0,2},{1,9},{2,4},{3,11},{4,6},{5,13},{6,0},{7,15},{8,10},{9,17},{... | collective-permute-start | bytes 884744 | tf_op jit(solution)/shard_map/ppermute | solution.py:28
  109.1 7.1 %collective-permute-start.21 = (bf16[36,4096]{1,0:T(8,128)(2,1)S(1)}, bf16[36,4096]{1,0:T(8,128)(2,1)S(1)}, u32[]{:S(2)}, u32[]{:S(2)}) collective-permute-start(bf16[36,4096]{1,0:T(8,128)(2,1)S(1)} %fusion.27), channel_id=1, source_target_pairs={{0,6},{1,25},{2,0},{3,27},{4,2},{5,29},{6,4},{7,31},{8,14},{9,1},{... | collective-permute-start | bytes 884744 | tf_op jit(solution)/shard_map/ppermute | solution.py:28
  116.5 8.1 %collective-permute-start.22 = (bf16[12,4096]{1,0:T(8,128)(2,1)S(1)}, bf16[12,4096]{1,0:T(8,128)(2,1)S(1)}, u32[]{:S(2)}, u32[]{:S(2)}) collective-permute-start(bf16[12,4096]{1,0:T(8,128)(2,1)S(1)} %get-tuple-element.97), channel_id=1, source_target_pairs={{96,0},{97,1},{98,2},{99,3},{100,4},{101,5},{102,6},{103,7},{104,8... | collective-permute-start | bytes 294920 | tf_op jit(solution)/shard_map/ppermute | solution.py:36
  117.8 6.8 %collective-permute-start.23 = (bf16[12,4096]{1,0:T(8,128)(2,1)S(1)}, bf16[12,4096]{1,0:T(8,128)(2,1)S(1)}, u32[]{:S(2)}, u32[]{:S(2)}) collective-permute-start(bf16[12,4096]{1,0:T(8,128)(2,1)S(1)} %get-tuple-element.95), channel_id=1, source_target_pairs={{96,32},{97,33},{98,34},{99,35},{100,36},{101,37},{102,38},{103,39... | collective-permute-start | bytes 294920 | tf_op jit(solution)/shard_map/ppermute | solution.py:36
  118.4 6.1 %collective-permute-start.24 = (bf16[12,4096]{1,0:T(8,128)(2,1)S(1)}, bf16[12,4096]{1,0:T(8,128)(2,1)S(1)}, u32[]{:S(2)}, u32[]{:S(2)}) collective-permute-start(bf16[12,4096]{1,0:T(8,128)(2,1)S(1)} %get-tuple-element.96), channel_id=1, source_target_pairs={{96,64},{97,65},{98,66},{99,67},{100,68},{101,69},{102,70},{103,71... | collective-permute-start | bytes 294920 | tf_op jit(solution)/shard_map/ppermute | solution.py:36
  (8 other events, 47.5 us)

commit v5 on v4

--- a/solution.py
+++ b/solution.py
@@ -96,9 +96,14 @@
     return (mixture / denominator[..., None]).astype(jnp.bfloat16).reshape(count_req, -1)
 
 
-def pack_kernel(experts, hidden, routes, gates, out):
+def pack_kernel(experts, hidden, routes_in, gates_in, out, routes, gates, sems):
     count, width = hidden.shape
-    out[:, :width] = hidden[...]
+    pairs = ((routes_in, routes), (gates_in, gates), (hidden, out.at[:, :width]))
+    copies = [pltpu.make_async_copy(*pair, sems.at[i]) for i, pair in enumerate(pairs)]
+    for copy in copies:
+        copy.start()
+    copies[0].wait()
+    copies[1].wait()
     combine = gates[...] / jnp.sum(gates[...], axis=0, keepdims=True)
     place = lax.broadcasted_iota(jnp.int32, (EXTRA, count), 0)
     share = jnp.zeros((EXTRA, count), jnp.float32)
@@ -121,6 +126,7 @@
         preferred_element_type=jnp.float32,
     )
     out[:, width:] = turned.astype(jnp.bfloat16)
+    copies[2].wait()
 
 
 def token_rows(hidden, routes, gates, experts):
@@ -128,34 +134,47 @@
     whole = pl.BlockSpec(memory_space=pltpu.VMEM)
     return pl.pallas_call(
         functools.partial(pack_kernel, experts),
-        in_specs=[whole] * 3,
+        in_specs=[pl.BlockSpec(memory_space=pl.ANY)] * 3,
         out_specs=whole,
         out_shape=jax.ShapeDtypeStruct((count, width + EXTRA), hidden.dtype),
+        scratch_shapes=[
+            pltpu.VMEM(routes.shape[::-1], routes.dtype),
+            pltpu.VMEM(gates.shape[::-1], gates.dtype),
+            pltpu.SemaphoreType.DMA((3,)),
+        ],
         compiler_params=pltpu.CompilerParams(vmem_limit_bytes=VMEM_LIMIT),
-    )(hidden, routes.T, gates.T)
+    )(*(pltpu.with_memory_space_constraint(w, pltpu.HBM) for w in (hidden, routes.T, gates.T)))
+
+
+def weight_copies(gate_up, down, kept, sems):
+    inner = down.shape[0]
+    sources = (gate_up.at[:, :inner], gate_up.at[:, inner:], down)
+    return [pltpu.make_async_copy(*pair, sems.at[i]) for i, pair in enumerate(zip(sources, kept))]
+
+
+def kept_shapes(gate_up, down):
+    inner, width = down.shape
+    shapes = [(width, inner), (width, inner), (inner, width)]
+    return [pltpu.VMEM(shape, down.dtype) for shape in shapes]
 
 
 def expert_kernel(parts, outputs, columns, load, *refs):
     refs = list(refs)
     pick = refs.pop(0)
     rows_in = [refs.pop(0) for _ in parts]
-    weights = [refs.pop(0) for _ in range(4 if load else 6)]
+    halves = [[refs.pop(0) for _ in range(2 if load else 3)] for _ in range(2)]
     outs = [refs.pop(0) for _ in range(outputs)]
     copies = []
     if load:
-        (gate_up, down, gate_up_other, down_other), weights = weights, [refs.pop(0) for _ in range(6)]
+        kept = [[refs.pop(0) for _ in range(3)] for _ in range(2)]
         sems = refs.pop()
-        sources = []
-        for both in (gate_up, gate_up_other):
-            inner = both.shape[1] // 2
-            sources += [both.at[:, :inner], both.at[:, inner:]]
-        sources += [down, down_other]
-        for i, (source, kept) in enumerate(zip(sources, weights)):
-            copies.append(pltpu.make_async_copy(source, kept, sems.at[i]))
-            copies[-1].start()
+        for half in range(2):
+            copies += weight_copies(*halves[half], kept[half], sems.at[half])
+        halves = kept
+        for index in (0, 1, 3, 4, 2, 5):
+            copies[index].start()
     rows, act, share = refs
-    gate_ups, (down_own, down_other) = (weights[:2], weights[2:4]), weights[4:]
-    inner, width = down_own.shape
+    inner, width = halves[0][2].shape
 
     def arrived(index):
         if load:
@@ -170,20 +189,20 @@
         )
         start += size
 
-    for half, (gate, up) in enumerate(gate_ups):
-        arrived(2 * half)
+    for half, (gate, up, _) in enumerate(halves):
+        arrived(3 * half)
         left = jnp.dot(rows[...], gate[...], preferred_element_type=jnp.float32)
-        arrived(2 * half + 1)
+        arrived(3 * half + 1)
         right = jnp.dot(rows[...], up[...], preferred_element_type=jnp.float32)
         act[:, half * inner : (half + 1) * inner] = (jax.nn.silu(left) * right).astype(jnp.bfloat16)
-    arrived(4)
+    arrived(2)
     arrived(5)
 
     @pl.loop(0, width // columns)
     def _(n):
         at = pl.ds(pl.multiple_of(n * columns, columns), columns)
-        total = jnp.dot(act[:, :inner], down_own[:, at], preferred_element_type=jnp.float32)
-        total += jnp.dot(act[:, inner:], down_other[:, at], preferred_element_type=jnp.float32)
+        total = jnp.dot(act[:, :inner], halves[0][2][:, at], preferred_element_type=jnp.float32)
+        total += jnp.dot(act[:, inner:], halves[1][2][:, at], preferred_element_type=jnp.float32)
         total = (total * share[...]).astype(jnp.bfloat16)
         start = 0
         for out in outs:
@@ -191,20 +210,20 @@
             start += out.shape[0]
 
 
-def experts_on(parts, sizes, pick, weights, load=False):
-    inner, width = weights[-1].shape
+def experts_on(parts, sizes, pick, halves):
+    inner, width = halves[0][-1].shape
+    load = len(halves[0]) == 2
     count = sum(sizes)
     pieces = [piece for piece, _, _ in parts]
     taken = tuple((first, size) for _, first, size in parts)
-    space = pltpu.HBM if load else pltpu.VMEM
-    held = [pltpu.with_memory_space_constraint(w, space) for w in weights]
     whole = pl.BlockSpec(memory_space=pltpu.VMEM)
-    there = pl.BlockSpec(memory_space=pl.ANY) if load else whole
-    kept = [(width, inner)] * 4 + [(inner, width)] * 2 if load else []
-    kept = [pltpu.VMEM(shape, jnp.bfloat16) for shape in kept]
+    space = pl.BlockSpec(memory_space=pl.ANY) if load else whole
+    constraint = pltpu.HBM if load else pltpu.VMEM
+    held = [pltpu.with_memory_space_constraint(w, constraint) for half in halves for w in half]
+    kept = [shape for half in halves for shape in kept_shapes(*half)] if load else []
     outs = pl.pallas_call(
         functools.partial(expert_kernel, taken, len(sizes), 1024, load),
-        in_specs=[whole] * (1 + len(pieces)) + [there] * len(weights),
+        in_specs=[whole] * (1 + len(pieces)) + [space] * len(held),
         out_specs=[whole] * (len(sizes) + len(kept)),
         out_shape=[jax.ShapeDtypeStruct((size, width), jnp.bfloat16) for size in sizes] + kept,
         scratch_shapes=[
@@ -212,7 +231,7 @@
             pltpu.VMEM((count, 2 * inner), jnp.bfloat16),
             pltpu.VMEM((count, 1), jnp.float32),
         ]
-        + ([pltpu.SemaphoreType.DMA((6,))] if load else []),
+        + ([pltpu.SemaphoreType.DMA((2, 3))] if load else []),
         compiler_params=pltpu.CompilerParams(vmem_limit_bytes=VMEM_LIMIT),
         cost_estimate=pl.CostEstimate(
             flops=12 * count * width * inner,
@@ -220,7 +239,8 @@
             transcendentals=2 * count * inner,
         ),
     )(pick, *pieces, *held)
-    return outs[: len(sizes)], outs[len(sizes) :]
+    kept = outs[len(sizes) :]
+    return outs[: len(sizes)], (kept[:3], kept[3:]) if load else halves
 
 
 def per_device(
@@ -235,10 +255,11 @@
     f32 = jnp.float32
 
     gate_up, down = w_gate_up[0], w_down[0]
-    weights = (gate_up, down, other_core(gate_up), other_core(down))
+    halves = ((gate_up, down), (other_core(gate_up), other_core(down)))
 
     packed = token_rows(hidden, routes, gates, experts)
-    block = jnp.concatenate([to_section(packed, s, sections - 1) for s in range(sections - 1)], axis=0)
+    blocks = [to_section(packed, s, sections - 1) for s in range(sections - 1)]
+    block = jnp.concatenate(blocks, axis=0)
 
     group = stacked([block, step_u(block, 1), step_u(block, -1), step_u(block, 2)])
     size = group.shape[0]
@@ -247,22 +268,22 @@
     before, after = step_v(group, 1), step_v(group, -1)
     column = lax.broadcasted_iota(jnp.int32, (1, EXTRA), 1)
     pick = ((column % experts == expert) & (column < 3 * experts)).astype(f32)
-    (own_a, own_b), kept = experts_on([(group, 0, size)], (cut, rest), pick, weights, load=True)
+    (own_a, own_b), halves = experts_on([(group, 0, size)], (cut, rest), pick, halves)
 
     before, after, own_a, own_b = lax.optimization_barrier((before, after, own_a, own_b))
     across_a, across_b = step_v(before[:cut], 1), step_v(after[cut:], -1)
-    (after_a, after_b, before_a, before_b), _ = experts_on(
-        [(after, 0, size), (before, 0, size)], (cut, rest, cut, rest), pick, kept
-    )
-    across_a, across_b, after_a, after_b, before_a, before_b = lax.optimization_barrier(
-        (across_a, across_b, after_a, after_b, before_a, before_b)
-    )
+    (after_b, before_a), _ = experts_on([(after, cut, rest), (before, 0, cut)], (rest, cut), pick, halves)
+    across_a, across_b, after_b, before_a = lax.optimization_barrier((across_a, across_b, after_b, before_a))
+
     from_after_b, from_before_a = step_v(after_b, 1), step_v(before_a, -1)
-    (cross_a, cross_b), _ = experts_on([(across_a, 0, cut), (across_b, 0, rest)], (cut, rest), pick, kept)
-    from_after_b, from_before_a, cross_a, cross_b = lax.optimization_barrier(
-        (from_after_b, from_before_a, cross_a, cross_b)
+    (cross_a, cross_b), _ = experts_on(
+        [(across_a, 0, cut), (across_b, 0, rest)], (cut, rest), pick, halves
     )
     from_cross_a, from_cross_b = step_v(cross_a, 1), step_v(cross_b, -1)
+    after, before, from_after_b, from_before_a, cross_a = lax.optimization_barrier(
+        (after, before, from_after_b, from_before_a, cross_a)
+    )
+    (after_a, before_b), _ = experts_on([(after, 0, cut), (before, cut, rest)], (cut, rest), pick, halves)
 
     query, _ = lax.optimization_barrier((query, cross_a))
     attention_out = lax.cond(

time: 126 us -> 120 us (0.952)
  waiting for transfers between devices: 42.8 us -> 30 us
  Pallas kernels: 34.7 us -> 40.2 us
    ppermute x10, waiting for transfers between devices: 23 us -> 10.5 us  [step_v(): return lax.ppermute(block, 'dev', along(False, distance))]
    pallas_call x3 -> x4, Pallas kernels: 34.6 us -> 39.2 us  [experts_on(): pl.pallas_call(functools.partial(expert_kernel, taken, len(sizes), 1024,...]
    unnamed x14 -> x8, local copies, waits for them, and re-layouts: 2.3 us -> 0.03 us
  transfers between devices with their start and end apart: 25 -> 25, of which waited for: 13 -> 11; matrix products, arithmetic and copies ran while one was open for 5% -> 7% of each run, Pallas kernels for 28% -> 34%
where the time goes in v5:
time: 120 us; the launch traced here: 119 us
  Pallas kernels  40.2 us (34%)
  starting transfers between devices  37.7 us (31%)
  waiting for transfers between devices  30 us (25%)
  local copies, waits for them, and re-layouts  5.21 us (4%)
  other arithmetic  3.38 us (3%)
  matrix products  1.33 us (1%)
    pallas_call x4, Pallas kernels, experts_on(): pl.pallas_call(functools.partial(expert_kernel, taken, len(sizes), 1024,...  39.2 us
    ppermute x10, starting transfers between devices, step_v(): return lax.ppermute(block, 'dev', along(False, distance))  16.3 us
    ppermute x7, waiting for transfers between devices, step_u(): return lax.ppermute(block, 'dev', along(True, distance))  14 us
    ppermute x7, starting transfers between devices, step_u(): return lax.ppermute(block, 'dev', along(True, distance))  11.9 us
    ppermute x10, waiting for transfers between devices, step_v(): return lax.ppermute(block, 'dev', along(False, distance))  10.5 us
    ppermute x6, starting transfers between devices, to_section(): return lax.ppermute(block, 'sec', [(source, target)])  8.98 us
    ppermute x6, waiting for transfers between devices, to_section(): return lax.ppermute(block, 'sec', [(source, target)])  5.51 us
    another operation x1, local copies, waits for them, and re-layouts  2.74 us
  transfers between devices with their start and end apart: 25, of which 11 were waited for; matrix products, arithmetic and copies ran while one was open for 7% of the time, Pallas kernels for 34%

profile of v5, /device:TPU:0, one launch (start us, length us, event | category | flops | bytes accessed | tf_op | source)
XLA Modules:
  0.0 118.8 jit_solution(6436328023140421832)
XLA Ops:
  2.2 5.0 %collective-permute-start = (bf16[12,4224]{1,0:T(8,128)(2,1)S(1)}, bf16[12,4224]{1,0:T(8,128)(2,1)S(1)}, u32[]{:S(2)}, u32[]{:S(2)}) collective-permute-start(bf16[12,4224]{1,0:T(8,128)(2,1)S(1)} %shard_map.107), channel_id=1, source_target_pairs={{0,96},{1,97},{2,98},{3,99},{4,100},{5,101},{6,102},{7,103},{8,104... | collective-permute-start | bytes 304136 | tf_op jit(solution)/shard_map/ppermute | solution.py:36
  8.6 4.7 %collective-permute-done = bf16[12,4224]{1,0:T(8,128)(2,1)S(1)} collective-permute-done((bf16[12,4224]{1,0:T(8,128)(2,1)S(1)}, bf16[12,4224]{1,0:T(8,128)(2,1)S(1)}, u32[]{:S(2)}, u32[]{:S(2)}) %collective-permute-start) | collective-permute-done | bytes 101408 | tf_op jit(solution)/shard_map/ppermute | solution.py:36
  13.3 1.6 %collective-permute-start.3 = (bf16[36,4224]{1,0:T(8,128)(2,1)S(1)}, bf16[36,4224]{1,0:T(8,128)(2,1)S(1)}, u32[]{:S(2)}, u32[]{:S(2)}) collective-permute-start(bf16[36,4224]{1,0:T(8,128)(2,1)S(1)} %pad_maximum_fusion), channel_id=1, source_target_pairs={{0,2},{1,9},{2,4},{3,11},{4,6},{5,13},{6,0},{7,15},{8,10},{9,17},{... | collective-permute-start | bytes 912392 | tf_op jit(solution)/shard_map/ppermute | solution.py:28
  14.9 1.7 %collective-permute-start.4 = (bf16[36,4224]{1,0:T(8,128)(2,1)S(1)}, bf16[36,4224]{1,0:T(8,128)(2,1)S(1)}, u32[]{:S(2)}, u32[]{:S(2)}) collective-permute-start(bf16[36,4224]{1,0:T(8,128)(2,1)S(1)} %pad_maximum_fusion), channel_id=1, source_target_pairs={{0,6},{1,25},{2,0},{3,27},{4,2},{5,29},{6,4},{7,31},{8,14},{9,1},{... | collective-permute-start | bytes 912392 | tf_op jit(solution)/shard_map/ppermute | solution.py:28
  16.6 1.8 %collective-permute-start.5 = (bf16[36,4224]{1,0:T(8,128)(2,1)S(1)}, bf16[36,4224]{1,0:T(8,128)(2,1)S(1)}, u32[]{:S(2)}, u32[]{:S(2)}) collective-permute-start(bf16[36,4224]{1,0:T(8,128)(2,1)S(1)} %pad_maximum_fusion), channel_id=1, source_target_pairs={{0,4},{1,17},{2,6},{3,19},{4,0},{5,21},{6,2},{7,23},{8,12},{9,25},... | collective-permute-start | bytes 912392 | tf_op jit(solution)/shard_map/ppermute | solution.py:28
  18.4 3.3 %collective-permute-done.3 = bf16[36,4224]{1,0:T(8,128)(2,1)S(1)} collective-permute-done((bf16[36,4224]{1,0:T(8,128)(2,1)S(1)}, bf16[36,4224]{1,0:T(8,128)(2,1)S(1)}, u32[]{:S(2)}, u32[]{:S(2)}) %collective-permute-start.3) | collective-permute-done | bytes 304160 | tf_op jit(solution)/shard_map/ppermute | solution.py:28
  21.8 3.2 %collective-permute-done.4 = bf16[36,4224]{1,0:T(8,128)(2,1)S(1)} collective-permute-done((bf16[36,4224]{1,0:T(8,128)(2,1)S(1)}, bf16[36,4224]{1,0:T(8,128)(2,1)S(1)}, u32[]{:S(2)}, u32[]{:S(2)}) %collective-permute-start.4) | collective-permute-done | bytes 304160 | tf_op jit(solution)/shard_map/ppermute | solution.py:28
  27.7 1.9 %collective-permute-start.6 = (bf16[144,4224]{1,0:T(8,128)(2,1)}, bf16[144,4224]{1,0:T(8,128)(2,1)}, u32[]{:S(2)}, u32[]{:S(2)}) collective-permute-start(bf16[144,4224]{1,0:T(8,128)(2,1)} %pad_add_fusion.refs_1_), channel_id=1, source_target_pairs={{0,8},{1,3},{2,10},{3,5},{4,12},{5,7},{6,14},{7,1},{8,16},{9,11},{... | collective-permute-start | bytes 3649544 | tf_op jit(solution)/shard_map/ppermute | solution.py:32
  29.6 2.1 %collective-permute-start.7 = (bf16[144,4224]{1,0:T(8,128)(2,1)}, bf16[144,4224]{1,0:T(8,128)(2,1)}, u32[]{:S(2)}, u32[]{:S(2)}) collective-permute-start(bf16[144,4224]{1,0:T(8,128)(2,1)} %pad_add_fusion.refs_1_), channel_id=1, source_target_pairs={{0,24},{1,7},{2,26},{3,1},{4,28},{5,3},{6,30},{7,5},{8,0},{9,15},{... | collective-permute-start | bytes 3649544 | tf_op jit(solution)/shard_map/ppermute | solution.py:32
  31.8 15.8 %shard_map.108 = (bf16[80,4096]{1,0:T(8,128)(2,1)S(1)}, bf16[64,4096]{1,0:T(8,128)(2,1)S(1)}, bf16[4096,768]{1,0:T(8,128)(2,1)S(1)}, bf16[4096,768]{1,0:T(8,128)...) custom-call(f32[1,128]{1,0:T(1,128)S(1)} %and_convert_fusion.refs_0_, ...), custom_call_target="tpu_custom_call" | custom-call | flops 5435817984 | bytes 37748736 | tf_op jit(solution)/shard_map/pallas_call | solution.py:224
  51.2 2.2 %collective-permute-start.11 = (bf16[64,4224]{1,0:T(8,128)(2,1)S(1)}, bf16[64,4224]{1,0:T(8,128)(2,1)S(1)}, u32[]{:S(2)}, u32[]{:S(2)}) collective-permute-start(bf16[64,4224]{1,0:T(8,128)(2,1)S(1)} %slice.50), channel_id=1, source_target_pairs={{0,24},{1,7},{2,26},{3,1},{4,28},{5,3},{6,30},{7,5},{8,0},{9,15},{... | collective-permute-start | bytes 1622024 | tf_op jit(solution)/shard_map/ppermute | solution.py:32
  53.4 8.3 %shard_map.109 = (bf16[64,4096]{1,0:T(8,128)(2,1)S(1)}, bf16[80,4096]{1,0:T(8,128)(2,1)S(1)}) custom-call(f32[1,128]{1,0:T(1,128)S(1)} %and_convert_fusion.refs_0_, bf16[144,4224]{1,0:T(8,128)(2,1)} %collective-permute-done.7.refs_1_, bf16[144,4224]{1,0:T(8,128)(2,1)} %collective-permute-done.6.refs_2_, bf16[4096,768]{1,0:T(8,128)(2,1)S(1)} %get-tuple-element.48.refs_3_, ...), custom_call_target="tpu_custom_call" | custom-call | flops 5435817984 | bytes 2359296 | tf_op jit(solution)/shard_map/pallas_call | solution.py:224
  61.7 2.3 %collective-permute-start.13 = (bf16[80,4096]{1,0:T(8,128)(2,1)S(1)}, bf16[80,4096]{1,0:T(8,128)(2,1)S(1)}, u32[]{:S(2)}, u32[]{:S(2)}) collective-permute-start(bf16[80,4096]{1,0:T(8,128)(2,1)S(1)} %get-tuple-element.57), channel_id=1, source_target_pairs={{0,24},{1,7},{2,26},{3,1},{4,28},{5,3},{6,30},{7,5},{8,0},{9,15},{... | collective-permute-start | bytes 1966088 | tf_op jit(solution)/shard_map/ppermute | solution.py:32
  64.0 6.8 %shard_map.110 = (bf16[80,4096]{1,0:T(8,128)(2,1)S(1)}, bf16[64,4096]{1,0:T(8,128)(2,1)S(1)}) custom-call(f32[1,128]{1,0:T(1,128)S(1)} %and_convert_fusion.refs_0_, bf16[80,4224]{1,0:T(8,128)(2,1)S(1)} %collective-permute-done.10.refs_1_, bf16[64,4224]{1,0:T(8,128)(2,1)S(1)} %collective-permute-done.11.refs_2_, ...), custom_call_target="tpu_custom_call" | custom-call | flops 5435817984 | bytes 2359296 | tf_op jit(solution)/shard_map/pallas_call | solution.py:224
  70.8 3.3 %collective-permute-start.16 = (bf16[64,4096]{1,0:T(8,128)(2,1)S(1)}, bf16[64,4096]{1,0:T(8,128)(2,1)S(1)}, u32[]{:S(2)}, u32[]{:S(2)}) collective-permute-start(bf16[64,4096]{1,0:T(8,128)(2,1)S(1)} %get-tuple-element.68), channel_id=1, source_target_pairs={{0,24},{1,7},{2,26},{3,1},{4,28},{5,3},{6,30},{7,5},{8,0},{9,15},{... | collective-permute-start | bytes 1572872 | tf_op jit(solution)/shard_map/ppermute | solution.py:32
  74.4 8.3 %shard_map.111 = (bf16[80,4096]{1,0:T(8,128)(2,1)S(1)}, bf16[64,4096]{1,0:T(8,128)(2,1)S(1)}) custom-call(f32[1,128]{1,0:T(1,128)S(1)} %and_convert_fusion.refs_0_, bf16[144,4224]{1,0:T(8,128)(2,1)} %collective-permute-done.7.refs_1_, bf16[144,4224]{1,0:T(8,128)(2,1)} %collective-permute-done.6.refs_2_, bf16[4096,768]{1,0:T(8,128)(2,1)S(1)} %get-tuple-element.48.refs_3_, ...), custom_call_target="tpu_custom_call" | custom-call | flops 5435817984 | bytes 2359296 | tf_op jit(solution)/shard_map/pallas_call | solution.py:224
  82.8 3.0 %collective-permute-start.17 = (bf16[64,4096]{1,0:T(8,128)(2,1)S(1)}, bf16[64,4096]{1,0:T(8,128)(2,1)S(1)}, u32[]{:S(2)}, u32[]{:S(2)}) collective-permute-start(bf16[64,4096]{1,0:T(8,128)(2,1)S(1)} %add_convert_fusion.1), channel_id=1, source_target_pairs={{0,24},{1,7},{2,26},{3,1},{4,28},{5,3},{6,30},{7,5},{8,0},{9,15},{... | collective-permute-start | bytes 1572872 | tf_op jit(solution)/shard_map/ppermute | solution.py:32
  86.1 7.2 %collective-permute-done.17 = bf16[64,4096]{1,0:T(8,128)(2,1)S(1)} collective-permute-done((bf16[64,4096]{1,0:T(8,128)(2,1)S(1)}, bf16[64,4096]{1,0:T(8,128)(2,1)S(1)}, u32[]{:S(2)}, u32[]{:S(2)}) %collective-permute-start.17) | collective-permute-done | bytes 524320 | tf_op jit(solution)/shard_map/ppermute | solution.py:32
  93.6 2.9 %collective-permute-start.18 = (bf16[18,4096]{1,0:T(8,128)(2,1)S(1)}, bf16[18,4096]{1,0:T(8,128)(2,1)S(1)}, u32[]{:S(2)}, u32[]{:S(2)}) collective-permute-start(bf16[18,4096]{1,0:T(8,128)(2,1)S(1)} %get-tuple-element.87), channel_id=1, source_target_pairs={{0,2},{1,9},{2,4},{3,11},{4,6},{5,13},{6,0},{7,15},{8,10},{9,17},{... | collective-permute-start | bytes 442376 | tf_op jit(solution)/shard_map/ppermute | solution.py:28
  97.0 3.0 %collective-permute-done.15 = bf16[80,4096]{1,0:T(8,128)(2,1)S(1)} collective-permute-done((bf16[80,4096]{1,0:T(8,128)(2,1)S(1)}, bf16[80,4096]{1,0:T(8,128)(2,1)S(1)}, u32[]{:S(2)}, u32[]{:S(2)}) %collective-permute-start.15) | collective-permute-done | bytes 655392 | tf_op jit(solution)/shard_map/ppermute | solution.py:32
  100.6 2.0 %collective-permute-start.19 = (bf16[36,4096]{1,0:T(8,128)(2,1)S(1)}, bf16[36,4096]{1,0:T(8,128)(2,1)S(1)}, u32[]{:S(2)}, u32[]{:S(2)}) collective-permute-start(bf16[36,4096]{1,0:T(8,128)(2,1)S(1)} %fusion.30), channel_id=1, source_target_pairs={{0,2},{1,9},{2,4},{3,11},{4,6},{5,13},{6,0},{7,15},{8,10},{9,17},{... | collective-permute-start | bytes 884744 | tf_op jit(solution)/shard_map/ppermute | solution.py:28
  104.1 4.9 %collective-permute-done.19 = bf16[36,4096]{1,0:T(8,128)(2,1)S(1)} collective-permute-done((bf16[36,4096]{1,0:T(8,128)(2,1)S(1)}, bf16[36,4096]{1,0:T(8,128)(2,1)S(1)}, u32[]{:S(2)}, u32[]{:S(2)}) %collective-permute-start.19) | collective-permute-done | bytes 294944 | tf_op jit(solution)/shard_map/ppermute | solution.py:28
  112.8 4.5 %conditional.1 = (bf16[2,8192]{1,0:T(2,128)(2,1)S(1)}) conditional(s32[]{:T(128)} %convert_element_type.87, (s32[2]{0:T(128)S(1)}, bf16[2,8192]{1,0:T(2,128)(2,1)S(1)}, bf16[2,1024,4,256]{3,2,1,0:T(4,128)(2,1)}, bf16[2,4,256]{2,1,0:T(4,128)(2,1)S(1)}) %tuple.36, () %tuple.19), branch_computations={%region_0.3_spmd, %region_3.4_spmd} | conditional | flops 68128512 | bytes 14426640 | solution.py:289
  112.8 2.7 %copy.14 = bf16[2,1024,4,256]{3,1,2,0:T(8,128)(2,1)S(1)} copy(bf16[2,1024,4,256]{3,2,1,0:T(4,128)(2,1)} %get-tuple-element.77) | data formatting | bytes 8388608 | tf_op jit(solution)/shard_map
  (69 shorter events, 19.8 us)
Async XLA Ops:
  0.6 31.1 %collective-permute-start.8 = (bf16[4096,1536]{1,0:T(8,128)(2,1)}, bf16[4096,1536]{1,0:T(8,128)(2,1)}, u32[]{:S(2)}, u32[]{:S(2)}) collective-permute-start(bf16[4096,1536]{1,0:T(8,128)(2,1)} %bitcast.18), channel_id=1, source_target_pairs={{0,1},{1,0},{2,3},{3,2},{4,5},{5,4},{6,7},{7,6},{8,9},{9,8},{10,11... | collective-permute-start | bytes 37748744 | tf_op jit(solution)/shard_map/ppermute | solution.py:51
  0.7 31.0 %collective-permute-start.9 = (bf16[768,4096]{1,0:T(8,128)(2,1)}, bf16[768,4096]{1,0:T(8,128)(2,1)}, u32[]{:S(2)}, u32[]{:S(2)}) collective-permute-start(bf16[768,4096]{1,0:T(8,128)(2,1)} %bitcast.20), channel_id=1, source_target_pairs={{0,1},{1,0},{2,3},{3,2},{4,5},{5,4},{6,7},{7,6},{8,9},{9,8},{10,11... | collective-permute-start | bytes 18874376 | tf_op jit(solution)/shard_map/ppermute | solution.py:51
  2.2 11.0 %collective-permute-start = (bf16[12,4224]{1,0:T(8,128)(2,1)S(1)}, bf16[12,4224]{1,0:T(8,128)(2,1)S(1)}, u32[]{:S(2)}, u32[]{:S(2)}) collective-permute-start(bf16[12,4224]{1,0:T(8,128)(2,1)S(1)} %shard_map.107), channel_id=1, source_target_pairs={{0,96},{1,97},{2,98},{3,99},{4,100},{5,101},{6,102},{7,103},{8,104... | collective-permute-start | bytes 304136 | tf_op jit(solution)/shard_map/ppermute | solution.py:36
  7.2 6.0 %collective-permute-start.1 = (bf16[12,4224]{1,0:T(8,128)(2,1)S(1)}, bf16[12,4224]{1,0:T(8,128)(2,1)S(1)}, u32[]{:S(2)}, u32[]{:S(2)}) collective-permute-start(bf16[12,4224]{1,0:T(8,128)(2,1)S(1)} %shard_map.107), channel_id=1, source_target_pairs={{32,96},{33,97},{34,98},{35,99},{36,100},{37,101},{38,102},{39,103... | collective-permute-start | bytes 304136 | tf_op jit(solution)/shard_map/ppermute | solution.py:36
  13.3 8.5 %collective-permute-start.3 = (bf16[36,4224]{1,0:T(8,128)(2,1)S(1)}, bf16[36,4224]{1,0:T(8,128)(2,1)S(1)}, u32[]{:S(2)}, u32[]{:S(2)}) collective-permute-start(bf16[36,4224]{1,0:T(8,128)(2,1)S(1)} %pad_maximum_fusion), channel_id=1, source_target_pairs={{0,2},{1,9},{2,4},{3,11},{4,6},{5,13},{6,0},{7,15},{8,10},{9,17},{... | collective-permute-start | bytes 912392 | tf_op jit(solution)/shard_map/ppermute | solution.py:28
  14.9 10.1 %collective-permute-start.4 = (bf16[36,4224]{1,0:T(8,128)(2,1)S(1)}, bf16[36,4224]{1,0:T(8,128)(2,1)S(1)}, u32[]{:S(2)}, u32[]{:S(2)}) collective-permute-start(bf16[36,4224]{1,0:T(8,128)(2,1)S(1)} %pad_maximum_fusion), channel_id=1, source_target_pairs={{0,6},{1,25},{2,0},{3,27},{4,2},{5,29},{6,4},{7,31},{8,14},{9,1},{... | collective-permute-start | bytes 912392 | tf_op jit(solution)/shard_map/ppermute | solution.py:28
  16.6 9.8 %collective-permute-start.5 = (bf16[36,4224]{1,0:T(8,128)(2,1)S(1)}, bf16[36,4224]{1,0:T(8,128)(2,1)S(1)}, u32[]{:S(2)}, u32[]{:S(2)}) collective-permute-start(bf16[36,4224]{1,0:T(8,128)(2,1)S(1)} %pad_maximum_fusion), channel_id=1, source_target_pairs={{0,4},{1,17},{2,6},{3,19},{4,0},{5,21},{6,2},{7,23},{8,12},{9,25},... | collective-permute-start | bytes 912392 | tf_op jit(solution)/shard_map/ppermute | solution.py:28
  27.7 19.9 %collective-permute-start.6 = (bf16[144,4224]{1,0:T(8,128)(2,1)}, bf16[144,4224]{1,0:T(8,128)(2,1)}, u32[]{:S(2)}, u32[]{:S(2)}) collective-permute-start(bf16[144,4224]{1,0:T(8,128)(2,1)} %pad_add_fusion.refs_1_), channel_id=1, source_target_pairs={{0,8},{1,3},{2,10},{3,5},{4,12},{5,7},{6,14},{7,1},{8,16},{9,11},{... | collective-permute-start | bytes 3649544 | tf_op jit(solution)/shard_map/ppermute | solution.py:32
  29.6 18.0 %collective-permute-start.7 = (bf16[144,4224]{1,0:T(8,128)(2,1)}, bf16[144,4224]{1,0:T(8,128)(2,1)}, u32[]{:S(2)}, u32[]{:S(2)}) collective-permute-start(bf16[144,4224]{1,0:T(8,128)(2,1)} %pad_add_fusion.refs_1_), channel_id=1, source_target_pairs={{0,24},{1,7},{2,26},{3,1},{4,28},{5,3},{6,30},{7,5},{8,0},{9,15},{... | collective-permute-start | bytes 3649544 | tf_op jit(solution)/shard_map/ppermute | solution.py:32
  48.8 13.0 %collective-permute-start.10 = (bf16[80,4224]{1,0:T(8,128)(2,1)S(1)}, bf16[80,4224]{1,0:T(8,128)(2,1)S(1)}, u32[]{:S(2)}, u32[]{:S(2)}) collective-permute-start(bf16[80,4224]{1,0:T(8,128)(2,1)S(1)} %slice.49), channel_id=1, source_target_pairs={{0,8},{1,3},{2,10},{3,5},{4,12},{5,7},{6,14},{7,1},{8,16},{9,11},{... | collective-permute-start | bytes 2027528 | tf_op jit(solution)/shard_map/ppermute | solution.py:32
  51.2 10.5 %collective-permute-start.11 = (bf16[64,4224]{1,0:T(8,128)(2,1)S(1)}, bf16[64,4224]{1,0:T(8,128)(2,1)S(1)}, u32[]{:S(2)}, u32[]{:S(2)}) collective-permute-start(bf16[64,4224]{1,0:T(8,128)(2,1)S(1)} %slice.50), channel_id=1, source_target_pairs={{0,24},{1,7},{2,26},{3,1},{4,28},{5,3},{6,30},{7,5},{8,0},{9,15},{... | collective-permute-start | bytes 1622024 | tf_op jit(solution)/shard_map/ppermute | solution.py:32
  61.7 12.6 %collective-permute-start.13 = (bf16[80,4096]{1,0:T(8,128)(2,1)S(1)}, bf16[80,4096]{1,0:T(8,128)(2,1)S(1)}, u32[]{:S(2)}, u32[]{:S(2)}) collective-permute-start(bf16[80,4096]{1,0:T(8,128)(2,1)S(1)} %get-tuple-element.57), channel_id=1, source_target_pairs={{0,24},{1,7},{2,26},{3,1},{4,28},{5,3},{6,30},{7,5},{8,0},{9,15},{... | collective-permute-start | bytes 1966088 | tf_op jit(solution)/shard_map/ppermute | solution.py:32
  64.0 10.4 %collective-permute-start.12 = (bf16[64,4096]{1,0:T(8,128)(2,1)S(1)}, bf16[64,4096]{1,0:T(8,128)(2,1)S(1)}, u32[]{:S(2)}, u32[]{:S(2)}) collective-permute-start(bf16[64,4096]{1,0:T(8,128)(2,1)S(1)} %get-tuple-element.56), channel_id=1, source_target_pairs={{0,8},{1,3},{2,10},{3,5},{4,12},{5,7},{6,14},{7,1},{8,16},{9,11},{... | collective-permute-start | bytes 1572872 | tf_op jit(solution)/shard_map/ppermute | solution.py:32
  70.8 11.9 %collective-permute-start.16 = (bf16[64,4096]{1,0:T(8,128)(2,1)S(1)}, bf16[64,4096]{1,0:T(8,128)(2,1)S(1)}, u32[]{:S(2)}, u32[]{:S(2)}) collective-permute-start(bf16[64,4096]{1,0:T(8,128)(2,1)S(1)} %get-tuple-element.68), channel_id=1, source_target_pairs={{0,24},{1,7},{2,26},{3,1},{4,28},{5,3},{6,30},{7,5},{8,0},{9,15},{... | collective-permute-start | bytes 1572872 | tf_op jit(solution)/shard_map/ppermute | solution.py:32
  74.1 11.8 %collective-permute-start.14 = (bf16[80,4096]{1,0:T(8,128)(2,1)S(1)}, bf16[80,4096]{1,0:T(8,128)(2,1)S(1)}, u32[]{:S(2)}, u32[]{:S(2)}) collective-permute-start(bf16[80,4096]{1,0:T(8,128)(2,1)S(1)} %get-tuple-element.60), channel_id=1, source_target_pairs={{0,8},{1,3},{2,10},{3,5},{4,12},{5,7},{6,14},{7,1},{8,16},{9,11},{... | collective-permute-start | bytes 1966088 | tf_op jit(solution)/shard_map/ppermute | solution.py:32
  82.8 10.5 %collective-permute-start.17 = (bf16[64,4096]{1,0:T(8,128)(2,1)S(1)}, bf16[64,4096]{1,0:T(8,128)(2,1)S(1)}, u32[]{:S(2)}, u32[]{:S(2)}) collective-permute-start(bf16[64,4096]{1,0:T(8,128)(2,1)S(1)} %add_convert_fusion.1), channel_id=1, source_target_pairs={{0,24},{1,7},{2,26},{3,1},{4,28},{5,3},{6,30},{7,5},{8,0},{9,15},{... | collective-permute-start | bytes 1572872 | tf_op jit(solution)/shard_map/ppermute | solution.py:32
  86.1 14.0 %collective-permute-start.15 = (bf16[80,4096]{1,0:T(8,128)(2,1)S(1)}, bf16[80,4096]{1,0:T(8,128)(2,1)S(1)}, u32[]{:S(2)}, u32[]{:S(2)}) collective-permute-start(bf16[80,4096]{1,0:T(8,128)(2,1)S(1)} %add_convert_fusion), channel_id=1, source_target_pairs={{0,8},{1,3},{2,10},{3,5},{4,12},{5,7},{6,14},{7,1},{8,16},{9,11},{... | collective-permute-start | bytes 1966088 | tf_op jit(solution)/shard_map/ppermute | solution.py:32
  93.6 6.9 %collective-permute-start.18 = (bf16[18,4096]{1,0:T(8,128)(2,1)S(1)}, bf16[18,4096]{1,0:T(8,128)(2,1)S(1)}, u32[]{:S(2)}, u32[]{:S(2)}) collective-permute-start(bf16[18,4096]{1,0:T(8,128)(2,1)S(1)} %get-tuple-element.87), channel_id=1, source_target_pairs={{0,2},{1,9},{2,4},{3,11},{4,6},{5,13},{6,0},{7,15},{8,10},{9,17},{... | collective-permute-start | bytes 442376 | tf_op jit(solution)/shard_map/ppermute | solution.py:28
  96.5 6.1 %collective-permute-start.20 = (bf16[18,4096]{1,0:T(8,128)(2,1)S(1)}, bf16[18,4096]{1,0:T(8,128)(2,1)S(1)}, u32[]{:S(2)}, u32[]{:S(2)}) collective-permute-start(bf16[18,4096]{1,0:T(8,128)(2,1)S(1)} %get-tuple-element.88), channel_id=1, source_target_pairs={{0,6},{1,25},{2,0},{3,27},{4,2},{5,29},{6,4},{7,31},{8,14},{9,1},{... | collective-permute-start | bytes 442376 | tf_op jit(solution)/shard_map/ppermute | solution.py:28
  100.6 8.4 %collective-permute-start.19 = (bf16[36,4096]{1,0:T(8,128)(2,1)S(1)}, bf16[36,4096]{1,0:T(8,128)(2,1)S(1)}, u32[]{:S(2)}, u32[]{:S(2)}) collective-permute-start(bf16[36,4096]{1,0:T(8,128)(2,1)S(1)} %fusion.30), channel_id=1, source_target_pairs={{0,2},{1,9},{2,4},{3,11},{4,6},{5,13},{6,0},{7,15},{8,10},{9,17},{... | collective-permute-start | bytes 884744 | tf_op jit(solution)/shard_map/ppermute | solution.py:28
  102.8 7.1 %collective-permute-start.21 = (bf16[36,4096]{1,0:T(8,128)(2,1)S(1)}, bf16[36,4096]{1,0:T(8,128)(2,1)S(1)}, u32[]{:S(2)}, u32[]{:S(2)}) collective-permute-start(bf16[36,4096]{1,0:T(8,128)(2,1)S(1)} %fusion.27), channel_id=1, source_target_pairs={{0,6},{1,25},{2,0},{3,27},{4,2},{5,29},{6,4},{7,31},{8,14},{9,1},{... | collective-permute-start | bytes 884744 | tf_op jit(solution)/shard_map/ppermute | solution.py:28
  110.1 8.1 %collective-permute-start.22 = (bf16[12,4096]{1,0:T(8,128)(2,1)S(1)}, bf16[12,4096]{1,0:T(8,128)(2,1)S(1)}, u32[]{:S(2)}, u32[]{:S(2)}) collective-permute-start(bf16[12,4096]{1,0:T(8,128)(2,1)S(1)} %get-tuple-element.91), channel_id=1, source_target_pairs={{96,0},{97,1},{98,2},{99,3},{100,4},{101,5},{102,6},{103,7},{104,8... | collective-permute-start | bytes 294920 | tf_op jit(solution)/shard_map/ppermute | solution.py:36
  111.4 6.8 %collective-permute-start.23 = (bf16[12,4096]{1,0:T(8,128)(2,1)S(1)}, bf16[12,4096]{1,0:T(8,128)(2,1)S(1)}, u32[]{:S(2)}, u32[]{:S(2)}) collective-permute-start(bf16[12,4096]{1,0:T(8,128)(2,1)S(1)} %get-tuple-element.89), channel_id=1, source_target_pairs={{96,32},{97,33},{98,34},{99,35},{100,36},{101,37},{102,38},{103,39... | collective-permute-start | bytes 294920 | tf_op jit(solution)/shard_map/ppermute | solution.py:36
  112.1 6.1 %collective-permute-start.24 = (bf16[12,4096]{1,0:T(8,128)(2,1)S(1)}, bf16[12,4096]{1,0:T(8,128)(2,1)S(1)}, u32[]{:S(2)}, u32[]{:S(2)}) collective-permute-start(bf16[12,4096]{1,0:T(8,128)(2,1)S(1)} %get-tuple-element.90), channel_id=1, source_target_pairs={{96,64},{97,65},{98,66},{99,67},{100,68},{101,69},{102,70},{103,71... | collective-permute-start | bytes 294920 | tf_op jit(solution)/shard_map/ppermute | solution.py:36
  (5 other events, 44.3 us)

commit v6 on v5

--- a/solution.py
+++ b/solution.py
@@ -158,12 +158,12 @@
     return [pltpu.VMEM(shape, down.dtype) for shape in shapes]
 
 
-def expert_kernel(parts, outputs, columns, load, *refs):
+def expert_kernel(pieces, columns, load, *refs):
     refs = list(refs)
     pick = refs.pop(0)
-    rows_in = [refs.pop(0) for _ in parts]
+    rows_in = [refs.pop(0) for _ in range(pieces)]
     halves = [[refs.pop(0) for _ in range(2 if load else 3)] for _ in range(2)]
-    outs = [refs.pop(0) for _ in range(outputs)]
+    outs = [refs.pop(0) for _ in range(pieces)]
     copies = []
     if load:
         kept = [[refs.pop(0) for _ in range(3)] for _ in range(2)]
@@ -181,11 +181,11 @@
             copies[index].wait()
 
     start = 0
-    for ref, (first, size) in zip(rows_in, parts):
-        taken = slice(first, first + size)
-        rows[start : start + size, :] = ref[taken, :width]
+    for ref in rows_in:
+        size = ref.shape[0]
+        rows[start : start + size, :] = ref[:, :width]
         share[start : start + size, :] = jnp.sum(
-            ref[taken, width:].astype(jnp.float32) * pick[...], axis=1, keepdims=True
+            ref[:, width:].astype(jnp.float32) * pick[...], axis=1, keepdims=True
         )
         start += size
 
@@ -210,19 +210,18 @@
             start += out.shape[0]
 
 
-def experts_on(parts, sizes, pick, halves):
+def experts_on(pieces, pick, halves):
     inner, width = halves[0][-1].shape
     load = len(halves[0]) == 2
+    sizes = [piece.shape[0] for piece in pieces]
     count = sum(sizes)
-    pieces = [piece for piece, _, _ in parts]
-    taken = tuple((first, size) for _, first, size in parts)
     whole = pl.BlockSpec(memory_space=pltpu.VMEM)
     space = pl.BlockSpec(memory_space=pl.ANY) if load else whole
     constraint = pltpu.HBM if load else pltpu.VMEM
     held = [pltpu.with_memory_space_constraint(w, constraint) for half in halves for w in half]
     kept = [shape for half in halves for shape in kept_shapes(*half)] if load else []
     outs = pl.pallas_call(
-        functools.partial(expert_kernel, taken, len(sizes), 1024, load),
+        functools.partial(expert_kernel, len(pieces), 1024, load),
         in_specs=[whole] * (1 + len(pieces)) + [space] * len(held),
         out_specs=[whole] * (len(sizes) + len(kept)),
         out_shape=[jax.ShapeDtypeStruct((size, width), jnp.bfloat16) for size in sizes] + kept,
@@ -238,7 +237,7 @@
             bytes_accessed=12 * width * inner if load else 4 * count * width,
             transcendentals=2 * count * inner,
         ),
-    )(pick, *pieces, *held)
+    )(pick, *(pltpu.with_memory_space_constraint(w, pltpu.VMEM) for w in pieces), *held)
     kept = outs[len(sizes) :]
     return outs[: len(sizes)], (kept[:3], kept[3:]) if load else halves
 
@@ -261,29 +260,32 @@
     blocks = [to_section(packed, s, sections - 1) for s in range(sections - 1)]
     block = jnp.concatenate(blocks, axis=0)
 
-    group = stacked([block, step_u(block, 1), step_u(block, -1), step_u(block, 2)])
-    size = group.shape[0]
+    held = block.shape[0]
+    size = SIDE * held
     cut = 16 * ((size // 2 + 15) // 16)
-    rest = size - cut
-    before, after = step_v(group, 1), step_v(group, -1)
+    lead = cut - 2 * held
+    behind, ahead, far = step_u(block, 1), step_u(block, -1), step_u(block, 2)
+    group_a, group_b = stacked([block, behind, ahead[:lead]]), stacked([ahead[lead:], far])
+    before_a, after_b = step_v(group_a, 1), step_v(group_b, -1)
+    before_b, after_a = step_v(group_b, 1), step_v(group_a, -1)
     column = lax.broadcasted_iota(jnp.int32, (1, EXTRA), 1)
     pick = ((column % experts == expert) & (column < 3 * experts)).astype(f32)
-    (own_a, own_b), halves = experts_on([(group, 0, size)], (cut, rest), pick, halves)
-
-    before, after, own_a, own_b = lax.optimization_barrier((before, after, own_a, own_b))
-    across_a, across_b = step_v(before[:cut], 1), step_v(after[cut:], -1)
-    (after_b, before_a), _ = experts_on([(after, cut, rest), (before, 0, cut)], (rest, cut), pick, halves)
+    (own_a, own_b), halves = experts_on([group_a, group_b], pick, halves)
+
+    before_a, after_b, before_b, after_a, own_a, own_b = lax.optimization_barrier(
+        (before_a, after_b, before_b, after_a, own_a, own_b)
+    )
+    across_a, across_b = step_v(before_a, 1), step_v(after_b, -1)
+    (after_b, before_a), _ = experts_on([after_b, before_a], pick, halves)
     across_a, across_b, after_b, before_a = lax.optimization_barrier((across_a, across_b, after_b, before_a))
 
     from_after_b, from_before_a = step_v(after_b, 1), step_v(before_a, -1)
-    (cross_a, cross_b), _ = experts_on(
-        [(across_a, 0, cut), (across_b, 0, rest)], (cut, rest), pick, halves
-    )
+    (cross_a, cross_b), _ = experts_on([across_a, across_b], pick, halves)
     from_cross_a, from_cross_b = step_v(cross_a, 1), step_v(cross_b, -1)
-    after, before, from_after_b, from_before_a, cross_a = lax.optimization_barrier(
-        (after, before, from_after_b, from_before_a, cross_a)
-    )
-    (after_a, before_b), _ = experts_on([(after, 0, cut), (before, cut, rest)], (cut, rest), pick, halves)
+    after_a, before_b, from_after_b, from_before_a, cross_a = lax.optimization_barrier(
+        (after_a, before_b, from_after_b, from_before_a, cross_a)
+    )
+    (after_a, before_b), _ = experts_on([after_a, before_b], pick, halves)
 
     query, _ = lax.optimization_barrier((query, cross_a))
     attention_out = lax.cond(
@@ -298,8 +300,7 @@
 
     from_before_b = step_v((before_b.astype(f32) + from_cross_b.astype(f32)).astype(jnp.bfloat16), -1)
     from_after_a = step_v((after_a.astype(f32) + from_cross_a.astype(f32)).astype(jnp.bfloat16), 1)
-    held = size // SIDE
-    near = 2 * held - (cut - held)
+    near = held - lead
     sum_b = own_b.astype(f32) + from_after_b.astype(f32) + from_before_b.astype(f32)
     far = sum_b[near:].astype(jnp.bfloat16)
     part = held // 2

time: 120 us -> 120 us (level)
  Pallas kernels: 40.2 us -> 35.9 us
  waiting for transfers between devices: 30 us -> 34.2 us
  starting transfers between devices: 37.7 us -> 40.6 us
  local copies, waits for them, and re-layouts: 5.21 us -> 3.01 us
    pallas_call x4, Pallas kernels: 39.2 us -> 34.9 us  [experts_on(): pl.pallas_call(functools.partial(expert_kernel, len(pieces), 1024, load),...]
    ppermute x10 -> x12, waiting for transfers between devices: 10.5 us -> 14.1 us  [step_v(): return lax.ppermute(block, 'dev', along(False, distance))]
    ppermute x10 -> x12, starting transfers between devices: 16.3 us -> 19.2 us  [step_v(): return lax.ppermute(block, 'dev', along(False, distance))]
    slice x2, local copies, waits for them, and re-layouts: 2.23 us -> 0.02 us  [the longest x1 0.02 us: per_device(): ahead[lead:]]
  transfers between devices with their start and end apart: 25 -> 27, of which waited for: 11 -> 11; matrix products, arithmetic and copies ran while one was open for 7% -> 5% of each run, Pallas kernels for 34% -> 30%
where the time goes in v6:
time: 120 us; the launch traced here: 118 us
  starting transfers between devices  40.6 us (34%)
  Pallas kernels  35.9 us (30%)
  waiting for transfers between devices  34.2 us (29%)
  local copies, waits for them, and re-layouts  3.01 us (3%)
  other arithmetic  2.31 us (2%)
  matrix products  1.33 us (1%)
    pallas_call x4, Pallas kernels, experts_on(): pl.pallas_call(functools.partial(expert_kernel, len(pieces), 1024, load),...  34.9 us
    ppermute x12, starting transfers between devices, step_v(): return lax.ppermute(block, 'dev', along(False, distance))  19.2 us
    ppermute x7, waiting for transfers between devices, step_u(): return lax.ppermute(block, 'dev', along(True, distance))  14.6 us
    ppermute x12, waiting for transfers between devices, step_v(): return lax.ppermute(block, 'dev', along(False, distance))  14.1 us
    ppermute x7, starting transfers between devices, step_u(): return lax.ppermute(block, 'dev', along(True, distance))  11.8 us
    ppermute x6, starting transfers between devices, to_section(): return lax.ppermute(block, 'sec', [(source, target)])  8.98 us
    ppermute x6, waiting for transfers between devices, to_section(): return lax.ppermute(block, 'sec', [(source, target)])  5.51 us
    another operation x1, local copies, waits for them, and re-layouts  2.74 us
  transfers between devices with their start and end apart: 27, of which 11 were waited for; matrix products, arithmetic and copies ran while one was open for 5% of the time, Pallas kernels for 30%

profile of v6, /device:TPU:0, one launch (start us, length us, event | category | flops | bytes accessed | tf_op | source)
XLA Modules:
  0.0 118.4 jit_solution(13619355618029656989)
XLA Ops:
  2.2 5.0 %collective-permute-start = (bf16[12,4224]{1,0:T(8,128)(2,1)S(1)}, bf16[12,4224]{1,0:T(8,128)(2,1)S(1)}, u32[]{:S(2)}, u32[]{:S(2)}) collective-permute-start(bf16[12,4224]{1,0:T(8,128)(2,1)S(1)} %shard_map.107), channel_id=1, source_target_pairs={{0,96},{1,97},{2,98},{3,99},{4,100},{5,101},{6,102},{7,103},{8,104... | collective-permute-start | bytes 304136 | tf_op jit(solution)/shard_map/ppermute | solution.py:36
  8.6 4.7 %collective-permute-done = bf16[12,4224]{1,0:T(8,128)(2,1)S(1)} collective-permute-done((bf16[12,4224]{1,0:T(8,128)(2,1)S(1)}, bf16[12,4224]{1,0:T(8,128)(2,1)S(1)}, u32[]{:S(2)}, u32[]{:S(2)}) %collective-permute-start) | collective-permute-done | bytes 101408 | tf_op jit(solution)/shard_map/ppermute | solution.py:36
  13.3 2.8 %collective-permute-start.4 = (bf16[36,4224]{1,0:T(8,128)(2,1)S(1)}, bf16[36,4224]{1,0:T(8,128)(2,1)S(1)}, u32[]{:S(2)}, u32[]{:S(2)}) collective-permute-start(bf16[36,4224]{1,0:T(8,128)(2,1)S(1)} %pad_maximum_fusion), channel_id=1, source_target_pairs={{0,6},{1,25},{2,0},{3,27},{4,2},{5,29},{6,4},{7,31},{8,14},{9,1},{... | collective-permute-start | bytes 912392 | tf_op jit(solution)/shard_map/ppermute | solution.py:28
  16.1 2.3 %collective-permute-start.6 = (bf16[36,4224]{1,0:T(8,128)(2,1)S(1)}, bf16[36,4224]{1,0:T(8,128)(2,1)S(1)}, u32[]{:S(2)}, u32[]{:S(2)}) collective-permute-start(bf16[36,4224]{1,0:T(8,128)(2,1)S(1)} %pad_maximum_fusion), channel_id=1, source_target_pairs={{0,4},{1,17},{2,6},{3,19},{4,0},{5,21},{6,2},{7,23},{8,12},{9,25},... | collective-permute-start | bytes 912392 | tf_op jit(solution)/shard_map/ppermute | solution.py:28
  18.4 2.5 %collective-permute-done.4 = bf16[36,4224]{1,0:T(8,128)(2,1)S(1)} collective-permute-done((bf16[36,4224]{1,0:T(8,128)(2,1)S(1)}, bf16[36,4224]{1,0:T(8,128)(2,1)S(1)}, u32[]{:S(2)}, u32[]{:S(2)}) %collective-permute-start.4) | collective-permute-done | bytes 304160 | tf_op jit(solution)/shard_map/ppermute | solution.py:28
  21.0 7.2 %collective-permute-done.3 = bf16[36,4224]{1,0:T(8,128)(2,1)S(1)} collective-permute-done((bf16[36,4224]{1,0:T(8,128)(2,1)S(1)}, bf16[36,4224]{1,0:T(8,128)(2,1)S(1)}, u32[]{:S(2)}, u32[]{:S(2)}) %collective-permute-start.3) | collective-permute-done | bytes 304160 | tf_op jit(solution)/shard_map/ppermute | solution.py:28
  28.3 3.8 %collective-permute-start.5 = (bf16[80,4224]{1,0:T(8,128)(2,1)S(1)}, bf16[80,4224]{1,0:T(8,128)(2,1)S(1)}, u32[]{:S(2)}, u32[]{:S(2)}) collective-permute-start(bf16[80,4224]{1,0:T(8,128)(2,1)S(1)} %pad_add_fusion.refs_1_), channel_id=1, source_target_pairs={{0,8},{1,3},{2,10},{3,5},{4,12},{5,7},{6,14},{7,1},{8,16},{9,11},{... | collective-permute-start | bytes 2027528 | tf_op jit(solution)/shard_map/ppermute | solution.py:32
  33.4 2.0 %collective-permute-start.7 = (bf16[64,4224]{1,0:T(8,128)(2,1)S(1)}, bf16[64,4224]{1,0:T(8,128)(2,1)S(1)}, u32[]{:S(2)}, u32[]{:S(2)}) collective-permute-start(bf16[64,4224]{1,0:T(8,128)(2,1)S(1)} %pad_add_fusion.1.refs_2_), channel_id=1, source_target_pairs={{0,24},{1,7},{2,26},{3,1},{4,28},{5,3},{6,30},{7,5},{8,0},{9,15},{... | collective-permute-start | bytes 1622024 | tf_op jit(solution)/shard_map/ppermute | solution.py:32
  35.5 14.6 %shard_map.108 = (bf16[80,4096]{1,0:T(8,128)(2,1)S(1)}, bf16[64,4096]{1,0:T(8,128)(2,1)S(1)}, bf16[4096,768]{1,0:T(8,128)(2,1)S(1)}, bf16[4096,768]{1,0:T(8,128)...) custom-call(f32[1,128]{1,0:T(1,128)S(1)} %and_convert_fusion.refs_0_, ...), custom_call_target="tpu_custom_call" | custom-call | flops 5435817984 | bytes 37748736 | tf_op jit(solution)/shard_map/pallas_call | solution.py:223
  50.1 2.4 %collective-permute-start.12 = (bf16[80,4224]{1,0:T(8,128)(2,1)S(1)}, bf16[80,4224]{1,0:T(8,128)(2,1)S(1)}, u32[]{:S(2)}, u32[]{:S(2)}) collective-permute-start(bf16[80,4224]{1,0:T(8,128)(2,1)S(1)} %collective-permute-done.5.refs_2_), channel_id=1, source_target_pairs={{0,8},{1,3},{2,10},{3,5},{4,12},{5,7},{6,14},{7,1},{8,16},{9,11},{... | collective-permute-start | bytes 2027528 | tf_op jit(solution)/shard_map/ppermute | solution.py:32
  53.6 6.7 %shard_map.109 = (bf16[64,4096]{1,0:T(8,128)(2,1)S(1)}, bf16[80,4096]{1,0:T(8,128)(2,1)S(1)}) custom-call(f32[1,128]{1,0:T(1,128)S(1)} %and_convert_fusion.refs_0_, bf16[64,4224]{1,0:T(8,128)(2,1)S(1)} %collective-permute-done.7.refs_1_, bf16[80,4224]{1,0:T(8,128)(2,1)S(1)} %collective-permute-done.5.refs_2_, ...), custom_call_target="tpu_custom_call" | custom-call | flops 5435817984 | bytes 2359296 | tf_op jit(solution)/shard_map/pallas_call | solution.py:223
  60.4 1.6 %collective-permute-done.13.refs_2_ = bf16[64,4224]{1,0:T(8,128)(2,1)S(1)} collective-permute-done((bf16[64,4224]{1,0:T(8,128)(2,1)S(1)}, bf16[64,4224]{1,0:T(8,128)(2,1)S(1)}, u32[]{:S(2)}, u32[]{:S(2)}) %collective-permute-start.13) | collective-permute-done | bytes 540704 | tf_op jit(solution)/shard_map/ppermute | solution.py:32
  62.2 2.0 %collective-permute-start.15 = (bf16[80,4096]{1,0:T(8,128)(2,1)S(1)}, bf16[80,4096]{1,0:T(8,128)(2,1)S(1)}, u32[]{:S(2)}, u32[]{:S(2)}) collective-permute-start(bf16[80,4096]{1,0:T(8,128)(2,1)S(1)} %get-tuple-element.61), channel_id=1, source_target_pairs={{0,24},{1,7},{2,26},{3,1},{4,28},{5,3},{6,30},{7,5},{8,0},{9,15},{... | collective-permute-start | bytes 1966088 | tf_op jit(solution)/shard_map/ppermute | solution.py:32
  64.3 6.8 %shard_map.110 = (bf16[80,4096]{1,0:T(8,128)(2,1)S(1)}, bf16[64,4096]{1,0:T(8,128)(2,1)S(1)}) custom-call(f32[1,128]{1,0:T(1,128)S(1)} %and_convert_fusion.refs_0_, bf16[80,4224]{1,0:T(8,128)(2,1)S(1)} %collective-permute-done.12.refs_1_, bf16[64,4224]{1,0:T(8,128)(2,1)S(1)} %collective-permute-done.13.refs_2_, ...), custom_call_target="tpu_custom_call" | custom-call | flops 5435817984 | bytes 2359296 | tf_op jit(solution)/shard_map/pallas_call | solution.py:223
  71.1 3.2 %collective-permute-start.18 = (bf16[64,4096]{1,0:T(8,128)(2,1)S(1)}, bf16[64,4096]{1,0:T(8,128)(2,1)S(1)}, u32[]{:S(2)}, u32[]{:S(2)}) collective-permute-start(bf16[64,4096]{1,0:T(8,128)(2,1)S(1)} %get-tuple-element.72), channel_id=1, source_target_pairs={{0,24},{1,7},{2,26},{3,1},{4,28},{5,3},{6,30},{7,5},{8,0},{9,15},{... | collective-permute-start | bytes 1572872 | tf_op jit(solution)/shard_map/ppermute | solution.py:32
  74.6 6.8 %shard_map.111 = (bf16[80,4096]{1,0:T(8,128)(2,1)S(1)}, bf16[64,4096]{1,0:T(8,128)(2,1)S(1)}) custom-call(f32[1,128]{1,0:T(1,128)S(1)} %and_convert_fusion.refs_0_, bf16[80,4224]{1,0:T(8,128)(2,1)S(1)} %collective-permute-done.9.refs_1_, bf16[64,4224]{1,0:T(8,128)(2,1)S(1)} %collective-permute-done.8.refs_2_, ...), custom_call_target="tpu_custom_call" | custom-call | flops 5435817984 | bytes 2359296 | tf_op jit(solution)/shard_map/pallas_call | solution.py:223
  81.5 3.3 %collective-permute-start.19 = (bf16[64,4096]{1,0:T(8,128)(2,1)S(1)}, bf16[64,4096]{1,0:T(8,128)(2,1)S(1)}, u32[]{:S(2)}, u32[]{:S(2)}) collective-permute-start(bf16[64,4096]{1,0:T(8,128)(2,1)S(1)} %add_convert_fusion.1), channel_id=1, source_target_pairs={{0,24},{1,7},{2,26},{3,1},{4,28},{5,3},{6,30},{7,5},{8,0},{9,15},{... | collective-permute-start | bytes 1572872 | tf_op jit(solution)/shard_map/ppermute | solution.py:32
  86.3 7.4 %collective-permute-done.19 = bf16[64,4096]{1,0:T(8,128)(2,1)S(1)} collective-permute-done((bf16[64,4096]{1,0:T(8,128)(2,1)S(1)}, bf16[64,4096]{1,0:T(8,128)(2,1)S(1)}, u32[]{:S(2)}, u32[]{:S(2)}) %collective-permute-start.19) | collective-permute-done | bytes 524320 | tf_op jit(solution)/shard_map/ppermute | solution.py:32
  94.1 3.3 %collective-permute-start.22 = (bf16[18,4096]{1,0:T(8,128)(2,1)S(1)}, bf16[18,4096]{1,0:T(8,128)(2,1)S(1)}, u32[]{:S(2)}, u32[]{:S(2)}) collective-permute-start(bf16[18,4096]{1,0:T(8,128)(2,1)S(1)} %get-tuple-element.92), channel_id=1, source_target_pairs={{0,6},{1,25},{2,0},{3,27},{4,2},{5,29},{6,4},{7,31},{8,14},{9,1},{... | collective-permute-start | bytes 442376 | tf_op jit(solution)/shard_map/ppermute | solution.py:28
  97.4 3.3 %collective-permute-done.17 = bf16[80,4096]{1,0:T(8,128)(2,1)S(1)} collective-permute-done((bf16[80,4096]{1,0:T(8,128)(2,1)S(1)}, bf16[80,4096]{1,0:T(8,128)(2,1)S(1)}, u32[]{:S(2)}, u32[]{:S(2)}) %collective-permute-start.17) | collective-permute-done | bytes 655392 | tf_op jit(solution)/shard_map/ppermute | solution.py:32
  101.3 3.3 %collective-permute-start.23 = (bf16[36,4096]{1,0:T(8,128)(2,1)S(1)}, bf16[36,4096]{1,0:T(8,128)(2,1)S(1)}, u32[]{:S(2)}, u32[]{:S(2)}) collective-permute-start(bf16[36,4096]{1,0:T(8,128)(2,1)S(1)} %fusion.27), channel_id=1, source_target_pairs={{0,6},{1,25},{2,0},{3,27},{4,2},{5,29},{6,4},{7,31},{8,14},{9,1},{... | collective-permute-start | bytes 884744 | tf_op jit(solution)/shard_map/ppermute | solution.py:28
  104.6 4.9 %collective-permute-done.21 = bf16[36,4096]{1,0:T(8,128)(2,1)S(1)} collective-permute-done((bf16[36,4096]{1,0:T(8,128)(2,1)S(1)}, bf16[36,4096]{1,0:T(8,128)(2,1)S(1)}, u32[]{:S(2)}, u32[]{:S(2)}) %collective-permute-start.21) | collective-permute-done | bytes 294944 | tf_op jit(solution)/shard_map/ppermute | solution.py:28
  112.3 4.5 %conditional.1 = (bf16[2,8192]{1,0:T(2,128)(2,1)S(1)}) conditional(s32[]{:T(128)} %convert_element_type.89, (s32[2]{0:T(128)S(1)}, bf16[2,8192]{1,0:T(2,128)(2,1)S(1)}, bf16[2,1024,4,256]{3,2,1,0:T(4,128)(2,1)}, bf16[2,4,256]{2,1,0:T(4,128)(2,1)S(1)}) %tuple.36, () %tuple.19), branch_computations={%region_0.3_spmd, %region_3.4_spmd} | conditional | flops 68128512 | bytes 14426640 | solution.py:291
  112.3 2.7 %copy.14 = bf16[2,1024,4,256]{3,1,2,0:T(8,128)(2,1)S(1)} copy(bf16[2,1024,4,256]{3,2,1,0:T(4,128)(2,1)} %get-tuple-element.81) | data formatting | bytes 8388608 | tf_op jit(solution)/shard_map
  (74 shorter events, 14.7 us)
Async XLA Ops:
  0.6 34.9 %collective-permute-start.10 = (bf16[4096,1536]{1,0:T(8,128)(2,1)}, bf16[4096,1536]{1,0:T(8,128)(2,1)}, u32[]{:S(2)}, u32[]{:S(2)}) collective-permute-start(bf16[4096,1536]{1,0:T(8,128)(2,1)} %bitcast.18), channel_id=1, source_target_pairs={{0,1},{1,0},{2,3},{3,2},{4,5},{5,4},{6,7},{7,6},{8,9},{9,8},{10,11... | collective-permute-start | bytes 37748744 | tf_op jit(solution)/shard_map/ppermute | solution.py:51
  0.7 34.7 %collective-permute-start.11 = (bf16[768,4096]{1,0:T(8,128)(2,1)}, bf16[768,4096]{1,0:T(8,128)(2,1)}, u32[]{:S(2)}, u32[]{:S(2)}) collective-permute-start(bf16[768,4096]{1,0:T(8,128)(2,1)} %bitcast.20), channel_id=1, source_target_pairs={{0,1},{1,0},{2,3},{3,2},{4,5},{5,4},{6,7},{7,6},{8,9},{9,8},{10,11... | collective-permute-start | bytes 18874376 | tf_op jit(solution)/shard_map/ppermute | solution.py:51
  2.2 11.0 %collective-permute-start = (bf16[12,4224]{1,0:T(8,128)(2,1)S(1)}, bf16[12,4224]{1,0:T(8,128)(2,1)S(1)}, u32[]{:S(2)}, u32[]{:S(2)}) collective-permute-start(bf16[12,4224]{1,0:T(8,128)(2,1)S(1)} %shard_map.107), channel_id=1, source_target_pairs={{0,96},{1,97},{2,98},{3,99},{4,100},{5,101},{6,102},{7,103},{8,104... | collective-permute-start | bytes 304136 | tf_op jit(solution)/shard_map/ppermute | solution.py:36
  13.3 7.7 %collective-permute-start.4 = (bf16[36,4224]{1,0:T(8,128)(2,1)S(1)}, bf16[36,4224]{1,0:T(8,128)(2,1)S(1)}, u32[]{:S(2)}, u32[]{:S(2)}) collective-permute-start(bf16[36,4224]{1,0:T(8,128)(2,1)S(1)} %pad_maximum_fusion), channel_id=1, source_target_pairs={{0,6},{1,25},{2,0},{3,27},{4,2},{5,29},{6,4},{7,31},{8,14},{9,1},{... | collective-permute-start | bytes 912392 | tf_op jit(solution)/shard_map/ppermute | solution.py:28
  16.1 12.0 %collective-permute-start.3 = (bf16[36,4224]{1,0:T(8,128)(2,1)S(1)}, bf16[36,4224]{1,0:T(8,128)(2,1)S(1)}, u32[]{:S(2)}, u32[]{:S(2)}) collective-permute-start(bf16[36,4224]{1,0:T(8,128)(2,1)S(1)} %pad_maximum_fusion), channel_id=1, source_target_pairs={{0,2},{1,9},{2,4},{3,11},{4,6},{5,13},{6,0},{7,15},{8,10},{9,17},{... | collective-permute-start | bytes 912392 | tf_op jit(solution)/shard_map/ppermute | solution.py:28
  16.1 17.1 %collective-permute-start.6 = (bf16[36,4224]{1,0:T(8,128)(2,1)S(1)}, bf16[36,4224]{1,0:T(8,128)(2,1)S(1)}, u32[]{:S(2)}, u32[]{:S(2)}) collective-permute-start(bf16[36,4224]{1,0:T(8,128)(2,1)S(1)} %pad_maximum_fusion), channel_id=1, source_target_pairs={{0,4},{1,17},{2,6},{3,19},{4,0},{5,21},{6,2},{7,23},{8,12},{9,25},... | collective-permute-start | bytes 912392 | tf_op jit(solution)/shard_map/ppermute | solution.py:28
  28.3 21.8 %collective-permute-start.5 = (bf16[80,4224]{1,0:T(8,128)(2,1)S(1)}, bf16[80,4224]{1,0:T(8,128)(2,1)S(1)}, u32[]{:S(2)}, u32[]{:S(2)}) collective-permute-start(bf16[80,4224]{1,0:T(8,128)(2,1)S(1)} %pad_add_fusion.refs_1_), channel_id=1, source_target_pairs={{0,8},{1,3},{2,10},{3,5},{4,12},{5,7},{6,14},{7,1},{8,16},{9,11},{... | collective-permute-start | bytes 2027528 | tf_op jit(solution)/shard_map/ppermute | solution.py:32
  32.1 18.1 %collective-permute-start.9 = (bf16[80,4224]{1,0:T(8,128)(2,1)S(1)}, bf16[80,4224]{1,0:T(8,128)(2,1)S(1)}, u32[]{:S(2)}, u32[]{:S(2)}) collective-permute-start(bf16[80,4224]{1,0:T(8,128)(2,1)S(1)} %pad_add_fusion.refs_1_), channel_id=1, source_target_pairs={{0,24},{1,7},{2,26},{3,1},{4,28},{5,3},{6,30},{7,5},{8,0},{9,15},{... | collective-permute-start | bytes 2027528 | tf_op jit(solution)/shard_map/ppermute | solution.py:32
  33.4 16.7 %collective-permute-start.7 = (bf16[64,4224]{1,0:T(8,128)(2,1)S(1)}, bf16[64,4224]{1,0:T(8,128)(2,1)S(1)}, u32[]{:S(2)}, u32[]{:S(2)}) collective-permute-start(bf16[64,4224]{1,0:T(8,128)(2,1)S(1)} %pad_add_fusion.1.refs_2_), channel_id=1, source_target_pairs={{0,24},{1,7},{2,26},{3,1},{4,28},{5,3},{6,30},{7,5},{8,0},{9,15},{... | collective-permute-start | bytes 1622024 | tf_op jit(solution)/shard_map/ppermute | solution.py:32
  35.4 14.7 %collective-permute-start.8 = (bf16[64,4224]{1,0:T(8,128)(2,1)S(1)}, bf16[64,4224]{1,0:T(8,128)(2,1)S(1)}, u32[]{:S(2)}, u32[]{:S(2)}) collective-permute-start(bf16[64,4224]{1,0:T(8,128)(2,1)S(1)} %pad_add_fusion.1.refs_2_), channel_id=1, source_target_pairs={{0,8},{1,3},{2,10},{3,5},{4,12},{5,7},{6,14},{7,1},{8,16},{9,11},{... | collective-permute-start | bytes 1622024 | tf_op jit(solution)/shard_map/ppermute | solution.py:32
  50.1 12.1 %collective-permute-start.12 = (bf16[80,4224]{1,0:T(8,128)(2,1)S(1)}, bf16[80,4224]{1,0:T(8,128)(2,1)S(1)}, u32[]{:S(2)}, u32[]{:S(2)}) collective-permute-start(bf16[80,4224]{1,0:T(8,128)(2,1)S(1)} %collective-permute-done.5.refs_2_), channel_id=1, source_target_pairs={{0,8},{1,3},{2,10},{3,5},{4,12},{5,7},{6,14},{7,1},{8,16},{9,11},{... | collective-permute-start | bytes 2027528 | tf_op jit(solution)/shard_map/ppermute | solution.py:32
  52.6 9.4 %collective-permute-start.13 = (bf16[64,4224]{1,0:T(8,128)(2,1)S(1)}, bf16[64,4224]{1,0:T(8,128)(2,1)S(1)}, u32[]{:S(2)}, u32[]{:S(2)}) collective-permute-start(bf16[64,4224]{1,0:T(8,128)(2,1)S(1)} %collective-permute-done.7.refs_1_), channel_id=1, source_target_pairs={{0,24},{1,7},{2,26},{3,1},{4,28},{5,3},{6,30},{7,5},{8,0},{9,15},{... | collective-permute-start | bytes 1622024 | tf_op jit(solution)/shard_map/ppermute | solution.py:32
  62.2 12.4 %collective-permute-start.15 = (bf16[80,4096]{1,0:T(8,128)(2,1)S(1)}, bf16[80,4096]{1,0:T(8,128)(2,1)S(1)}, u32[]{:S(2)}, u32[]{:S(2)}) collective-permute-start(bf16[80,4096]{1,0:T(8,128)(2,1)S(1)} %get-tuple-element.61), channel_id=1, source_target_pairs={{0,24},{1,7},{2,26},{3,1},{4,28},{5,3},{6,30},{7,5},{8,0},{9,15},{... | collective-permute-start | bytes 1966088 | tf_op jit(solution)/shard_map/ppermute | solution.py:32
  64.2 10.4 %collective-permute-start.14 = (bf16[64,4096]{1,0:T(8,128)(2,1)S(1)}, bf16[64,4096]{1,0:T(8,128)(2,1)S(1)}, u32[]{:S(2)}, u32[]{:S(2)}) collective-permute-start(bf16[64,4096]{1,0:T(8,128)(2,1)S(1)} %get-tuple-element.60), channel_id=1, source_target_pairs={{0,8},{1,3},{2,10},{3,5},{4,12},{5,7},{6,14},{7,1},{8,16},{9,11},{... | collective-permute-start | bytes 1572872 | tf_op jit(solution)/shard_map/ppermute | solution.py:32
  71.1 10.3 %collective-permute-start.18 = (bf16[64,4096]{1,0:T(8,128)(2,1)S(1)}, bf16[64,4096]{1,0:T(8,128)(2,1)S(1)}, u32[]{:S(2)}, u32[]{:S(2)}) collective-permute-start(bf16[64,4096]{1,0:T(8,128)(2,1)S(1)} %get-tuple-element.72), channel_id=1, source_target_pairs={{0,24},{1,7},{2,26},{3,1},{4,28},{5,3},{6,30},{7,5},{8,0},{9,15},{... | collective-permute-start | bytes 1572872 | tf_op jit(solution)/shard_map/ppermute | solution.py:32
  74.3 11.8 %collective-permute-start.16 = (bf16[80,4096]{1,0:T(8,128)(2,1)S(1)}, bf16[80,4096]{1,0:T(8,128)(2,1)S(1)}, u32[]{:S(2)}, u32[]{:S(2)}) collective-permute-start(bf16[80,4096]{1,0:T(8,128)(2,1)S(1)} %get-tuple-element.64), channel_id=1, source_target_pairs={{0,8},{1,3},{2,10},{3,5},{4,12},{5,7},{6,14},{7,1},{8,16},{9,11},{... | collective-permute-start | bytes 1966088 | tf_op jit(solution)/shard_map/ppermute | solution.py:32
  81.5 12.2 %collective-permute-start.19 = (bf16[64,4096]{1,0:T(8,128)(2,1)S(1)}, bf16[64,4096]{1,0:T(8,128)(2,1)S(1)}, u32[]{:S(2)}, u32[]{:S(2)}) collective-permute-start(bf16[64,4096]{1,0:T(8,128)(2,1)S(1)} %add_convert_fusion.1), channel_id=1, source_target_pairs={{0,24},{1,7},{2,26},{3,1},{4,28},{5,3},{6,30},{7,5},{8,0},{9,15},{... | collective-permute-start | bytes 1572872 | tf_op jit(solution)/shard_map/ppermute | solution.py:32
  86.2 14.5 %collective-permute-start.17 = (bf16[80,4096]{1,0:T(8,128)(2,1)S(1)}, bf16[80,4096]{1,0:T(8,128)(2,1)S(1)}, u32[]{:S(2)}, u32[]{:S(2)}) collective-permute-start(bf16[80,4096]{1,0:T(8,128)(2,1)S(1)} %add_convert_fusion), channel_id=1, source_target_pairs={{0,8},{1,3},{2,10},{3,5},{4,12},{5,7},{6,14},{7,1},{8,16},{9,11},{... | collective-permute-start | bytes 1966088 | tf_op jit(solution)/shard_map/ppermute | solution.py:32
  94.0 7.0 %collective-permute-start.20 = (bf16[18,4096]{1,0:T(8,128)(2,1)S(1)}, bf16[18,4096]{1,0:T(8,128)(2,1)S(1)}, u32[]{:S(2)}, u32[]{:S(2)}) collective-permute-start(bf16[18,4096]{1,0:T(8,128)(2,1)S(1)} %get-tuple-element.91), channel_id=1, source_target_pairs={{0,2},{1,9},{2,4},{3,11},{4,6},{5,13},{6,0},{7,15},{8,10},{9,17},{... | collective-permute-start | bytes 442376 | tf_op jit(solution)/shard_map/ppermute | solution.py:28
  94.1 7.1 %collective-permute-start.22 = (bf16[18,4096]{1,0:T(8,128)(2,1)S(1)}, bf16[18,4096]{1,0:T(8,128)(2,1)S(1)}, u32[]{:S(2)}, u32[]{:S(2)}) collective-permute-start(bf16[18,4096]{1,0:T(8,128)(2,1)S(1)} %get-tuple-element.92), channel_id=1, source_target_pairs={{0,6},{1,25},{2,0},{3,27},{4,2},{5,29},{6,4},{7,31},{8,14},{9,1},{... | collective-permute-start | bytes 442376 | tf_op jit(solution)/shard_map/ppermute | solution.py:28
  101.1 8.4 %collective-permute-start.21 = (bf16[36,4096]{1,0:T(8,128)(2,1)S(1)}, bf16[36,4096]{1,0:T(8,128)(2,1)S(1)}, u32[]{:S(2)}, u32[]{:S(2)}) collective-permute-start(bf16[36,4096]{1,0:T(8,128)(2,1)S(1)} %fusion.30), channel_id=1, source_target_pairs={{0,2},{1,9},{2,4},{3,11},{4,6},{5,13},{6,0},{7,15},{8,10},{9,17},{... | collective-permute-start | bytes 884744 | tf_op jit(solution)/shard_map/ppermute | solution.py:28
  101.3 8.1 %collective-permute-start.23 = (bf16[36,4096]{1,0:T(8,128)(2,1)S(1)}, bf16[36,4096]{1,0:T(8,128)(2,1)S(1)}, u32[]{:S(2)}, u32[]{:S(2)}) collective-permute-start(bf16[36,4096]{1,0:T(8,128)(2,1)S(1)} %fusion.27), channel_id=1, source_target_pairs={{0,6},{1,25},{2,0},{3,27},{4,2},{5,29},{6,4},{7,31},{8,14},{9,1},{... | collective-permute-start | bytes 884744 | tf_op jit(solution)/shard_map/ppermute | solution.py:28
  109.6 8.1 %collective-permute-start.24 = (bf16[12,4096]{1,0:T(8,128)(2,1)S(1)}, bf16[12,4096]{1,0:T(8,128)(2,1)S(1)}, u32[]{:S(2)}, u32[]{:S(2)}) collective-permute-start(bf16[12,4096]{1,0:T(8,128)(2,1)S(1)} %get-tuple-element.95), channel_id=1, source_target_pairs={{96,0},{97,1},{98,2},{99,3},{100,4},{101,5},{102,6},{103,7},{104,8... | collective-permute-start | bytes 294920 | tf_op jit(solution)/shard_map/ppermute | solution.py:36
  110.9 6.8 %collective-permute-start.25 = (bf16[12,4096]{1,0:T(8,128)(2,1)S(1)}, bf16[12,4096]{1,0:T(8,128)(2,1)S(1)}, u32[]{:S(2)}, u32[]{:S(2)}) collective-permute-start(bf16[12,4096]{1,0:T(8,128)(2,1)S(1)} %get-tuple-element.93), channel_id=1, source_target_pairs={{96,32},{97,33},{98,34},{99,35},{100,36},{101,37},{102,38},{103,39... | collective-permute-start | bytes 294920 | tf_op jit(solution)/shard_map/ppermute | solution.py:36
  (7 other events, 52.7 us)

commit v7 on v6

--- a/solution.py
+++ b/solution.py
@@ -264,8 +264,10 @@
     size = SIDE * held
     cut = 16 * ((size // 2 + 15) // 16)
     lead = cut - 2 * held
-    behind, ahead, far = step_u(block, 1), step_u(block, -1), step_u(block, 2)
-    group_a, group_b = stacked([block, behind, ahead[:lead]]), stacked([ahead[lead:], far])
+    part = held // 2
+    behind, ahead = step_u(block, 1), step_u(block, -1)
+    far_a, far_b = step_u(behind[:part], 1), step_u(ahead[part:], -1)
+    group_a, group_b = stacked([block, behind, ahead[:lead]]), stacked([ahead[lead:], far_a, far_b])
     before_a, after_b = step_v(group_a, 1), step_v(group_b, -1)
     before_b, after_a = step_v(group_b, 1), step_v(group_a, -1)
     column = lax.broadcasted_iota(jnp.int32, (1, EXTRA), 1)
@@ -303,7 +305,6 @@
     near = held - lead
     sum_b = own_b.astype(f32) + from_after_b.astype(f32) + from_before_b.astype(f32)
     far = sum_b[near:].astype(jnp.bfloat16)
-    part = held // 2
     from_far_a, from_far_b = step_u(far[:part], 1), step_u(far[part:], -1)
     sum_a = own_a.astype(f32) + from_after_a.astype(f32) + from_before_a.astype(f32)
     ahead = jnp.concatenate([sum_a[2 * held :], sum_b[:near]], axis=0)

time: 120 us -> 124 us (1.033)
  starting transfers between devices: 40.6 us -> 45.4 us
    ppermute x12, starting transfers between devices: 19.2 us -> 22.5 us  [step_v(): return lax.ppermute(block, 'dev', along(False, distance))]
    ppermute x7 -> x8, waiting for transfers between devices: 14.6 us -> 12.5 us  [step_u(): return lax.ppermute(block, 'dev', along(True, distance))]
    ppermute x7 -> x8, starting transfers between devices: 11.8 us -> 13.4 us  [step_u(): return lax.ppermute(block, 'dev', along(True, distance))]
    ppermute x12, waiting for transfers between devices: 14.1 us -> 15.4 us  [step_v(): return lax.ppermute(block, 'dev', along(False, distance))]
  transfers between devices with their start and end apart: 27 -> 28, of which waited for: 11 -> 12; matrix products, arithmetic and copies ran while one was open for 5% -> 5% of each run, Pallas kernels for 30% -> 29%
where the time goes in v7:
time: 124 us; the launch traced here: 122 us
  starting transfers between devices  45.4 us (37%)
  Pallas kernels  35.8 us (29%)
  waiting for transfers between devices  33.4 us (27%)
  local copies, waits for them, and re-layouts  3.08 us (2%)
  other arithmetic  2.35 us (2%)
  matrix products  1.33 us (1%)
    pallas_call x4, Pallas kernels, experts_on(): pl.pallas_call(functools.partial(expert_kernel, len(pieces), 1024, load),...  34.8 us
    ppermute x12, starting transfers between devices, step_v(): return lax.ppermute(block, 'dev', along(False, distance))  22.5 us
    ppermute x12, waiting for transfers between devices, step_v(): return lax.ppermute(block, 'dev', along(False, distance))  15.4 us
    ppermute x8, starting transfers between devices, step_u(): return lax.ppermute(block, 'dev', along(True, distance))  13.4 us
    ppermute x8, waiting for transfers between devices, step_u(): return lax.ppermute(block, 'dev', along(True, distance))  12.5 us
    ppermute x6, starting transfers between devices, to_section(): return lax.ppermute(block, 'sec', [(source, target)])  8.98 us
    ppermute x6, waiting for transfers between devices, to_section(): return lax.ppermute(block, 'sec', [(source, target)])  5.51 us
    another operation x1, local copies, waits for them, and re-layouts  2.74 us
  transfers between devices with their start and end apart: 28, of which 12 were waited for; matrix products, arithmetic and copies ran while one was open for 5% of the time, Pallas kernels for 29%

profile of v7, /device:TPU:0, one launch (start us, length us, event | category | flops | bytes accessed | tf_op | source)
XLA Modules:
  0.0 122.4 jit_solution(10379564647845843922)
XLA Ops:
  2.2 5.0 %collective-permute-start = (bf16[12,4224]{1,0:T(8,128)(2,1)S(1)}, bf16[12,4224]{1,0:T(8,128)(2,1)S(1)}, u32[]{:S(2)}, u32[]{:S(2)}) collective-permute-start(bf16[12,4224]{1,0:T(8,128)(2,1)S(1)} %shard_map.107), channel_id=1, source_target_pairs={{0,96},{1,97},{2,98},{3,99},{4,100},{5,101},{6,102},{7,103},{8,104... | collective-permute-start | bytes 304136 | tf_op jit(solution)/shard_map/ppermute | solution.py:36
  8.6 4.7 %collective-permute-done = bf16[12,4224]{1,0:T(8,128)(2,1)S(1)} collective-permute-done((bf16[12,4224]{1,0:T(8,128)(2,1)S(1)}, bf16[12,4224]{1,0:T(8,128)(2,1)S(1)}, u32[]{:S(2)}, u32[]{:S(2)}) %collective-permute-start) | collective-permute-done | bytes 101408 | tf_op jit(solution)/shard_map/ppermute | solution.py:36
  13.3 2.8 %collective-permute-start.4 = (bf16[36,4224]{1,0:T(8,128)(2,1)S(1)}, bf16[36,4224]{1,0:T(8,128)(2,1)S(1)}, u32[]{:S(2)}, u32[]{:S(2)}) collective-permute-start(bf16[36,4224]{1,0:T(8,128)(2,1)S(1)} %pad_maximum_fusion), channel_id=1, source_target_pairs={{0,6},{1,25},{2,0},{3,27},{4,2},{5,29},{6,4},{7,31},{8,14},{9,1},{... | collective-permute-start | bytes 912392 | tf_op jit(solution)/shard_map/ppermute | solution.py:28
  16.1 4.7 %collective-permute-done.4 = bf16[36,4224]{1,0:T(8,128)(2,1)S(1)} collective-permute-done((bf16[36,4224]{1,0:T(8,128)(2,1)S(1)}, bf16[36,4224]{1,0:T(8,128)(2,1)S(1)}, u32[]{:S(2)}, u32[]{:S(2)}) %collective-permute-start.4) | collective-permute-done | bytes 304160 | tf_op jit(solution)/shard_map/ppermute | solution.py:28
  20.9 3.8 %collective-permute-start.7 = (bf16[18,4224]{1,0:T(8,128)(2,1)S(1)}, bf16[18,4224]{1,0:T(8,128)(2,1)S(1)}, u32[]{:S(2)}, u32[]{:S(2)}) collective-permute-start(bf16[18,4224]{1,0:T(8,128)(2,1)S(1)} %slice.73), channel_id=1, source_target_pairs={{0,6},{1,25},{2,0},{3,27},{4,2},{5,29},{6,4},{7,31},{8,14},{9,1},{... | collective-permute-start | bytes 456200 | tf_op jit(solution)/shard_map/ppermute | solution.py:28
  24.9 4.1 %collective-permute-start.10 = (bf16[80,4224]{1,0:T(8,128)(2,1)S(1)}, bf16[80,4224]{1,0:T(8,128)(2,1)S(1)}, u32[]{:S(2)}, u32[]{:S(2)}) collective-permute-start(bf16[80,4224]{1,0:T(8,128)(2,1)S(1)} %pad_add_fusion.refs_1_), channel_id=1, source_target_pairs={{0,24},{1,7},{2,26},{3,1},{4,28},{5,3},{6,30},{7,5},{8,0},{9,15},{... | collective-permute-start | bytes 2027528 | tf_op jit(solution)/shard_map/ppermute | solution.py:32
  30.2 1.9 %collective-permute-start.5 = (bf16[80,4224]{1,0:T(8,128)(2,1)S(1)}, bf16[80,4224]{1,0:T(8,128)(2,1)S(1)}, u32[]{:S(2)}, u32[]{:S(2)}) collective-permute-start(bf16[80,4224]{1,0:T(8,128)(2,1)S(1)} %pad_add_fusion.refs_1_), channel_id=1, source_target_pairs={{0,8},{1,3},{2,10},{3,5},{4,12},{5,7},{6,14},{7,1},{8,16},{9,11},{... | collective-permute-start | bytes 2027528 | tf_op jit(solution)/shard_map/ppermute | solution.py:32
  32.1 1.9 %collective-permute-done.6 = bf16[18,4224]{1,0:T(8,128)(2,1)S(1)} collective-permute-done((bf16[18,4224]{1,0:T(8,128)(2,1)S(1)}, bf16[18,4224]{1,0:T(8,128)(2,1)S(1)}, u32[]{:S(2)}, u32[]{:S(2)}) %collective-permute-start.6) | collective-permute-done | bytes 152096 | tf_op jit(solution)/shard_map/ppermute | solution.py:28
  34.1 4.1 %collective-permute-start.8 = (bf16[64,4224]{1,0:T(8,128)(2,1)S(1)}, bf16[64,4224]{1,0:T(8,128)(2,1)S(1)}, u32[]{:S(2)}, u32[]{:S(2)}) collective-permute-start(bf16[64,4224]{1,0:T(8,128)(2,1)S(1)} %pad_add_fusion.1.refs_2_), channel_id=1, source_target_pairs={{0,24},{1,7},{2,26},{3,1},{4,28},{5,3},{6,30},{7,5},{8,0},{9,15},{... | collective-permute-start | bytes 1622024 | tf_op jit(solution)/shard_map/ppermute | solution.py:32
  38.2 14.6 %shard_map.108 = (bf16[80,4096]{1,0:T(8,128)(2,1)S(1)}, bf16[64,4096]{1,0:T(8,128)(2,1)S(1)}, bf16[4096,768]{1,0:T(8,128)(2,1)S(1)}, bf16[4096,768]{1,0:T(8,128)...) custom-call(f32[1,128]{1,0:T(1,128)S(1)} %and_convert_fusion.refs_0_, ...), custom_call_target="tpu_custom_call" | custom-call | flops 5435817984 | bytes 37748736 | tf_op jit(solution)/shard_map/pallas_call | solution.py:223
  52.9 3.5 %collective-permute-start.14 = (bf16[64,4224]{1,0:T(8,128)(2,1)S(1)}, bf16[64,4224]{1,0:T(8,128)(2,1)S(1)}, u32[]{:S(2)}, u32[]{:S(2)}) collective-permute-start(bf16[64,4224]{1,0:T(8,128)(2,1)S(1)} %collective-permute-done.8.refs_1_), channel_id=1, source_target_pairs={{0,24},{1,7},{2,26},{3,1},{4,28},{5,3},{6,30},{7,5},{8,0},{9,15},{... | collective-permute-start | bytes 1622024 | tf_op jit(solution)/shard_map/ppermute | solution.py:32
  56.4 6.7 %shard_map.109 = (bf16[64,4096]{1,0:T(8,128)(2,1)S(1)}, bf16[80,4096]{1,0:T(8,128)(2,1)S(1)}) custom-call(f32[1,128]{1,0:T(1,128)S(1)} %and_convert_fusion.refs_0_, bf16[64,4224]{1,0:T(8,128)(2,1)S(1)} %collective-permute-done.8.refs_1_, bf16[80,4224]{1,0:T(8,128)(2,1)S(1)} %collective-permute-done.5.refs_2_, ...), custom_call_target="tpu_custom_call" | custom-call | flops 5435817984 | bytes 2359296 | tf_op jit(solution)/shard_map/pallas_call | solution.py:223
  64.9 2.0 %collective-permute-start.16 = (bf16[80,4096]{1,0:T(8,128)(2,1)S(1)}, bf16[80,4096]{1,0:T(8,128)(2,1)S(1)}, u32[]{:S(2)}, u32[]{:S(2)}) collective-permute-start(bf16[80,4096]{1,0:T(8,128)(2,1)S(1)} %get-tuple-element.61), channel_id=1, source_target_pairs={{0,24},{1,7},{2,26},{3,1},{4,28},{5,3},{6,30},{7,5},{8,0},{9,15},{... | collective-permute-start | bytes 1966088 | tf_op jit(solution)/shard_map/ppermute | solution.py:32
  67.0 6.8 %shard_map.110 = (bf16[80,4096]{1,0:T(8,128)(2,1)S(1)}, bf16[64,4096]{1,0:T(8,128)(2,1)S(1)}) custom-call(f32[1,128]{1,0:T(1,128)S(1)} %and_convert_fusion.refs_0_, bf16[80,4224]{1,0:T(8,128)(2,1)S(1)} %collective-permute-done.13.refs_1_, bf16[64,4224]{1,0:T(8,128)(2,1)S(1)} %collective-permute-done.14.refs_2_, ...), custom_call_target="tpu_custom_call" | custom-call | flops 5435817984 | bytes 2359296 | tf_op jit(solution)/shard_map/pallas_call | solution.py:223
  73.8 3.3 %collective-permute-start.19 = (bf16[64,4096]{1,0:T(8,128)(2,1)S(1)}, bf16[64,4096]{1,0:T(8,128)(2,1)S(1)}, u32[]{:S(2)}, u32[]{:S(2)}) collective-permute-start(bf16[64,4096]{1,0:T(8,128)(2,1)S(1)} %get-tuple-element.72), channel_id=1, source_target_pairs={{0,24},{1,7},{2,26},{3,1},{4,28},{5,3},{6,30},{7,5},{8,0},{9,15},{... | collective-permute-start | bytes 1572872 | tf_op jit(solution)/shard_map/ppermute | solution.py:32
  77.4 6.8 %shard_map.111 = (bf16[80,4096]{1,0:T(8,128)(2,1)S(1)}, bf16[64,4096]{1,0:T(8,128)(2,1)S(1)}) custom-call(f32[1,128]{1,0:T(1,128)S(1)} %and_convert_fusion.refs_0_, bf16[80,4224]{1,0:T(8,128)(2,1)S(1)} %collective-permute-done.10.refs_1_, bf16[64,4224]{1,0:T(8,128)(2,1)S(1)} %collective-permute-done.9.refs_2_, ...), custom_call_target="tpu_custom_call" | custom-call | flops 5435817984 | bytes 2359296 | tf_op jit(solution)/shard_map/pallas_call | solution.py:223
  84.3 3.3 %collective-permute-start.20 = (bf16[64,4096]{1,0:T(8,128)(2,1)S(1)}, bf16[64,4096]{1,0:T(8,128)(2,1)S(1)}, u32[]{:S(2)}, u32[]{:S(2)}) collective-permute-start(bf16[64,4096]{1,0:T(8,128)(2,1)S(1)} %add_convert_fusion.1), channel_id=1, source_target_pairs={{0,24},{1,7},{2,26},{3,1},{4,28},{5,3},{6,30},{7,5},{8,0},{9,15},{... | collective-permute-start | bytes 1572872 | tf_op jit(solution)/shard_map/ppermute | solution.py:32
  89.5 6.2 %collective-permute-done.20 = bf16[64,4096]{1,0:T(8,128)(2,1)S(1)} collective-permute-done((bf16[64,4096]{1,0:T(8,128)(2,1)S(1)}, bf16[64,4096]{1,0:T(8,128)(2,1)S(1)}, u32[]{:S(2)}, u32[]{:S(2)}) %collective-permute-start.20) | collective-permute-done | bytes 524320 | tf_op jit(solution)/shard_map/ppermute | solution.py:32
  96.2 3.3 %collective-permute-start.23 = (bf16[18,4096]{1,0:T(8,128)(2,1)S(1)}, bf16[18,4096]{1,0:T(8,128)(2,1)S(1)}, u32[]{:S(2)}, u32[]{:S(2)}) collective-permute-start(bf16[18,4096]{1,0:T(8,128)(2,1)S(1)} %get-tuple-element.92), channel_id=1, source_target_pairs={{0,6},{1,25},{2,0},{3,27},{4,2},{5,29},{6,4},{7,31},{8,14},{9,1},{... | collective-permute-start | bytes 442376 | tf_op jit(solution)/shard_map/ppermute | solution.py:28
  99.5 5.3 %collective-permute-done.18 = bf16[80,4096]{1,0:T(8,128)(2,1)S(1)} collective-permute-done((bf16[80,4096]{1,0:T(8,128)(2,1)S(1)}, bf16[80,4096]{1,0:T(8,128)(2,1)S(1)}, u32[]{:S(2)}, u32[]{:S(2)}) %collective-permute-start.18) | collective-permute-done | bytes 655392 | tf_op jit(solution)/shard_map/ppermute | solution.py:32
  105.4 3.3 %collective-permute-start.24 = (bf16[36,4096]{1,0:T(8,128)(2,1)S(1)}, bf16[36,4096]{1,0:T(8,128)(2,1)S(1)}, u32[]{:S(2)}, u32[]{:S(2)}) collective-permute-start(bf16[36,4096]{1,0:T(8,128)(2,1)S(1)} %fusion.27), channel_id=1, source_target_pairs={{0,6},{1,25},{2,0},{3,27},{4,2},{5,29},{6,4},{7,31},{8,14},{9,1},{... | collective-permute-start | bytes 884744 | tf_op jit(solution)/shard_map/ppermute | solution.py:28
  108.7 4.8 %collective-permute-done.22 = bf16[36,4096]{1,0:T(8,128)(2,1)S(1)} collective-permute-done((bf16[36,4096]{1,0:T(8,128)(2,1)S(1)}, bf16[36,4096]{1,0:T(8,128)(2,1)S(1)}, u32[]{:S(2)}, u32[]{:S(2)}) %collective-permute-start.22) | collective-permute-done | bytes 294944 | tf_op jit(solution)/shard_map/ppermute | solution.py:28
  116.3 4.5 %conditional.1 = (bf16[2,8192]{1,0:T(2,128)(2,1)S(1)}) conditional(s32[]{:T(128)} %convert_element_type.91, (s32[2]{0:T(128)S(1)}, bf16[2,8192]{1,0:T(2,128)(2,1)S(1)}, bf16[2,1024,4,256]{3,2,1,0:T(4,128)(2,1)}, bf16[2,4,256]{2,1,0:T(4,128)(2,1)S(1)}) %tuple.36, () %tuple.19), branch_computations={%region_0.3_spmd, %region_3.4_spmd} | conditional | flops 68128512 | bytes 14426640 | solution.py:293
  116.4 2.7 %copy.14 = bf16[2,1024,4,256]{3,1,2,0:T(8,128)(2,1)S(1)} copy(bf16[2,1024,4,256]{3,2,1,0:T(4,128)(2,1)} %get-tuple-element.81) | data formatting | bytes 8388608 | tf_op jit(solution)/shard_map
  (78 shorter events, 15.7 us)
Async XLA Ops:
  0.6 37.6 %collective-permute-start.11 = (bf16[4096,1536]{1,0:T(8,128)(2,1)}, bf16[4096,1536]{1,0:T(8,128)(2,1)}, u32[]{:S(2)}, u32[]{:S(2)}) collective-permute-start(bf16[4096,1536]{1,0:T(8,128)(2,1)} %bitcast.18), channel_id=1, source_target_pairs={{0,1},{1,0},{2,3},{3,2},{4,5},{5,4},{6,7},{7,6},{8,9},{9,8},{10,11... | collective-permute-start | bytes 37748744 | tf_op jit(solution)/shard_map/ppermute | solution.py:51
  0.7 37.5 %collective-permute-start.12 = (bf16[768,4096]{1,0:T(8,128)(2,1)}, bf16[768,4096]{1,0:T(8,128)(2,1)}, u32[]{:S(2)}, u32[]{:S(2)}) collective-permute-start(bf16[768,4096]{1,0:T(8,128)(2,1)} %bitcast.20), channel_id=1, source_target_pairs={{0,1},{1,0},{2,3},{3,2},{4,5},{5,4},{6,7},{7,6},{8,9},{9,8},{10,11... | collective-permute-start | bytes 18874376 | tf_op jit(solution)/shard_map/ppermute | solution.py:51
  2.2 11.0 %collective-permute-start = (bf16[12,4224]{1,0:T(8,128)(2,1)S(1)}, bf16[12,4224]{1,0:T(8,128)(2,1)S(1)}, u32[]{:S(2)}, u32[]{:S(2)}) collective-permute-start(bf16[12,4224]{1,0:T(8,128)(2,1)S(1)} %shard_map.107), channel_id=1, source_target_pairs={{0,96},{1,97},{2,98},{3,99},{4,100},{5,101},{6,102},{7,103},{8,104... | collective-permute-start | bytes 304136 | tf_op jit(solution)/shard_map/ppermute | solution.py:36
  13.3 7.5 %collective-permute-start.4 = (bf16[36,4224]{1,0:T(8,128)(2,1)S(1)}, bf16[36,4224]{1,0:T(8,128)(2,1)S(1)}, u32[]{:S(2)}, u32[]{:S(2)}) collective-permute-start(bf16[36,4224]{1,0:T(8,128)(2,1)S(1)} %pad_maximum_fusion), channel_id=1, source_target_pairs={{0,6},{1,25},{2,0},{3,27},{4,2},{5,29},{6,4},{7,31},{8,14},{9,1},{... | collective-permute-start | bytes 912392 | tf_op jit(solution)/shard_map/ppermute | solution.py:28
  16.1 8.5 %collective-permute-start.3 = (bf16[36,4224]{1,0:T(8,128)(2,1)S(1)}, bf16[36,4224]{1,0:T(8,128)(2,1)S(1)}, u32[]{:S(2)}, u32[]{:S(2)}) collective-permute-start(bf16[36,4224]{1,0:T(8,128)(2,1)S(1)} %pad_maximum_fusion), channel_id=1, source_target_pairs={{0,2},{1,9},{2,4},{3,11},{4,6},{5,13},{6,0},{7,15},{8,10},{9,17},{... | collective-permute-start | bytes 912392 | tf_op jit(solution)/shard_map/ppermute | solution.py:28
  20.9 9.3 %collective-permute-start.7 = (bf16[18,4224]{1,0:T(8,128)(2,1)S(1)}, bf16[18,4224]{1,0:T(8,128)(2,1)S(1)}, u32[]{:S(2)}, u32[]{:S(2)}) collective-permute-start(bf16[18,4224]{1,0:T(8,128)(2,1)S(1)} %slice.73), channel_id=1, source_target_pairs={{0,6},{1,25},{2,0},{3,27},{4,2},{5,29},{6,4},{7,31},{8,14},{9,1},{... | collective-permute-start | bytes 456200 | tf_op jit(solution)/shard_map/ppermute | solution.py:28
  24.7 9.3 %collective-permute-start.6 = (bf16[18,4224]{1,0:T(8,128)(2,1)S(1)}, bf16[18,4224]{1,0:T(8,128)(2,1)S(1)}, u32[]{:S(2)}, u32[]{:S(2)}) collective-permute-start(bf16[18,4224]{1,0:T(8,128)(2,1)S(1)} %slice.72), channel_id=1, source_target_pairs={{0,2},{1,9},{2,4},{3,11},{4,6},{5,13},{6,0},{7,15},{8,10},{9,17},{... | collective-permute-start | bytes 456200 | tf_op jit(solution)/shard_map/ppermute | solution.py:28
  24.9 27.9 %collective-permute-start.10 = (bf16[80,4224]{1,0:T(8,128)(2,1)S(1)}, bf16[80,4224]{1,0:T(8,128)(2,1)S(1)}, u32[]{:S(2)}, u32[]{:S(2)}) collective-permute-start(bf16[80,4224]{1,0:T(8,128)(2,1)S(1)} %pad_add_fusion.refs_1_), channel_id=1, source_target_pairs={{0,24},{1,7},{2,26},{3,1},{4,28},{5,3},{6,30},{7,5},{8,0},{9,15},{... | collective-permute-start | bytes 2027528 | tf_op jit(solution)/shard_map/ppermute | solution.py:32
  30.2 22.6 %collective-permute-start.5 = (bf16[80,4224]{1,0:T(8,128)(2,1)S(1)}, bf16[80,4224]{1,0:T(8,128)(2,1)S(1)}, u32[]{:S(2)}, u32[]{:S(2)}) collective-permute-start(bf16[80,4224]{1,0:T(8,128)(2,1)S(1)} %pad_add_fusion.refs_1_), channel_id=1, source_target_pairs={{0,8},{1,3},{2,10},{3,5},{4,12},{5,7},{6,14},{7,1},{8,16},{9,11},{... | collective-permute-start | bytes 2027528 | tf_op jit(solution)/shard_map/ppermute | solution.py:32
  34.1 18.7 %collective-permute-start.8 = (bf16[64,4224]{1,0:T(8,128)(2,1)S(1)}, bf16[64,4224]{1,0:T(8,128)(2,1)S(1)}, u32[]{:S(2)}, u32[]{:S(2)}) collective-permute-start(bf16[64,4224]{1,0:T(8,128)(2,1)S(1)} %pad_add_fusion.1.refs_2_), channel_id=1, source_target_pairs={{0,24},{1,7},{2,26},{3,1},{4,28},{5,3},{6,30},{7,5},{8,0},{9,15},{... | collective-permute-start | bytes 1622024 | tf_op jit(solution)/shard_map/ppermute | solution.py:32
  38.2 14.6 %collective-permute-start.9 = (bf16[64,4224]{1,0:T(8,128)(2,1)S(1)}, bf16[64,4224]{1,0:T(8,128)(2,1)S(1)}, u32[]{:S(2)}, u32[]{:S(2)}) collective-permute-start(bf16[64,4224]{1,0:T(8,128)(2,1)S(1)} %pad_add_fusion.1.refs_2_), channel_id=1, source_target_pairs={{0,8},{1,3},{2,10},{3,5},{4,12},{5,7},{6,14},{7,1},{8,16},{9,11},{... | collective-permute-start | bytes 1622024 | tf_op jit(solution)/shard_map/ppermute | solution.py:32
  52.8 12.1 %collective-permute-start.13 = (bf16[80,4224]{1,0:T(8,128)(2,1)S(1)}, bf16[80,4224]{1,0:T(8,128)(2,1)S(1)}, u32[]{:S(2)}, u32[]{:S(2)}) collective-permute-start(bf16[80,4224]{1,0:T(8,128)(2,1)S(1)} %collective-permute-done.5.refs_2_), channel_id=1, source_target_pairs={{0,8},{1,3},{2,10},{3,5},{4,12},{5,7},{6,14},{7,1},{8,16},{9,11},{... | collective-permute-start | bytes 2027528 | tf_op jit(solution)/shard_map/ppermute | solution.py:32
  52.9 10.4 %collective-permute-start.14 = (bf16[64,4224]{1,0:T(8,128)(2,1)S(1)}, bf16[64,4224]{1,0:T(8,128)(2,1)S(1)}, u32[]{:S(2)}, u32[]{:S(2)}) collective-permute-start(bf16[64,4224]{1,0:T(8,128)(2,1)S(1)} %collective-permute-done.8.refs_1_), channel_id=1, source_target_pairs={{0,24},{1,7},{2,26},{3,1},{4,28},{5,3},{6,30},{7,5},{8,0},{9,15},{... | collective-permute-start | bytes 1622024 | tf_op jit(solution)/shard_map/ppermute | solution.py:32
  64.9 12.4 %collective-permute-start.16 = (bf16[80,4096]{1,0:T(8,128)(2,1)S(1)}, bf16[80,4096]{1,0:T(8,128)(2,1)S(1)}, u32[]{:S(2)}, u32[]{:S(2)}) collective-permute-start(bf16[80,4096]{1,0:T(8,128)(2,1)S(1)} %get-tuple-element.61), channel_id=1, source_target_pairs={{0,24},{1,7},{2,26},{3,1},{4,28},{5,3},{6,30},{7,5},{8,0},{9,15},{... | collective-permute-start | bytes 1966088 | tf_op jit(solution)/shard_map/ppermute | solution.py:32
  67.0 10.4 %collective-permute-start.15 = (bf16[64,4096]{1,0:T(8,128)(2,1)S(1)}, bf16[64,4096]{1,0:T(8,128)(2,1)S(1)}, u32[]{:S(2)}, u32[]{:S(2)}) collective-permute-start(bf16[64,4096]{1,0:T(8,128)(2,1)S(1)} %get-tuple-element.60), channel_id=1, source_target_pairs={{0,8},{1,3},{2,10},{3,5},{4,12},{5,7},{6,14},{7,1},{8,16},{9,11},{... | collective-permute-start | bytes 1572872 | tf_op jit(solution)/shard_map/ppermute | solution.py:32
  73.8 10.4 %collective-permute-start.19 = (bf16[64,4096]{1,0:T(8,128)(2,1)S(1)}, bf16[64,4096]{1,0:T(8,128)(2,1)S(1)}, u32[]{:S(2)}, u32[]{:S(2)}) collective-permute-start(bf16[64,4096]{1,0:T(8,128)(2,1)S(1)} %get-tuple-element.72), channel_id=1, source_target_pairs={{0,24},{1,7},{2,26},{3,1},{4,28},{5,3},{6,30},{7,5},{8,0},{9,15},{... | collective-permute-start | bytes 1572872 | tf_op jit(solution)/shard_map/ppermute | solution.py:32
  77.1 12.2 %collective-permute-start.17 = (bf16[80,4096]{1,0:T(8,128)(2,1)S(1)}, bf16[80,4096]{1,0:T(8,128)(2,1)S(1)}, u32[]{:S(2)}, u32[]{:S(2)}) collective-permute-start(bf16[80,4096]{1,0:T(8,128)(2,1)S(1)} %get-tuple-element.64), channel_id=1, source_target_pairs={{0,8},{1,3},{2,10},{3,5},{4,12},{5,7},{6,14},{7,1},{8,16},{9,11},{... | collective-permute-start | bytes 1966088 | tf_op jit(solution)/shard_map/ppermute | solution.py:32
  84.3 11.4 %collective-permute-start.20 = (bf16[64,4096]{1,0:T(8,128)(2,1)S(1)}, bf16[64,4096]{1,0:T(8,128)(2,1)S(1)}, u32[]{:S(2)}, u32[]{:S(2)}) collective-permute-start(bf16[64,4096]{1,0:T(8,128)(2,1)S(1)} %add_convert_fusion.1), channel_id=1, source_target_pairs={{0,24},{1,7},{2,26},{3,1},{4,28},{5,3},{6,30},{7,5},{8,0},{9,15},{... | collective-permute-start | bytes 1572872 | tf_op jit(solution)/shard_map/ppermute | solution.py:32
  89.4 15.4 %collective-permute-start.18 = (bf16[80,4096]{1,0:T(8,128)(2,1)S(1)}, bf16[80,4096]{1,0:T(8,128)(2,1)S(1)}, u32[]{:S(2)}, u32[]{:S(2)}) collective-permute-start(bf16[80,4096]{1,0:T(8,128)(2,1)S(1)} %add_convert_fusion), channel_id=1, source_target_pairs={{0,8},{1,3},{2,10},{3,5},{4,12},{5,7},{6,14},{7,1},{8,16},{9,11},{... | collective-permute-start | bytes 1966088 | tf_op jit(solution)/shard_map/ppermute | solution.py:32
  96.1 9.0 %collective-permute-start.21 = (bf16[18,4096]{1,0:T(8,128)(2,1)S(1)}, bf16[18,4096]{1,0:T(8,128)(2,1)S(1)}, u32[]{:S(2)}, u32[]{:S(2)}) collective-permute-start(bf16[18,4096]{1,0:T(8,128)(2,1)S(1)} %get-tuple-element.91), channel_id=1, source_target_pairs={{0,2},{1,9},{2,4},{3,11},{4,6},{5,13},{6,0},{7,15},{8,10},{9,17},{... | collective-permute-start | bytes 442376 | tf_op jit(solution)/shard_map/ppermute | solution.py:28
  96.2 9.0 %collective-permute-start.23 = (bf16[18,4096]{1,0:T(8,128)(2,1)S(1)}, bf16[18,4096]{1,0:T(8,128)(2,1)S(1)}, u32[]{:S(2)}, u32[]{:S(2)}) collective-permute-start(bf16[18,4096]{1,0:T(8,128)(2,1)S(1)} %get-tuple-element.92), channel_id=1, source_target_pairs={{0,6},{1,25},{2,0},{3,27},{4,2},{5,29},{6,4},{7,31},{8,14},{9,1},{... | collective-permute-start | bytes 442376 | tf_op jit(solution)/shard_map/ppermute | solution.py:28
  105.1 8.4 %collective-permute-start.22 = (bf16[36,4096]{1,0:T(8,128)(2,1)S(1)}, bf16[36,4096]{1,0:T(8,128)(2,1)S(1)}, u32[]{:S(2)}, u32[]{:S(2)}) collective-permute-start(bf16[36,4096]{1,0:T(8,128)(2,1)S(1)} %fusion.30), channel_id=1, source_target_pairs={{0,2},{1,9},{2,4},{3,11},{4,6},{5,13},{6,0},{7,15},{8,10},{9,17},{... | collective-permute-start | bytes 884744 | tf_op jit(solution)/shard_map/ppermute | solution.py:28
  105.4 8.1 %collective-permute-start.24 = (bf16[36,4096]{1,0:T(8,128)(2,1)S(1)}, bf16[36,4096]{1,0:T(8,128)(2,1)S(1)}, u32[]{:S(2)}, u32[]{:S(2)}) collective-permute-start(bf16[36,4096]{1,0:T(8,128)(2,1)S(1)} %fusion.27), channel_id=1, source_target_pairs={{0,6},{1,25},{2,0},{3,27},{4,2},{5,29},{6,4},{7,31},{8,14},{9,1},{... | collective-permute-start | bytes 884744 | tf_op jit(solution)/shard_map/ppermute | solution.py:28
  113.7 8.1 %collective-permute-start.25 = (bf16[12,4096]{1,0:T(8,128)(2,1)S(1)}, bf16[12,4096]{1,0:T(8,128)(2,1)S(1)}, u32[]{:S(2)}, u32[]{:S(2)}) collective-permute-start(bf16[12,4096]{1,0:T(8,128)(2,1)S(1)} %get-tuple-element.95), channel_id=1, source_target_pairs={{96,0},{97,1},{98,2},{99,3},{100,4},{101,5},{102,6},{103,7},{104,8... | collective-permute-start | bytes 294920 | tf_op jit(solution)/shard_map/ppermute | solution.py:36
  (8 other events, 58.7 us)

commit v8 on v6

--- a/solution.py
+++ b/solution.py
@@ -267,15 +267,15 @@
     behind, ahead, far = step_u(block, 1), step_u(block, -1), step_u(block, 2)
     group_a, group_b = stacked([block, behind, ahead[:lead]]), stacked([ahead[lead:], far])
     before_a, after_b = step_v(group_a, 1), step_v(group_b, -1)
-    before_b, after_a = step_v(group_b, 1), step_v(group_a, -1)
     column = lax.broadcasted_iota(jnp.int32, (1, EXTRA), 1)
     pick = ((column % experts == expert) & (column < 3 * experts)).astype(f32)
     (own_a, own_b), halves = experts_on([group_a, group_b], pick, halves)
 
-    before_a, after_b, before_b, after_a, own_a, own_b = lax.optimization_barrier(
-        (before_a, after_b, before_b, after_a, own_a, own_b)
+    before_a, after_b, group_a, group_b, own_a, own_b = lax.optimization_barrier(
+        (before_a, after_b, group_a, group_b, own_a, own_b)
     )
     across_a, across_b = step_v(before_a, 1), step_v(after_b, -1)
+    before_b, after_a = step_v(group_b, 1), step_v(group_a, -1)
     (after_b, before_a), _ = experts_on([after_b, before_a], pick, halves)
     across_a, across_b, after_b, before_a = lax.optimization_barrier((across_a, across_b, after_b, before_a))
 

time: 120 us -> 125 us (1.042)
  waiting for transfers between devices: 34.2 us -> 38.8 us
    ppermute x7, waiting for transfers between devices: 14.6 us -> 17.9 us  [step_u(): return lax.ppermute(block, 'dev', along(True, distance))]
    ppermute x12, waiting for transfers between devices: 14.1 us -> 15.4 us  [step_v(): return lax.ppermute(block, 'dev', along(False, distance))]
  transfers between devices with their start and end apart: 27 -> 27, of which waited for: 11 -> 11; matrix products, arithmetic and copies ran while one was open for 5% -> 5% of each run, Pallas kernels for 30% -> 29%
where the time goes in v8:
time: 125 us; the launch traced here: 123 us
  starting transfers between devices  40.9 us (33%)
  waiting for transfers between devices  38.8 us (31%)
  Pallas kernels  35.5 us (28%)
  local copies, waits for them, and re-layouts  3.01 us (2%)
  other arithmetic  2.32 us (2%)
  matrix products  1.33 us (1%)
    pallas_call x4, Pallas kernels, experts_on(): pl.pallas_call(functools.partial(expert_kernel, len(pieces), 1024, load),...  34.6 us
    ppermute x12, starting transfers between devices, step_v(): return lax.ppermute(block, 'dev', along(False, distance))  19.5 us
    ppermute x7, waiting for transfers between devices, step_u(): return lax.ppermute(block, 'dev', along(True, distance))  17.9 us
    ppermute x12, waiting for transfers between devices, step_v(): return lax.ppermute(block, 'dev', along(False, distance))  15.4 us
    ppermute x7, starting transfers between devices, step_u(): return lax.ppermute(block, 'dev', along(True, distance))  11.8 us
    ppermute x6, starting transfers between devices, to_section(): return lax.ppermute(block, 'sec', [(source, target)])  8.98 us
    ppermute x6, waiting for transfers between devices, to_section(): return lax.ppermute(block, 'sec', [(source, target)])  5.51 us
    another operation x1, local copies, waits for them, and re-layouts  2.74 us
  transfers between devices with their start and end apart: 27, of which 11 were waited for; matrix products, arithmetic and copies ran while one was open for 5% of the time, Pallas kernels for 29%

profile of v8, /device:TPU:0, one launch (start us, length us, event | category | flops | bytes accessed | tf_op | source)
XLA Modules:
  0.0 122.9 jit_solution(1898326381924953086)
XLA Ops:
  2.2 5.0 %collective-permute-start = (bf16[12,4224]{1,0:T(8,128)(2,1)S(1)}, bf16[12,4224]{1,0:T(8,128)(2,1)S(1)}, u32[]{:S(2)}, u32[]{:S(2)}) collective-permute-start(bf16[12,4224]{1,0:T(8,128)(2,1)S(1)} %shard_map.107), channel_id=1, source_target_pairs={{0,96},{1,97},{2,98},{3,99},{4,100},{5,101},{6,102},{7,103},{8,104... | collective-permute-start | bytes 304136 | tf_op jit(solution)/shard_map/ppermute | solution.py:36
  8.6 4.7 %collective-permute-done = bf16[12,4224]{1,0:T(8,128)(2,1)S(1)} collective-permute-done((bf16[12,4224]{1,0:T(8,128)(2,1)S(1)}, bf16[12,4224]{1,0:T(8,128)(2,1)S(1)}, u32[]{:S(2)}, u32[]{:S(2)}) %collective-permute-start) | collective-permute-done | bytes 101408 | tf_op jit(solution)/shard_map/ppermute | solution.py:36
  13.3 2.8 %collective-permute-start.4 = (bf16[36,4224]{1,0:T(8,128)(2,1)S(1)}, bf16[36,4224]{1,0:T(8,128)(2,1)S(1)}, u32[]{:S(2)}, u32[]{:S(2)}) collective-permute-start(bf16[36,4224]{1,0:T(8,128)(2,1)S(1)} %pad_maximum_fusion), channel_id=1, source_target_pairs={{0,6},{1,25},{2,0},{3,27},{4,2},{5,29},{6,4},{7,31},{8,14},{9,1},{... | collective-permute-start | bytes 912392 | tf_op jit(solution)/shard_map/ppermute | solution.py:28
  16.1 2.3 %collective-permute-start.6 = (bf16[36,4224]{1,0:T(8,128)(2,1)S(1)}, bf16[36,4224]{1,0:T(8,128)(2,1)S(1)}, u32[]{:S(2)}, u32[]{:S(2)}) collective-permute-start(bf16[36,4224]{1,0:T(8,128)(2,1)S(1)} %pad_maximum_fusion), channel_id=1, source_target_pairs={{0,4},{1,17},{2,6},{3,19},{4,0},{5,21},{6,2},{7,23},{8,12},{9,25},... | collective-permute-start | bytes 912392 | tf_op jit(solution)/shard_map/ppermute | solution.py:28
  18.4 2.5 %collective-permute-done.4 = bf16[36,4224]{1,0:T(8,128)(2,1)S(1)} collective-permute-done((bf16[36,4224]{1,0:T(8,128)(2,1)S(1)}, bf16[36,4224]{1,0:T(8,128)(2,1)S(1)}, u32[]{:S(2)}, u32[]{:S(2)}) %collective-permute-start.4) | collective-permute-done | bytes 304160 | tf_op jit(solution)/shard_map/ppermute | solution.py:28
  21.0 7.2 %collective-permute-done.3 = bf16[36,4224]{1,0:T(8,128)(2,1)S(1)} collective-permute-done((bf16[36,4224]{1,0:T(8,128)(2,1)S(1)}, bf16[36,4224]{1,0:T(8,128)(2,1)S(1)}, u32[]{:S(2)}, u32[]{:S(2)}) %collective-permute-start.3) | collective-permute-done | bytes 304160 | tf_op jit(solution)/shard_map/ppermute | solution.py:28
  28.3 3.8 %collective-permute-start.5 = (bf16[80,4224]{1,0:T(8,128)(2,1)S(1)}, bf16[80,4224]{1,0:T(8,128)(2,1)S(1)}, u32[]{:S(2)}, u32[]{:S(2)}) collective-permute-start(bf16[80,4224]{1,0:T(8,128)(2,1)S(1)} %pad_add_fusion.refs_1_), channel_id=1, source_target_pairs={{0,8},{1,3},{2,10},{3,5},{4,12},{5,7},{6,14},{7,1},{8,16},{9,11},{... | collective-permute-start | bytes 2027528 | tf_op jit(solution)/shard_map/ppermute | solution.py:32
  33.4 14.6 %shard_map.108 = (bf16[80,4096]{1,0:T(8,128)(2,1)S(1)}, bf16[64,4096]{1,0:T(8,128)(2,1)S(1)}, bf16[4096,768]{1,0:T(8,128)(2,1)S(1)}, bf16[4096,768]{1,0:T(8,128)...) custom-call(f32[1,128]{1,0:T(1,128)S(1)} %and_convert_fusion.refs_0_, ...), custom_call_target="tpu_custom_call" | custom-call | flops 5435817984 | bytes 37748736 | tf_op jit(solution)/shard_map/pallas_call | solution.py:223
  49.0 4.2 %collective-permute-start.13 = (bf16[64,4224]{1,0:T(8,128)(2,1)S(1)}, bf16[64,4224]{1,0:T(8,128)(2,1)S(1)}, u32[]{:S(2)}, u32[]{:S(2)}) collective-permute-start(bf16[64,4224]{1,0:T(8,128)(2,1)S(1)} %collective-permute-done.7.refs_1_), channel_id=1, source_target_pairs={{0,24},{1,7},{2,26},{3,1},{4,28},{5,3},{6,30},{7,5},{8,0},{9,15},{... | collective-permute-start | bytes 1622024 | tf_op jit(solution)/shard_map/ppermute | solution.py:32
  53.2 1.9 %collective-permute-start.10 = (bf16[80,4224]{1,0:T(8,128)(2,1)S(1)}, bf16[80,4224]{1,0:T(8,128)(2,1)S(1)}, u32[]{:S(2)}, u32[]{:S(2)}) collective-permute-start(bf16[80,4224]{1,0:T(8,128)(2,1)S(1)} %pad_add_fusion.refs_1_), channel_id=1, source_target_pairs={{0,24},{1,7},{2,26},{3,1},{4,28},{5,3},{6,30},{7,5},{8,0},{9,15},{... | collective-permute-start | bytes 2027528 | tf_op jit(solution)/shard_map/ppermute | solution.py:32
  55.1 6.6 %shard_map.109 = (bf16[64,4096]{1,0:T(8,128)(2,1)S(1)}, bf16[80,4096]{1,0:T(8,128)(2,1)S(1)}) custom-call(f32[1,128]{1,0:T(1,128)S(1)} %and_convert_fusion.refs_0_, bf16[64,4224]{1,0:T(8,128)(2,1)S(1)} %collective-permute-done.7.refs_1_, bf16[80,4224]{1,0:T(8,128)(2,1)S(1)} %collective-permute-done.5.refs_2_, ...), custom_call_target="tpu_custom_call" | custom-call | flops 5435817984 | bytes 2359296 | tf_op jit(solution)/shard_map/pallas_call | solution.py:223
  61.9 2.0 %collective-permute-start.15 = (bf16[80,4096]{1,0:T(8,128)(2,1)S(1)}, bf16[80,4096]{1,0:T(8,128)(2,1)S(1)}, u32[]{:S(2)}, u32[]{:S(2)}) collective-permute-start(bf16[80,4096]{1,0:T(8,128)(2,1)S(1)} %get-tuple-element.61), channel_id=1, source_target_pairs={{0,24},{1,7},{2,26},{3,1},{4,28},{5,3},{6,30},{7,5},{8,0},{9,15},{... | collective-permute-start | bytes 1966088 | tf_op jit(solution)/shard_map/ppermute | solution.py:32
  63.9 6.7 %shard_map.110 = (bf16[80,4096]{1,0:T(8,128)(2,1)S(1)}, bf16[64,4096]{1,0:T(8,128)(2,1)S(1)}) custom-call(f32[1,128]{1,0:T(1,128)S(1)} %and_convert_fusion.refs_0_, bf16[80,4224]{1,0:T(8,128)(2,1)S(1)} %collective-permute-done.12.refs_1_, bf16[64,4224]{1,0:T(8,128)(2,1)S(1)} %collective-permute-done.13.refs_2_, ...), custom_call_target="tpu_custom_call" | custom-call | flops 5435817984 | bytes 2359296 | tf_op jit(solution)/shard_map/pallas_call | solution.py:223
  70.7 3.3 %collective-permute-start.18 = (bf16[64,4096]{1,0:T(8,128)(2,1)S(1)}, bf16[64,4096]{1,0:T(8,128)(2,1)S(1)}, u32[]{:S(2)}, u32[]{:S(2)}) collective-permute-start(bf16[64,4096]{1,0:T(8,128)(2,1)S(1)} %get-tuple-element.72), channel_id=1, source_target_pairs={{0,24},{1,7},{2,26},{3,1},{4,28},{5,3},{6,30},{7,5},{8,0},{9,15},{... | collective-permute-start | bytes 1572872 | tf_op jit(solution)/shard_map/ppermute | solution.py:32
  74.5 5.6 %collective-permute-done.14 = bf16[64,4096]{1,0:T(8,128)(2,1)S(1)} collective-permute-done((bf16[64,4096]{1,0:T(8,128)(2,1)S(1)}, bf16[64,4096]{1,0:T(8,128)(2,1)S(1)}, u32[]{:S(2)}, u32[]{:S(2)}) %collective-permute-start.14) | collective-permute-done | bytes 524320 | tf_op jit(solution)/shard_map/ppermute | solution.py:32
  80.1 6.7 %shard_map.111 = (bf16[80,4096]{1,0:T(8,128)(2,1)S(1)}, bf16[64,4096]{1,0:T(8,128)(2,1)S(1)}) custom-call(f32[1,128]{1,0:T(1,128)S(1)} %and_convert_fusion.refs_0_, bf16[80,4224]{1,0:T(8,128)(2,1)S(1)} %collective-permute-done.10.refs_1_, bf16[64,4224]{1,0:T(8,128)(2,1)S(1)} %collective-permute-done.11.refs_2_, ...), custom_call_target="tpu_custom_call" | custom-call | flops 5435817984 | bytes 2359296 | tf_op jit(solution)/shard_map/pallas_call | solution.py:223
  87.3 2.0 %collective-permute-start.17 = (bf16[80,4096]{1,0:T(8,128)(2,1)S(1)}, bf16[80,4096]{1,0:T(8,128)(2,1)S(1)}, u32[]{:S(2)}, u32[]{:S(2)}) collective-permute-start(bf16[80,4096]{1,0:T(8,128)(2,1)S(1)} %add_convert_fusion), channel_id=1, source_target_pairs={{0,8},{1,3},{2,10},{3,5},{4,12},{5,7},{6,14},{7,1},{8,16},{9,11},{... | collective-permute-start | bytes 1966088 | tf_op jit(solution)/shard_map/ppermute | solution.py:32
  89.3 9.0 %collective-permute-done.19 = bf16[64,4096]{1,0:T(8,128)(2,1)S(1)} collective-permute-done((bf16[64,4096]{1,0:T(8,128)(2,1)S(1)}, bf16[64,4096]{1,0:T(8,128)(2,1)S(1)}, u32[]{:S(2)}, u32[]{:S(2)}) %collective-permute-start.19) | collective-permute-done | bytes 524320 | tf_op jit(solution)/shard_map/ppermute | solution.py:32
  98.7 3.3 %collective-permute-start.22 = (bf16[18,4096]{1,0:T(8,128)(2,1)S(1)}, bf16[18,4096]{1,0:T(8,128)(2,1)S(1)}, u32[]{:S(2)}, u32[]{:S(2)}) collective-permute-start(bf16[18,4096]{1,0:T(8,128)(2,1)S(1)} %get-tuple-element.92), channel_id=1, source_target_pairs={{0,6},{1,25},{2,0},{3,27},{4,2},{5,29},{6,4},{7,31},{8,14},{9,1},{... | collective-permute-start | bytes 442376 | tf_op jit(solution)/shard_map/ppermute | solution.py:28
  102.3 3.3 %collective-permute-done.20 = bf16[18,4096]{1,0:T(8,128)(2,1)S(1)} collective-permute-done((bf16[18,4096]{1,0:T(8,128)(2,1)S(1)}, bf16[18,4096]{1,0:T(8,128)(2,1)S(1)}, u32[]{:S(2)}, u32[]{:S(2)}) %collective-permute-start.20) | collective-permute-done | bytes 147488 | tf_op jit(solution)/shard_map/ppermute | solution.py:28
  105.9 3.3 %collective-permute-start.23 = (bf16[36,4096]{1,0:T(8,128)(2,1)S(1)}, bf16[36,4096]{1,0:T(8,128)(2,1)S(1)}, u32[]{:S(2)}, u32[]{:S(2)}) collective-permute-start(bf16[36,4096]{1,0:T(8,128)(2,1)S(1)} %fusion.27), channel_id=1, source_target_pairs={{0,6},{1,25},{2,0},{3,27},{4,2},{5,29},{6,4},{7,31},{8,14},{9,1},{... | collective-permute-start | bytes 884744 | tf_op jit(solution)/shard_map/ppermute | solution.py:28
  109.1 4.9 %collective-permute-done.21 = bf16[36,4096]{1,0:T(8,128)(2,1)S(1)} collective-permute-done((bf16[36,4096]{1,0:T(8,128)(2,1)S(1)}, bf16[36,4096]{1,0:T(8,128)(2,1)S(1)}, u32[]{:S(2)}, u32[]{:S(2)}) %collective-permute-start.21) | collective-permute-done | bytes 294944 | tf_op jit(solution)/shard_map/ppermute | solution.py:28
  116.9 4.5 %conditional.1 = (bf16[2,8192]{1,0:T(2,128)(2,1)S(1)}) conditional(s32[]{:T(128)} %convert_element_type.89, (s32[2]{0:T(128)S(1)}, bf16[2,8192]{1,0:T(2,128)(2,1)S(1)}, bf16[2,1024,4,256]{3,2,1,0:T(4,128)(2,1)}, bf16[2,4,256]{2,1,0:T(4,128)(2,1)S(1)}) %tuple.36, () %tuple.19), branch_computations={%region_0.3_spmd, %region_3.4_spmd} | conditional | flops 68128512 | bytes 14426640 | solution.py:291
  116.9 2.7 %copy.14 = bf16[2,1024,4,256]{3,1,2,0:T(8,128)(2,1)S(1)} copy(bf16[2,1024,4,256]{3,2,1,0:T(4,128)(2,1)} %get-tuple-element.81) | data formatting | bytes 8388608 | tf_op jit(solution)/shard_map
  (74 shorter events, 13.5 us)
Async XLA Ops:
  0.6 32.8 %collective-permute-start.8 = (bf16[4096,1536]{1,0:T(8,128)(2,1)}, bf16[4096,1536]{1,0:T(8,128)(2,1)}, u32[]{:S(2)}, u32[]{:S(2)}) collective-permute-start(bf16[4096,1536]{1,0:T(8,128)(2,1)} %bitcast.18), channel_id=1, source_target_pairs={{0,1},{1,0},{2,3},{3,2},{4,5},{5,4},{6,7},{7,6},{8,9},{9,8},{10,11... | collective-permute-start | bytes 37748744 | tf_op jit(solution)/shard_map/ppermute | solution.py:51
  0.7 32.7 %collective-permute-start.9 = (bf16[768,4096]{1,0:T(8,128)(2,1)}, bf16[768,4096]{1,0:T(8,128)(2,1)}, u32[]{:S(2)}, u32[]{:S(2)}) collective-permute-start(bf16[768,4096]{1,0:T(8,128)(2,1)} %bitcast.20), channel_id=1, source_target_pairs={{0,1},{1,0},{2,3},{3,2},{4,5},{5,4},{6,7},{7,6},{8,9},{9,8},{10,11... | collective-permute-start | bytes 18874376 | tf_op jit(solution)/shard_map/ppermute | solution.py:51
  2.2 11.0 %collective-permute-start = (bf16[12,4224]{1,0:T(8,128)(2,1)S(1)}, bf16[12,4224]{1,0:T(8,128)(2,1)S(1)}, u32[]{:S(2)}, u32[]{:S(2)}) collective-permute-start(bf16[12,4224]{1,0:T(8,128)(2,1)S(1)} %shard_map.107), channel_id=1, source_target_pairs={{0,96},{1,97},{2,98},{3,99},{4,100},{5,101},{6,102},{7,103},{8,104... | collective-permute-start | bytes 304136 | tf_op jit(solution)/shard_map/ppermute | solution.py:36
  13.3 7.7 %collective-permute-start.4 = (bf16[36,4224]{1,0:T(8,128)(2,1)S(1)}, bf16[36,4224]{1,0:T(8,128)(2,1)S(1)}, u32[]{:S(2)}, u32[]{:S(2)}) collective-permute-start(bf16[36,4224]{1,0:T(8,128)(2,1)S(1)} %pad_maximum_fusion), channel_id=1, source_target_pairs={{0,6},{1,25},{2,0},{3,27},{4,2},{5,29},{6,4},{7,31},{8,14},{9,1},{... | collective-permute-start | bytes 912392 | tf_op jit(solution)/shard_map/ppermute | solution.py:28
  16.1 12.0 %collective-permute-start.3 = (bf16[36,4224]{1,0:T(8,128)(2,1)S(1)}, bf16[36,4224]{1,0:T(8,128)(2,1)S(1)}, u32[]{:S(2)}, u32[]{:S(2)}) collective-permute-start(bf16[36,4224]{1,0:T(8,128)(2,1)S(1)} %pad_maximum_fusion), channel_id=1, source_target_pairs={{0,2},{1,9},{2,4},{3,11},{4,6},{5,13},{6,0},{7,15},{8,10},{9,17},{... | collective-permute-start | bytes 912392 | tf_op jit(solution)/shard_map/ppermute | solution.py:28
  16.1 15.9 %collective-permute-start.6 = (bf16[36,4224]{1,0:T(8,128)(2,1)S(1)}, bf16[36,4224]{1,0:T(8,128)(2,1)S(1)}, u32[]{:S(2)}, u32[]{:S(2)}) collective-permute-start(bf16[36,4224]{1,0:T(8,128)(2,1)S(1)} %pad_maximum_fusion), channel_id=1, source_target_pairs={{0,4},{1,17},{2,6},{3,19},{4,0},{5,21},{6,2},{7,23},{8,12},{9,25},... | collective-permute-start | bytes 912392 | tf_op jit(solution)/shard_map/ppermute | solution.py:28
  28.3 19.7 %collective-permute-start.5 = (bf16[80,4224]{1,0:T(8,128)(2,1)S(1)}, bf16[80,4224]{1,0:T(8,128)(2,1)S(1)}, u32[]{:S(2)}, u32[]{:S(2)}) collective-permute-start(bf16[80,4224]{1,0:T(8,128)(2,1)S(1)} %pad_add_fusion.refs_1_), channel_id=1, source_target_pairs={{0,8},{1,3},{2,10},{3,5},{4,12},{5,7},{6,14},{7,1},{8,16},{9,11},{... | collective-permute-start | bytes 2027528 | tf_op jit(solution)/shard_map/ppermute | solution.py:32
  32.2 15.8 %collective-permute-start.7 = (bf16[64,4224]{1,0:T(8,128)(2,1)S(1)}, bf16[64,4224]{1,0:T(8,128)(2,1)S(1)}, u32[]{:S(2)}, u32[]{:S(2)}) collective-permute-start(bf16[64,4224]{1,0:T(8,128)(2,1)S(1)} %pad_add_fusion.1.refs_2_), channel_id=1, source_target_pairs={{0,24},{1,7},{2,26},{3,1},{4,28},{5,3},{6,30},{7,5},{8,0},{9,15},{... | collective-permute-start | bytes 1622024 | tf_op jit(solution)/shard_map/ppermute | solution.py:32
  48.0 13.9 %collective-permute-start.12 = (bf16[80,4224]{1,0:T(8,128)(2,1)S(1)}, bf16[80,4224]{1,0:T(8,128)(2,1)S(1)}, u32[]{:S(2)}, u32[]{:S(2)}) collective-permute-start(bf16[80,4224]{1,0:T(8,128)(2,1)S(1)} %collective-permute-done.5.refs_2_), channel_id=1, source_target_pairs={{0,8},{1,3},{2,10},{3,5},{4,12},{5,7},{6,14},{7,1},{8,16},{9,11},{... | collective-permute-start | bytes 2027528 | tf_op jit(solution)/shard_map/ppermute | solution.py:32
  49.0 12.7 %collective-permute-start.13 = (bf16[64,4224]{1,0:T(8,128)(2,1)S(1)}, bf16[64,4224]{1,0:T(8,128)(2,1)S(1)}, u32[]{:S(2)}, u32[]{:S(2)}) collective-permute-start(bf16[64,4224]{1,0:T(8,128)(2,1)S(1)} %collective-permute-done.7.refs_1_), channel_id=1, source_target_pairs={{0,24},{1,7},{2,26},{3,1},{4,28},{5,3},{6,30},{7,5},{8,0},{9,15},{... | collective-permute-start | bytes 1622024 | tf_op jit(solution)/shard_map/ppermute | solution.py:32
  53.2 21.3 %collective-permute-start.10 = (bf16[80,4224]{1,0:T(8,128)(2,1)S(1)}, bf16[80,4224]{1,0:T(8,128)(2,1)S(1)}, u32[]{:S(2)}, u32[]{:S(2)}) collective-permute-start(bf16[80,4224]{1,0:T(8,128)(2,1)S(1)} %pad_add_fusion.refs_1_), channel_id=1, source_target_pairs={{0,24},{1,7},{2,26},{3,1},{4,28},{5,3},{6,30},{7,5},{8,0},{9,15},{... | collective-permute-start | bytes 2027528 | tf_op jit(solution)/shard_map/ppermute | solution.py:32
  61.9 18.2 %collective-permute-start.15 = (bf16[80,4096]{1,0:T(8,128)(2,1)S(1)}, bf16[80,4096]{1,0:T(8,128)(2,1)S(1)}, u32[]{:S(2)}, u32[]{:S(2)}) collective-permute-start(bf16[80,4096]{1,0:T(8,128)(2,1)S(1)} %get-tuple-element.61), channel_id=1, source_target_pairs={{0,24},{1,7},{2,26},{3,1},{4,28},{5,3},{6,30},{7,5},{8,0},{9,15},{... | collective-permute-start | bytes 1966088 | tf_op jit(solution)/shard_map/ppermute | solution.py:32
  63.9 10.6 %collective-permute-start.11 = (bf16[64,4224]{1,0:T(8,128)(2,1)S(1)}, bf16[64,4224]{1,0:T(8,128)(2,1)S(1)}, u32[]{:S(2)}, u32[]{:S(2)}) collective-permute-start(bf16[64,4224]{1,0:T(8,128)(2,1)S(1)} %pad_add_fusion.1.refs_2_), channel_id=1, source_target_pairs={{0,8},{1,3},{2,10},{3,5},{4,12},{5,7},{6,14},{7,1},{8,16},{9,11},{... | collective-permute-start | bytes 1622024 | tf_op jit(solution)/shard_map/ppermute | solution.py:32
  63.9 16.2 %collective-permute-start.14 = (bf16[64,4096]{1,0:T(8,128)(2,1)S(1)}, bf16[64,4096]{1,0:T(8,128)(2,1)S(1)}, u32[]{:S(2)}, u32[]{:S(2)}) collective-permute-start(bf16[64,4096]{1,0:T(8,128)(2,1)S(1)} %get-tuple-element.60), channel_id=1, source_target_pairs={{0,8},{1,3},{2,10},{3,5},{4,12},{5,7},{6,14},{7,1},{8,16},{9,11},{... | collective-permute-start | bytes 1572872 | tf_op jit(solution)/shard_map/ppermute | solution.py:32
  70.7 16.1 %collective-permute-start.18 = (bf16[64,4096]{1,0:T(8,128)(2,1)S(1)}, bf16[64,4096]{1,0:T(8,128)(2,1)S(1)}, u32[]{:S(2)}, u32[]{:S(2)}) collective-permute-start(bf16[64,4096]{1,0:T(8,128)(2,1)S(1)} %get-tuple-element.72), channel_id=1, source_target_pairs={{0,24},{1,7},{2,26},{3,1},{4,28},{5,3},{6,30},{7,5},{8,0},{9,15},{... | collective-permute-start | bytes 1572872 | tf_op jit(solution)/shard_map/ppermute | solution.py:32
  74.5 12.6 %collective-permute-start.16 = (bf16[80,4096]{1,0:T(8,128)(2,1)S(1)}, bf16[80,4096]{1,0:T(8,128)(2,1)S(1)}, u32[]{:S(2)}, u32[]{:S(2)}) collective-permute-start(bf16[80,4096]{1,0:T(8,128)(2,1)S(1)} %get-tuple-element.64), channel_id=1, source_target_pairs={{0,8},{1,3},{2,10},{3,5},{4,12},{5,7},{6,14},{7,1},{8,16},{9,11},{... | collective-permute-start | bytes 1966088 | tf_op jit(solution)/shard_map/ppermute | solution.py:32
  86.9 11.4 %collective-permute-start.19 = (bf16[64,4096]{1,0:T(8,128)(2,1)S(1)}, bf16[64,4096]{1,0:T(8,128)(2,1)S(1)}, u32[]{:S(2)}, u32[]{:S(2)}) collective-permute-start(bf16[64,4096]{1,0:T(8,128)(2,1)S(1)} %add_convert_fusion.1), channel_id=1, source_target_pairs={{0,24},{1,7},{2,26},{3,1},{4,28},{5,3},{6,30},{7,5},{8,0},{9,15},{... | collective-permute-start | bytes 1572872 | tf_op jit(solution)/shard_map/ppermute | solution.py:32
  87.3 14.7 %collective-permute-start.17 = (bf16[80,4096]{1,0:T(8,128)(2,1)S(1)}, bf16[80,4096]{1,0:T(8,128)(2,1)S(1)}, u32[]{:S(2)}, u32[]{:S(2)}) collective-permute-start(bf16[80,4096]{1,0:T(8,128)(2,1)S(1)} %add_convert_fusion), channel_id=1, source_target_pairs={{0,8},{1,3},{2,10},{3,5},{4,12},{5,7},{6,14},{7,1},{8,16},{9,11},{... | collective-permute-start | bytes 1966088 | tf_op jit(solution)/shard_map/ppermute | solution.py:32
  98.6 6.9 %collective-permute-start.20 = (bf16[18,4096]{1,0:T(8,128)(2,1)S(1)}, bf16[18,4096]{1,0:T(8,128)(2,1)S(1)}, u32[]{:S(2)}, u32[]{:S(2)}) collective-permute-start(bf16[18,4096]{1,0:T(8,128)(2,1)S(1)} %get-tuple-element.91), channel_id=1, source_target_pairs={{0,2},{1,9},{2,4},{3,11},{4,6},{5,13},{6,0},{7,15},{8,10},{9,17},{... | collective-permute-start | bytes 442376 | tf_op jit(solution)/shard_map/ppermute | solution.py:28
  98.7 7.0 %collective-permute-start.22 = (bf16[18,4096]{1,0:T(8,128)(2,1)S(1)}, bf16[18,4096]{1,0:T(8,128)(2,1)S(1)}, u32[]{:S(2)}, u32[]{:S(2)}) collective-permute-start(bf16[18,4096]{1,0:T(8,128)(2,1)S(1)} %get-tuple-element.92), channel_id=1, source_target_pairs={{0,6},{1,25},{2,0},{3,27},{4,2},{5,29},{6,4},{7,31},{8,14},{9,1},{... | collective-permute-start | bytes 442376 | tf_op jit(solution)/shard_map/ppermute | solution.py:28
  105.6 8.4 %collective-permute-start.21 = (bf16[36,4096]{1,0:T(8,128)(2,1)S(1)}, bf16[36,4096]{1,0:T(8,128)(2,1)S(1)}, u32[]{:S(2)}, u32[]{:S(2)}) collective-permute-start(bf16[36,4096]{1,0:T(8,128)(2,1)S(1)} %fusion.30), channel_id=1, source_target_pairs={{0,2},{1,9},{2,4},{3,11},{4,6},{5,13},{6,0},{7,15},{8,10},{9,17},{... | collective-permute-start | bytes 884744 | tf_op jit(solution)/shard_map/ppermute | solution.py:28
  105.9 8.1 %collective-permute-start.23 = (bf16[36,4096]{1,0:T(8,128)(2,1)S(1)}, bf16[36,4096]{1,0:T(8,128)(2,1)S(1)}, u32[]{:S(2)}, u32[]{:S(2)}) collective-permute-start(bf16[36,4096]{1,0:T(8,128)(2,1)S(1)} %fusion.27), channel_id=1, source_target_pairs={{0,6},{1,25},{2,0},{3,27},{4,2},{5,29},{6,4},{7,31},{8,14},{9,1},{... | collective-permute-start | bytes 884744 | tf_op jit(solution)/shard_map/ppermute | solution.py:28
  114.2 8.1 %collective-permute-start.24 = (bf16[12,4096]{1,0:T(8,128)(2,1)S(1)}, bf16[12,4096]{1,0:T(8,128)(2,1)S(1)}, u32[]{:S(2)}, u32[]{:S(2)}) collective-permute-start(bf16[12,4096]{1,0:T(8,128)(2,1)S(1)} %get-tuple-element.95), channel_id=1, source_target_pairs={{96,0},{97,1},{98,2},{99,3},{100,4},{101,5},{102,6},{103,7},{104,8... | collective-permute-start | bytes 294920 | tf_op jit(solution)/shard_map/ppermute | solution.py:36
  115.5 6.8 %collective-permute-start.25 = (bf16[12,4096]{1,0:T(8,128)(2,1)S(1)}, bf16[12,4096]{1,0:T(8,128)(2,1)S(1)}, u32[]{:S(2)}, u32[]{:S(2)}) collective-permute-start(bf16[12,4096]{1,0:T(8,128)(2,1)S(1)} %get-tuple-element.93), channel_id=1, source_target_pairs={{96,32},{97,33},{98,34},{99,35},{100,36},{101,37},{102,38},{103,39... | collective-permute-start | bytes 294920 | tf_op jit(solution)/shard_map/ppermute | solution.py:36
  (7 other events, 52.7 us)

commit v9 on v6

--- a/solution.py
+++ b/solution.py
@@ -158,7 +158,13 @@
     return [pltpu.VMEM(shape, down.dtype) for shape in shapes]
 
 
-def expert_kernel(pieces, columns, load, *refs):
+def expert_kernel(pieces, columns, load, serving, *refs):
+    @pl.when(serving[0] > 0)
+    def _():
+        expert_rows(pieces, columns, load, *refs)
+
+
+def expert_rows(pieces, columns, load, *refs):
     refs = list(refs)
     pick = refs.pop(0)
     rows_in = [refs.pop(0) for _ in range(pieces)]
@@ -210,7 +216,7 @@
             start += out.shape[0]
 
 
-def experts_on(pieces, pick, halves):
+def experts_on(pieces, serving, pick, halves):
     inner, width = halves[0][-1].shape
     load = len(halves[0]) == 2
     sizes = [piece.shape[0] for piece in pieces]
@@ -222,7 +228,7 @@
     kept = [shape for half in halves for shape in kept_shapes(*half)] if load else []
     outs = pl.pallas_call(
         functools.partial(expert_kernel, len(pieces), 1024, load),
-        in_specs=[whole] * (1 + len(pieces)) + [space] * len(held),
+        in_specs=[pl.BlockSpec(memory_space=pltpu.SMEM)] + [whole] * (1 + len(pieces)) + [space] * len(held),
         out_specs=[whole] * (len(sizes) + len(kept)),
         out_shape=[jax.ShapeDtypeStruct((size, width), jnp.bfloat16) for size in sizes] + kept,
         scratch_shapes=[
@@ -237,7 +243,7 @@
             bytes_accessed=12 * width * inner if load else 4 * count * width,
             transcendentals=2 * count * inner,
         ),
-    )(pick, *(pltpu.with_memory_space_constraint(w, pltpu.VMEM) for w in pieces), *held)
+    )(serving, pick, *(pltpu.with_memory_space_constraint(w, pltpu.VMEM) for w in pieces), *held)
     kept = outs[len(sizes) :]
     return outs[: len(sizes)], (kept[:3], kept[3:]) if load else halves
 
@@ -270,22 +276,23 @@
     before_b, after_a = step_v(group_b, 1), step_v(group_a, -1)
     column = lax.broadcasted_iota(jnp.int32, (1, EXTRA), 1)
     pick = ((column % experts == expert) & (column < 3 * experts)).astype(f32)
-    (own_a, own_b), halves = experts_on([group_a, group_b], pick, halves)
+    serving = expert_side.astype(jnp.int32).reshape(1)
+    (own_a, own_b), halves = experts_on([group_a, group_b], serving, pick, halves)
 
     before_a, after_b, before_b, after_a, own_a, own_b = lax.optimization_barrier(
         (before_a, after_b, before_b, after_a, own_a, own_b)
     )
     across_a, across_b = step_v(before_a, 1), step_v(after_b, -1)
-    (after_b, before_a), _ = experts_on([after_b, before_a], pick, halves)
+    (after_b, before_a), _ = experts_on([after_b, before_a], serving, pick, halves)
     across_a, across_b, after_b, before_a = lax.optimization_barrier((across_a, across_b, after_b, before_a))
 
     from_after_b, from_before_a = step_v(after_b, 1), step_v(before_a, -1)
-    (cross_a, cross_b), _ = experts_on([across_a, across_b], pick, halves)
+    (cross_a, cross_b), _ = experts_on([across_a, across_b], serving, pick, halves)
     from_cross_a, from_cross_b = step_v(cross_a, 1), step_v(cross_b, -1)
     after_a, before_b, from_after_b, from_before_a, cross_a = lax.optimization_barrier(
         (after_a, before_b, from_after_b, from_before_a, cross_a)
     )
-    (after_a, before_b), _ = experts_on([after_a, before_b], pick, halves)
+    (after_a, before_b), _ = experts_on([after_a, before_b], serving, pick, halves)
 
     query, _ = lax.optimization_barrier((query, cross_a))
     attention_out = lax.cond(

time: 120 us -> 119 us (level)
  waiting for transfers between devices: 34.2 us -> 69.6 us
  Pallas kernels: 35.9 us -> 2.11 us
  local copies, waits for them, and re-layouts: 3.01 us -> 0.82 us
    pallas_call x4, Pallas kernels: 34.9 us -> 1.15 us  [experts_on(): pl.pallas_call(functools.partial(expert_kernel, len(pieces), 1024, load),...]
    ppermute x12, waiting for transfers between devices: 14.1 us -> 43.4 us  [step_v(): return lax.ppermute(block, 'dev', along(False, distance))]
    ppermute x6, waiting for transfers between devices: 5.51 us -> 11.4 us  [to_section(): return lax.ppermute(block, 'sec', [(source, target)])]
    another operation x1, local copies, waits for them, and re-layouts: 2.74 us -> 0.54 us
  transfers between devices with their start and end apart: 27 -> 27, of which waited for: 11 -> 13; matrix products, arithmetic and copies ran while one was open for 5% -> 3% of each run, Pallas kernels for 30% -> 2%
where the time goes in v9:
time: 119 us; the launch traced here: 118 us
  waiting for transfers between devices  69.6 us (58%)
  starting transfers between devices  40.4 us (34%)
  other arithmetic  2.33 us (2%)
  Pallas kernels  2.11 us (2%)
  matrix products  1.33 us (1%)
    ppermute x12, waiting for transfers between devices, step_v(): return lax.ppermute(block, 'dev', along(False, distance))  43.4 us
    ppermute x12, starting transfers between devices, step_v(): return lax.ppermute(block, 'dev', along(False, distance))  19 us
    ppermute x7, waiting for transfers between devices, step_u(): return lax.ppermute(block, 'dev', along(True, distance))  14.7 us
    ppermute x7, starting transfers between devices, step_u(): return lax.ppermute(block, 'dev', along(True, distance))  11.8 us
    ppermute x6, waiting for transfers between devices, to_section(): return lax.ppermute(block, 'sec', [(source, target)])  11.4 us
    ppermute x6, starting transfers between devices, to_section(): return lax.ppermute(block, 'sec', [(source, target)])  8.98 us
  transfers between devices with their start and end apart: 27, of which 13 were waited for; matrix products, arithmetic and copies ran while one was open for 3% of the time, Pallas kernels for 2%

profile of v9, /device:TPU:0, one launch (start us, length us, event | category | flops | bytes accessed | tf_op | source)
XLA Modules:
  0.0 117.5 jit_solution(13399997814098710027)
XLA Ops:
  2.2 5.0 %collective-permute-start = (bf16[12,4224]{1,0:T(8,128)(2,1)S(1)}, bf16[12,4224]{1,0:T(8,128)(2,1)S(1)}, u32[]{:S(2)}, u32[]{:S(2)}) collective-permute-start(bf16[12,4224]{1,0:T(8,128)(2,1)S(1)} %shard_map.107), channel_id=1, source_target_pairs={{0,96},{1,97},{2,98},{3,99},{4,100},{5,101},{6,102},{7,103},{8,104... | collective-permute-start | bytes 304136 | tf_op jit(solution)/shard_map/ppermute | solution.py:36
  8.6 4.7 %collective-permute-done = bf16[12,4224]{1,0:T(8,128)(2,1)S(1)} collective-permute-done((bf16[12,4224]{1,0:T(8,128)(2,1)S(1)}, bf16[12,4224]{1,0:T(8,128)(2,1)S(1)}, u32[]{:S(2)}, u32[]{:S(2)}) %collective-permute-start) | collective-permute-done | bytes 101408 | tf_op jit(solution)/shard_map/ppermute | solution.py:36
  13.3 2.8 %collective-permute-start.4 = (bf16[36,4224]{1,0:T(8,128)(2,1)S(1)}, bf16[36,4224]{1,0:T(8,128)(2,1)S(1)}, u32[]{:S(2)}, u32[]{:S(2)}) collective-permute-start(bf16[36,4224]{1,0:T(8,128)(2,1)S(1)} %pad_maximum_fusion), channel_id=1, source_target_pairs={{0,6},{1,25},{2,0},{3,27},{4,2},{5,29},{6,4},{7,31},{8,14},{9,1},{... | collective-permute-start | bytes 912392 | tf_op jit(solution)/shard_map/ppermute | solution.py:28
  16.1 2.3 %collective-permute-start.6 = (bf16[36,4224]{1,0:T(8,128)(2,1)S(1)}, bf16[36,4224]{1,0:T(8,128)(2,1)S(1)}, u32[]{:S(2)}, u32[]{:S(2)}) collective-permute-start(bf16[36,4224]{1,0:T(8,128)(2,1)S(1)} %pad_maximum_fusion), channel_id=1, source_target_pairs={{0,4},{1,17},{2,6},{3,19},{4,0},{5,21},{6,2},{7,23},{8,12},{9,25},... | collective-permute-start | bytes 912392 | tf_op jit(solution)/shard_map/ppermute | solution.py:28
  18.4 2.5 %collective-permute-done.4 = bf16[36,4224]{1,0:T(8,128)(2,1)S(1)} collective-permute-done((bf16[36,4224]{1,0:T(8,128)(2,1)S(1)}, bf16[36,4224]{1,0:T(8,128)(2,1)S(1)}, u32[]{:S(2)}, u32[]{:S(2)}) %collective-permute-start.4) | collective-permute-done | bytes 304160 | tf_op jit(solution)/shard_map/ppermute | solution.py:28
  21.0 7.2 %collective-permute-done.3 = bf16[36,4224]{1,0:T(8,128)(2,1)S(1)} collective-permute-done((bf16[36,4224]{1,0:T(8,128)(2,1)S(1)}, bf16[36,4224]{1,0:T(8,128)(2,1)S(1)}, u32[]{:S(2)}, u32[]{:S(2)}) %collective-permute-start.3) | collective-permute-done | bytes 304160 | tf_op jit(solution)/shard_map/ppermute | solution.py:28
  28.3 3.8 %collective-permute-start.5 = (bf16[80,4224]{1,0:T(8,128)(2,1)S(1)}, bf16[80,4224]{1,0:T(8,128)(2,1)S(1)}, u32[]{:S(2)}, u32[]{:S(2)}) collective-permute-start(bf16[80,4224]{1,0:T(8,128)(2,1)S(1)} %pad_add_fusion.refs_1_), channel_id=1, source_target_pairs={{0,8},{1,3},{2,10},{3,5},{4,12},{5,7},{6,14},{7,1},{8,16},{9,11},{... | collective-permute-start | bytes 2027528 | tf_op jit(solution)/shard_map/ppermute | solution.py:32
  33.4 2.0 %collective-permute-start.7 = (bf16[64,4224]{1,0:T(8,128)(2,1)S(1)}, bf16[64,4224]{1,0:T(8,128)(2,1)}, u32[]{:S(2)}, u32[]{:S(2)}) collective-permute-start(bf16[64,4224]{1,0:T(8,128)(2,1)S(1)} %pad_add_fusion.1.refs_2_), channel_id=1, source_target_pairs={{0,24},{1,7},{2,26},{3,1},{4,28},{5,3},{6,30},{7,5},{8,0},{9,15},{... | collective-permute-start | bytes 1622024 | tf_op jit(solution)/shard_map/ppermute | solution.py:32
  35.6 13.2 %collective-permute-done.7.refs_1_ = bf16[64,4224]{1,0:T(8,128)(2,1)} collective-permute-done((bf16[64,4224]{1,0:T(8,128)(2,1)S(1)}, bf16[64,4224]{1,0:T(8,128)(2,1)}, u32[]{:S(2)}, u32[]{:S(2)}) %collective-permute-start.7) | collective-permute-done | bytes 540704 | tf_op jit(solution)/shard_map/ppermute | solution.py:32
  48.8 1.9 %collective-permute-start.12 = (bf16[80,4224]{1,0:T(8,128)(2,1)S(1)}, bf16[80,4224]{1,0:T(8,128)(2,1)S(1)}, u32[]{:S(2)}, u32[]{:S(2)}) collective-permute-start(bf16[80,4224]{1,0:T(8,128)(2,1)S(1)} %collective-permute-done.5.refs_2_), channel_id=1, source_target_pairs={{0,8},{1,3},{2,10},{3,5},{4,12},{5,7},{6,14},{7,1},{8,16},{9,11},{... | collective-permute-start | bytes 2027528 | tf_op jit(solution)/shard_map/ppermute | solution.py:32
  50.6 1.4 %collective-permute-start.13 = (bf16[64,4224]{1,0:T(8,128)(2,1)}, bf16[64,4224]{1,0:T(8,128)(2,1)S(1)}, u32[]{:S(2)}, u32[]{:S(2)}) collective-permute-start(bf16[64,4224]{1,0:T(8,128)(2,1)} %collective-permute-done.7.refs_1_), channel_id=1, source_target_pairs={{0,24},{1,7},{2,26},{3,1},{4,28},{5,3},{6,30},{7,5},{8,0},{9,15},{... | collective-permute-start | bytes 1622024 | tf_op jit(solution)/shard_map/ppermute | solution.py:32
  53.2 7.0 %collective-permute-done.13.refs_2_ = bf16[64,4224]{1,0:T(8,128)(2,1)S(1)} collective-permute-done((bf16[64,4224]{1,0:T(8,128)(2,1)}, bf16[64,4224]{1,0:T(8,128)(2,1)S(1)}, u32[]{:S(2)}, u32[]{:S(2)}) %collective-permute-start.13) | collective-permute-done | bytes 540704 | tf_op jit(solution)/shard_map/ppermute | solution.py:32
  60.9 2.0 %collective-permute-start.15 = (bf16[80,4096]{1,0:T(8,128)(2,1)S(1)}, bf16[80,4096]{1,0:T(8,128)(2,1)S(1)}, u32[]{:S(2)}, u32[]{:S(2)}) collective-permute-start(bf16[80,4096]{1,0:T(8,128)(2,1)S(1)} %get-tuple-element.61), channel_id=1, source_target_pairs={{0,24},{1,7},{2,26},{3,1},{4,28},{5,3},{6,30},{7,5},{8,0},{9,15},{... | collective-permute-start | bytes 1966088 | tf_op jit(solution)/shard_map/ppermute | solution.py:32
  62.9 3.2 %collective-permute-start.18 = (bf16[64,4096]{1,0:T(8,128)(2,1)S(1)}, bf16[64,4096]{1,0:T(8,128)(2,1)S(1)}, u32[]{:S(2)}, u32[]{:S(2)}) collective-permute-start(bf16[64,4096]{1,0:T(8,128)(2,1)S(1)} %get-tuple-element.72), channel_id=1, source_target_pairs={{0,24},{1,7},{2,26},{3,1},{4,28},{5,3},{6,30},{7,5},{8,0},{9,15},{... | collective-permute-start | bytes 1572872 | tf_op jit(solution)/shard_map/ppermute | solution.py:32
  66.1 7.2 %collective-permute-done.14 = bf16[64,4096]{1,0:T(8,128)(2,1)S(1)} collective-permute-done((bf16[64,4096]{1,0:T(8,128)(2,1)S(1)}, bf16[64,4096]{1,0:T(8,128)(2,1)S(1)}, u32[]{:S(2)}, u32[]{:S(2)}) %collective-permute-start.14) | collective-permute-done | bytes 524320 | tf_op jit(solution)/shard_map/ppermute | solution.py:32
  73.3 3.8 %collective-permute-done.18 = bf16[64,4096]{1,0:T(8,128)(2,1)S(1)} collective-permute-done((bf16[64,4096]{1,0:T(8,128)(2,1)S(1)}, bf16[64,4096]{1,0:T(8,128)(2,1)S(1)}, u32[]{:S(2)}, u32[]{:S(2)}) %collective-permute-start.18) | collective-permute-done | bytes 524320 | tf_op jit(solution)/shard_map/ppermute | solution.py:32
  77.2 3.3 %collective-permute-start.19 = (bf16[64,4096]{1,0:T(8,128)(2,1)S(1)}, bf16[64,4096]{1,0:T(8,128)(2,1)S(1)}, u32[]{:S(2)}, u32[]{:S(2)}) collective-permute-start(bf16[64,4096]{1,0:T(8,128)(2,1)S(1)} %add_convert_fusion.1), channel_id=1, source_target_pairs={{0,24},{1,7},{2,26},{3,1},{4,28},{5,3},{6,30},{7,5},{8,0},{9,15},{... | collective-permute-start | bytes 1572872 | tf_op jit(solution)/shard_map/ppermute | solution.py:32
  80.7 8.5 %collective-permute-done.19 = bf16[64,4096]{1,0:T(8,128)(2,1)S(1)} collective-permute-done((bf16[64,4096]{1,0:T(8,128)(2,1)S(1)}, bf16[64,4096]{1,0:T(8,128)(2,1)S(1)}, u32[]{:S(2)}, u32[]{:S(2)}) %collective-permute-start.19) | collective-permute-done | bytes 524320 | tf_op jit(solution)/shard_map/ppermute | solution.py:32
  89.6 3.3 %collective-permute-start.22 = (bf16[18,4096]{1,0:T(8,128)(2,1)S(1)}, bf16[18,4096]{1,0:T(8,128)(2,1)S(1)}, u32[]{:S(2)}, u32[]{:S(2)}) collective-permute-start(bf16[18,4096]{1,0:T(8,128)(2,1)S(1)} %get-tuple-element.92), channel_id=1, source_target_pairs={{0,6},{1,25},{2,0},{3,27},{4,2},{5,29},{6,4},{7,31},{8,14},{9,1},{... | collective-permute-start | bytes 442376 | tf_op jit(solution)/shard_map/ppermute | solution.py:28
  92.9 3.1 %collective-permute-done.17 = bf16[80,4096]{1,0:T(8,128)(2,1)S(1)} collective-permute-done((bf16[80,4096]{1,0:T(8,128)(2,1)S(1)}, bf16[80,4096]{1,0:T(8,128)(2,1)S(1)}, u32[]{:S(2)}, u32[]{:S(2)}) %collective-permute-start.17) | collective-permute-done | bytes 655392 | tf_op jit(solution)/shard_map/ppermute | solution.py:32
  96.7 3.3 %collective-permute-start.23 = (bf16[36,4096]{1,0:T(8,128)(2,1)S(1)}, bf16[36,4096]{1,0:T(8,128)(2,1)S(1)}, u32[]{:S(2)}, u32[]{:S(2)}) collective-permute-start(bf16[36,4096]{1,0:T(8,128)(2,1)S(1)} %fusion.27), channel_id=1, source_target_pairs={{0,6},{1,25},{2,0},{3,27},{4,2},{5,29},{6,4},{7,31},{8,14},{9,1},{... | collective-permute-start | bytes 884744 | tf_op jit(solution)/shard_map/ppermute | solution.py:28
  100.0 4.9 %collective-permute-done.21 = bf16[36,4096]{1,0:T(8,128)(2,1)S(1)} collective-permute-done((bf16[36,4096]{1,0:T(8,128)(2,1)S(1)}, bf16[36,4096]{1,0:T(8,128)(2,1)S(1)}, u32[]{:S(2)}, u32[]{:S(2)}) %collective-permute-start.21) | collective-permute-done | bytes 294944 | tf_op jit(solution)/shard_map/ppermute | solution.py:28
  107.7 2.3 %conditional.1 = (bf16[2,8192]{1,0:T(2,128)(2,1)S(1)}) conditional(s32[]{:T(128)} %convert_element_type.90, (s32[2]{0:T(128)S(1)}, bf16[2,8192]{1,0:T(2,128)(2,1)S(1)}, bf16[2,1024,4,256]{3,2,1,0:T(4,128)(2,1)S(1)}, bf16[2,4,256]{2,1,0:T(4,128)(2,1)S(1)}) %tuple.37, () %tuple.19), branch_computations={%region_0.3_spmd, %region_3.4_spmd} | conditional | flops 68128512 | bytes 14426640 | solution.py:298
  110.1 6.8 %collective-permute-done.24 = bf16[12,4096]{1,0:T(8,128)(2,1)S(1)} collective-permute-done((bf16[12,4096]{1,0:T(8,128)(2,1)S(1)}, bf16[12,4096]{1,0:T(8,128)(2,1)S(1)}, u32[]{:S(2)}, u32[]{:S(2)}) %collective-permute-start.24) | collective-permute-done | bytes 98336 | tf_op jit(solution)/shard_map/ppermute | solution.py:36
  (76 shorter events, 13.5 us)
Async XLA Ops:
  0.6 34.9 %collective-permute-start.10 = (bf16[4096,1536]{1,0:T(8,128)(2,1)}, bf16[4096,1536]{1,0:T(8,128)(2,1)}, u32[]{:S(2)}, u32[]{:S(2)}) collective-permute-start(bf16[4096,1536]{1,0:T(8,128)(2,1)} %bitcast.19), channel_id=1, source_target_pairs={{0,1},{1,0},{2,3},{3,2},{4,5},{5,4},{6,7},{7,6},{8,9},{9,8},{10,11... | collective-permute-start | bytes 37748744 | tf_op jit(solution)/shard_map/ppermute | solution.py:51
  0.7 34.7 %collective-permute-start.11 = (bf16[768,4096]{1,0:T(8,128)(2,1)}, bf16[768,4096]{1,0:T(8,128)(2,1)}, u32[]{:S(2)}, u32[]{:S(2)}) collective-permute-start(bf16[768,4096]{1,0:T(8,128)(2,1)} %bitcast.21), channel_id=1, source_target_pairs={{0,1},{1,0},{2,3},{3,2},{4,5},{5,4},{6,7},{7,6},{8,9},{9,8},{10,11... | collective-permute-start | bytes 18874376 | tf_op jit(solution)/shard_map/ppermute | solution.py:51
  2.2 11.0 %collective-permute-start = (bf16[12,4224]{1,0:T(8,128)(2,1)S(1)}, bf16[12,4224]{1,0:T(8,128)(2,1)S(1)}, u32[]{:S(2)}, u32[]{:S(2)}) collective-permute-start(bf16[12,4224]{1,0:T(8,128)(2,1)S(1)} %shard_map.107), channel_id=1, source_target_pairs={{0,96},{1,97},{2,98},{3,99},{4,100},{5,101},{6,102},{7,103},{8,104... | collective-permute-start | bytes 304136 | tf_op jit(solution)/shard_map/ppermute | solution.py:36
  13.3 7.7 %collective-permute-start.4 = (bf16[36,4224]{1,0:T(8,128)(2,1)S(1)}, bf16[36,4224]{1,0:T(8,128)(2,1)S(1)}, u32[]{:S(2)}, u32[]{:S(2)}) collective-permute-start(bf16[36,4224]{1,0:T(8,128)(2,1)S(1)} %pad_maximum_fusion), channel_id=1, source_target_pairs={{0,6},{1,25},{2,0},{3,27},{4,2},{5,29},{6,4},{7,31},{8,14},{9,1},{... | collective-permute-start | bytes 912392 | tf_op jit(solution)/shard_map/ppermute | solution.py:28
  16.1 12.0 %collective-permute-start.3 = (bf16[36,4224]{1,0:T(8,128)(2,1)S(1)}, bf16[36,4224]{1,0:T(8,128)(2,1)S(1)}, u32[]{:S(2)}, u32[]{:S(2)}) collective-permute-start(bf16[36,4224]{1,0:T(8,128)(2,1)S(1)} %pad_maximum_fusion), channel_id=1, source_target_pairs={{0,2},{1,9},{2,4},{3,11},{4,6},{5,13},{6,0},{7,15},{8,10},{9,17},{... | collective-permute-start | bytes 912392 | tf_op jit(solution)/shard_map/ppermute | solution.py:28
  16.1 17.1 %collective-permute-start.6 = (bf16[36,4224]{1,0:T(8,128)(2,1)S(1)}, bf16[36,4224]{1,0:T(8,128)(2,1)S(1)}, u32[]{:S(2)}, u32[]{:S(2)}) collective-permute-start(bf16[36,4224]{1,0:T(8,128)(2,1)S(1)} %pad_maximum_fusion), channel_id=1, source_target_pairs={{0,4},{1,17},{2,6},{3,19},{4,0},{5,21},{6,2},{7,23},{8,12},{9,25},... | collective-permute-start | bytes 912392 | tf_op jit(solution)/shard_map/ppermute | solution.py:28
  28.3 20.5 %collective-permute-start.5 = (bf16[80,4224]{1,0:T(8,128)(2,1)S(1)}, bf16[80,4224]{1,0:T(8,128)(2,1)S(1)}, u32[]{:S(2)}, u32[]{:S(2)}) collective-permute-start(bf16[80,4224]{1,0:T(8,128)(2,1)S(1)} %pad_add_fusion.refs_1_), channel_id=1, source_target_pairs={{0,8},{1,3},{2,10},{3,5},{4,12},{5,7},{6,14},{7,1},{8,16},{9,11},{... | collective-permute-start | bytes 2027528 | tf_op jit(solution)/shard_map/ppermute | solution.py:32
  32.1 16.7 %collective-permute-start.9 = (bf16[80,4224]{1,0:T(8,128)(2,1)S(1)}, bf16[80,4224]{1,0:T(8,128)(2,1)S(1)}, u32[]{:S(2)}, u32[]{:S(2)}) collective-permute-start(bf16[80,4224]{1,0:T(8,128)(2,1)S(1)} %pad_add_fusion.refs_1_), channel_id=1, source_target_pairs={{0,24},{1,7},{2,26},{3,1},{4,28},{5,3},{6,30},{7,5},{8,0},{9,15},{... | collective-permute-start | bytes 2027528 | tf_op jit(solution)/shard_map/ppermute | solution.py:32
  33.4 15.4 %collective-permute-start.7 = (bf16[64,4224]{1,0:T(8,128)(2,1)S(1)}, bf16[64,4224]{1,0:T(8,128)(2,1)}, u32[]{:S(2)}, u32[]{:S(2)}) collective-permute-start(bf16[64,4224]{1,0:T(8,128)(2,1)S(1)} %pad_add_fusion.1.refs_2_), channel_id=1, source_target_pairs={{0,24},{1,7},{2,26},{3,1},{4,28},{5,3},{6,30},{7,5},{8,0},{9,15},{... | collective-permute-start | bytes 1622024 | tf_op jit(solution)/shard_map/ppermute | solution.py:32
  35.4 13.4 %collective-permute-start.8 = (bf16[64,4224]{1,0:T(8,128)(2,1)S(1)}, bf16[64,4224]{1,0:T(8,128)(2,1)S(1)}, u32[]{:S(2)}, u32[]{:S(2)}) collective-permute-start(bf16[64,4224]{1,0:T(8,128)(2,1)S(1)} %pad_add_fusion.1.refs_2_), channel_id=1, source_target_pairs={{0,8},{1,3},{2,10},{3,5},{4,12},{5,7},{6,14},{7,1},{8,16},{9,11},{... | collective-permute-start | bytes 1622024 | tf_op jit(solution)/shard_map/ppermute | solution.py:32
  48.8 12.1 %collective-permute-start.12 = (bf16[80,4224]{1,0:T(8,128)(2,1)S(1)}, bf16[80,4224]{1,0:T(8,128)(2,1)S(1)}, u32[]{:S(2)}, u32[]{:S(2)}) collective-permute-start(bf16[80,4224]{1,0:T(8,128)(2,1)S(1)} %collective-permute-done.5.refs_2_), channel_id=1, source_target_pairs={{0,8},{1,3},{2,10},{3,5},{4,12},{5,7},{6,14},{7,1},{8,16},{9,11},{... | collective-permute-start | bytes 2027528 | tf_op jit(solution)/shard_map/ppermute | solution.py:32
  50.6 9.6 %collective-permute-start.13 = (bf16[64,4224]{1,0:T(8,128)(2,1)}, bf16[64,4224]{1,0:T(8,128)(2,1)S(1)}, u32[]{:S(2)}, u32[]{:S(2)}) collective-permute-start(bf16[64,4224]{1,0:T(8,128)(2,1)} %collective-permute-done.7.refs_1_), channel_id=1, source_target_pairs={{0,24},{1,7},{2,26},{3,1},{4,28},{5,3},{6,30},{7,5},{8,0},{9,15},{... | collective-permute-start | bytes 1622024 | tf_op jit(solution)/shard_map/ppermute | solution.py:32
  60.9 12.4 %collective-permute-start.15 = (bf16[80,4096]{1,0:T(8,128)(2,1)S(1)}, bf16[80,4096]{1,0:T(8,128)(2,1)S(1)}, u32[]{:S(2)}, u32[]{:S(2)}) collective-permute-start(bf16[80,4096]{1,0:T(8,128)(2,1)S(1)} %get-tuple-element.61), channel_id=1, source_target_pairs={{0,24},{1,7},{2,26},{3,1},{4,28},{5,3},{6,30},{7,5},{8,0},{9,15},{... | collective-permute-start | bytes 1966088 | tf_op jit(solution)/shard_map/ppermute | solution.py:32
  62.9 10.4 %collective-permute-start.14 = (bf16[64,4096]{1,0:T(8,128)(2,1)S(1)}, bf16[64,4096]{1,0:T(8,128)(2,1)S(1)}, u32[]{:S(2)}, u32[]{:S(2)}) collective-permute-start(bf16[64,4096]{1,0:T(8,128)(2,1)S(1)} %get-tuple-element.60), channel_id=1, source_target_pairs={{0,8},{1,3},{2,10},{3,5},{4,12},{5,7},{6,14},{7,1},{8,16},{9,11},{... | collective-permute-start | bytes 1572872 | tf_op jit(solution)/shard_map/ppermute | solution.py:32
  62.9 14.2 %collective-permute-start.18 = (bf16[64,4096]{1,0:T(8,128)(2,1)S(1)}, bf16[64,4096]{1,0:T(8,128)(2,1)S(1)}, u32[]{:S(2)}, u32[]{:S(2)}) collective-permute-start(bf16[64,4096]{1,0:T(8,128)(2,1)S(1)} %get-tuple-element.72), channel_id=1, source_target_pairs={{0,24},{1,7},{2,26},{3,1},{4,28},{5,3},{6,30},{7,5},{8,0},{9,15},{... | collective-permute-start | bytes 1572872 | tf_op jit(solution)/shard_map/ppermute | solution.py:32
  66.1 14.4 %collective-permute-start.16 = (bf16[80,4096]{1,0:T(8,128)(2,1)S(1)}, bf16[80,4096]{1,0:T(8,128)(2,1)S(1)}, u32[]{:S(2)}, u32[]{:S(2)}) collective-permute-start(bf16[80,4096]{1,0:T(8,128)(2,1)S(1)} %get-tuple-element.64), channel_id=1, source_target_pairs={{0,8},{1,3},{2,10},{3,5},{4,12},{5,7},{6,14},{7,1},{8,16},{9,11},{... | collective-permute-start | bytes 1966088 | tf_op jit(solution)/shard_map/ppermute | solution.py:32
  77.2 12.0 %collective-permute-start.19 = (bf16[64,4096]{1,0:T(8,128)(2,1)S(1)}, bf16[64,4096]{1,0:T(8,128)(2,1)S(1)}, u32[]{:S(2)}, u32[]{:S(2)}) collective-permute-start(bf16[64,4096]{1,0:T(8,128)(2,1)S(1)} %add_convert_fusion.1), channel_id=1, source_target_pairs={{0,24},{1,7},{2,26},{3,1},{4,28},{5,3},{6,30},{7,5},{8,0},{9,15},{... | collective-permute-start | bytes 1572872 | tf_op jit(solution)/shard_map/ppermute | solution.py:32
  80.6 15.4 %collective-permute-start.17 = (bf16[80,4096]{1,0:T(8,128)(2,1)S(1)}, bf16[80,4096]{1,0:T(8,128)(2,1)S(1)}, u32[]{:S(2)}, u32[]{:S(2)}) collective-permute-start(bf16[80,4096]{1,0:T(8,128)(2,1)S(1)} %add_convert_fusion), channel_id=1, source_target_pairs={{0,8},{1,3},{2,10},{3,5},{4,12},{5,7},{6,14},{7,1},{8,16},{9,11},{... | collective-permute-start | bytes 1966088 | tf_op jit(solution)/shard_map/ppermute | solution.py:32
  89.6 7.0 %collective-permute-start.22 = (bf16[18,4096]{1,0:T(8,128)(2,1)S(1)}, bf16[18,4096]{1,0:T(8,128)(2,1)S(1)}, u32[]{:S(2)}, u32[]{:S(2)}) collective-permute-start(bf16[18,4096]{1,0:T(8,128)(2,1)S(1)} %get-tuple-element.92), channel_id=1, source_target_pairs={{0,6},{1,25},{2,0},{3,27},{4,2},{5,29},{6,4},{7,31},{8,14},{9,1},{... | collective-permute-start | bytes 442376 | tf_op jit(solution)/shard_map/ppermute | solution.py:28
  96.5 8.4 %collective-permute-start.21 = (bf16[36,4096]{1,0:T(8,128)(2,1)S(1)}, bf16[36,4096]{1,0:T(8,128)(2,1)S(1)}, u32[]{:S(2)}, u32[]{:S(2)}) collective-permute-start(bf16[36,4096]{1,0:T(8,128)(2,1)S(1)} %fusion.30), channel_id=1, source_target_pairs={{0,2},{1,9},{2,4},{3,11},{4,6},{5,13},{6,0},{7,15},{8,10},{9,17},{... | collective-permute-start | bytes 884744 | tf_op jit(solution)/shard_map/ppermute | solution.py:28
  96.7 8.1 %collective-permute-start.23 = (bf16[36,4096]{1,0:T(8,128)(2,1)S(1)}, bf16[36,4096]{1,0:T(8,128)(2,1)S(1)}, u32[]{:S(2)}, u32[]{:S(2)}) collective-permute-start(bf16[36,4096]{1,0:T(8,128)(2,1)S(1)} %fusion.27), channel_id=1, source_target_pairs={{0,6},{1,25},{2,0},{3,27},{4,2},{5,29},{6,4},{7,31},{8,14},{9,1},{... | collective-permute-start | bytes 884744 | tf_op jit(solution)/shard_map/ppermute | solution.py:28
  105.1 11.8 %collective-permute-start.24 = (bf16[12,4096]{1,0:T(8,128)(2,1)S(1)}, bf16[12,4096]{1,0:T(8,128)(2,1)S(1)}, u32[]{:S(2)}, u32[]{:S(2)}) collective-permute-start(bf16[12,4096]{1,0:T(8,128)(2,1)S(1)} %get-tuple-element.95), channel_id=1, source_target_pairs={{96,0},{97,1},{98,2},{99,3},{100,4},{101,5},{102,6},{103,7},{104,8... | collective-permute-start | bytes 294920 | tf_op jit(solution)/shard_map/ppermute | solution.py:36
  106.4 10.5 %collective-permute-start.25 = (bf16[12,4096]{1,0:T(8,128)(2,1)S(1)}, bf16[12,4096]{1,0:T(8,128)(2,1)S(1)}, u32[]{:S(2)}, u32[]{:S(2)}) collective-permute-start(bf16[12,4096]{1,0:T(8,128)(2,1)S(1)} %get-tuple-element.93), channel_id=1, source_target_pairs={{96,32},{97,33},{98,34},{99,35},{100,36},{101,37},{102,38},{103,39... | collective-permute-start | bytes 294920 | tf_op jit(solution)/shard_map/ppermute | solution.py:36
  107.0 9.8 %collective-permute-start.26 = (bf16[12,4096]{1,0:T(8,128)(2,1)S(1)}, bf16[12,4096]{1,0:T(8,128)(2,1)S(1)}, u32[]{:S(2)}, u32[]{:S(2)}) collective-permute-start(bf16[12,4096]{1,0:T(8,128)(2,1)S(1)} %get-tuple-element.94), channel_id=1, source_target_pairs={{96,64},{97,65},{98,66},{99,67},{100,68},{101,69},{102,70},{103,71... | collective-permute-start | bytes 294920 | tf_op jit(solution)/shard_map/ppermute | solution.py:36
  (8 other events, 70.7 us)

commit v10 on v9

--- a/solution.py
+++ b/solution.py
@@ -270,7 +270,9 @@
     size = SIDE * held
     cut = 16 * ((size // 2 + 15) // 16)
     lead = cut - 2 * held
-    behind, ahead, far = step_u(block, 1), step_u(block, -1), step_u(block, 2)
+    behind, ahead = step_u(block, 1), step_u(block, -1)
+    block, behind, ahead = lax.optimization_barrier((block, behind, ahead))
+    far = step_u(block, 2)
     group_a, group_b = stacked([block, behind, ahead[:lead]]), stacked([ahead[lead:], far])
     before_a, after_b = step_v(group_a, 1), step_v(group_b, -1)
     before_b, after_a = step_v(group_b, 1), step_v(group_a, -1)

time: 119 us -> 124 us (1.042)
  waiting for transfers between devices: 69.6 us -> 72.7 us
  starting transfers between devices: 40.4 us -> 42.6 us
    ppermute x6, waiting for transfers between devices: 11.4 us -> 15.1 us  [to_section(): return lax.ppermute(block, 'sec', [(source, target)])]
    ppermute x12, waiting for transfers between devices: 43.4 us -> 40.4 us  [step_v(): return lax.ppermute(block, 'dev', along(False, distance))]
    ppermute x7, waiting for transfers between devices: 14.7 us -> 17.1 us  [step_u(): return lax.ppermute(block, 'dev', along(True, distance))]
    ppermute x7, starting transfers between devices: 11.8 us -> 13.5 us  [step_u(): return lax.ppermute(block, 'dev', along(True, distance))]
  transfers between devices with their start and end apart: 27 -> 27, of which waited for: 13 -> 17; matrix products, arithmetic and copies ran while one was open for 3% -> 3% of each run, Pallas kernels for 2% -> 2%
where the time goes in v10:
time: 124 us; the launch traced here: 123 us
  waiting for transfers between devices  72.7 us (59%)
  starting transfers between devices  42.6 us (34%)
  other arithmetic  2.34 us (2%)
  Pallas kernels  2.11 us (2%)
  matrix products  1.33 us (1%)
    ppermute x12, waiting for transfers between devices, step_v(): return lax.ppermute(block, 'dev', along(False, distance))  40.4 us
    ppermute x12, starting transfers between devices, step_v(): return lax.ppermute(block, 'dev', along(False, distance))  19.5 us
    ppermute x7, waiting for transfers between devices, step_u(): return lax.ppermute(block, 'dev', along(True, distance))  17.1 us
    ppermute x6, waiting for transfers between devices, to_section(): return lax.ppermute(block, 'sec', [(source, target)])  15.1 us
    ppermute x7, starting transfers between devices, step_u(): return lax.ppermute(block, 'dev', along(True, distance))  13.5 us
    ppermute x6, starting transfers between devices, to_section(): return lax.ppermute(block, 'sec', [(source, target)])  8.98 us
  transfers between devices with their start and end apart: 27, of which 17 were waited for; matrix products, arithmetic and copies ran while one was open for 3% of the time, Pallas kernels for 2%

profile of v10, /device:TPU:0, one launch (start us, length us, event | category | flops | bytes accessed | tf_op | source)
XLA Modules:
  0.0 122.8 jit_solution(3446334047865409569)
XLA Ops:
  2.2 5.0 %collective-permute-start = (bf16[12,4224]{1,0:T(8,128)(2,1)S(1)}, bf16[12,4224]{1,0:T(8,128)(2,1)S(1)}, u32[]{:S(2)}, u32[]{:S(2)}) collective-permute-start(bf16[12,4224]{1,0:T(8,128)(2,1)S(1)} %shard_map.107), channel_id=1, source_target_pairs={{0,96},{1,97},{2,98},{3,99},{4,100},{5,101},{6,102},{7,103},{8,104... | collective-permute-start | bytes 304136 | tf_op jit(solution)/shard_map/ppermute | solution.py:36
  8.6 4.7 %collective-permute-done = bf16[12,4224]{1,0:T(8,128)(2,1)S(1)} collective-permute-done((bf16[12,4224]{1,0:T(8,128)(2,1)S(1)}, bf16[12,4224]{1,0:T(8,128)(2,1)S(1)}, u32[]{:S(2)}, u32[]{:S(2)}) %collective-permute-start) | collective-permute-done | bytes 101408 | tf_op jit(solution)/shard_map/ppermute | solution.py:36
  16.6 5.2 %collective-permute-done.3 = bf16[36,4224]{1,0:T(8,128)(2,1)S(1)} collective-permute-done((bf16[36,4224]{1,0:T(8,128)(2,1)S(1)}, bf16[36,4224]{1,0:T(8,128)(2,1)S(1)}, u32[]{:S(2)}, u32[]{:S(2)}) %collective-permute-start.3) | collective-permute-done | bytes 304160 | tf_op jit(solution)/shard_map/ppermute | solution.py:28
  22.1 2.8 %collective-permute-start.6 = (bf16[36,4224]{1,0:T(8,128)(2,1)S(1)}, bf16[36,4224]{1,0:T(8,128)(2,1)S(1)}, u32[]{:S(2)}, u32[]{:S(2)}) collective-permute-start(bf16[36,4224]{1,0:T(8,128)(2,1)S(1)} %pad_maximum_fusion), channel_id=1, source_target_pairs={{0,4},{1,17},{2,6},{3,19},{4,0},{5,21},{6,2},{7,23},{8,12},{9,25},... | collective-permute-start | bytes 912392 | tf_op jit(solution)/shard_map/ppermute | solution.py:28
  25.0 2.0 %collective-permute-start.5 = (bf16[80,4224]{1,0:T(8,128)(2,1)S(1)}, bf16[80,4224]{1,0:T(8,128)(2,1)S(1)}, u32[]{:S(2)}, u32[]{:S(2)}) collective-permute-start(bf16[80,4224]{1,0:T(8,128)(2,1)S(1)} %pad_add_fusion.refs_1_), channel_id=1, source_target_pairs={{0,8},{1,3},{2,10},{3,5},{4,12},{5,7},{6,14},{7,1},{8,16},{9,11},{... | collective-permute-start | bytes 2027528 | tf_op jit(solution)/shard_map/ppermute | solution.py:32
  27.0 2.3 %collective-permute-start.9 = (bf16[80,4224]{1,0:T(8,128)(2,1)S(1)}, bf16[80,4224]{1,0:T(8,128)(2,1)S(1)}, u32[]{:S(2)}, u32[]{:S(2)}) collective-permute-start(bf16[80,4224]{1,0:T(8,128)(2,1)S(1)} %pad_add_fusion.refs_1_), channel_id=1, source_target_pairs={{0,24},{1,7},{2,26},{3,1},{4,28},{5,3},{6,30},{7,5},{8,0},{9,15},{... | collective-permute-start | bytes 2027528 | tf_op jit(solution)/shard_map/ppermute | solution.py:32
  29.3 5.2 %collective-permute-done.6 = bf16[36,4224]{1,0:T(8,128)(2,1)S(1)} collective-permute-done((bf16[36,4224]{1,0:T(8,128)(2,1)S(1)}, bf16[36,4224]{1,0:T(8,128)(2,1)S(1)}, u32[]{:S(2)}, u32[]{:S(2)}) %collective-permute-start.6) | collective-permute-done | bytes 304160 | tf_op jit(solution)/shard_map/ppermute | solution.py:28
  34.6 3.4 %collective-permute-start.7 = (bf16[64,4224]{1,0:T(8,128)(2,1)S(1)}, bf16[64,4224]{1,0:T(8,128)(2,1)}, u32[]{:S(2)}, u32[]{:S(2)}) collective-permute-start(bf16[64,4224]{1,0:T(8,128)(2,1)S(1)} %pad_add_fusion.1.refs_2_), channel_id=1, source_target_pairs={{0,24},{1,7},{2,26},{3,1},{4,28},{5,3},{6,30},{7,5},{8,0},{9,15},{... | collective-permute-start | bytes 1622024 | tf_op jit(solution)/shard_map/ppermute | solution.py:32
  38.3 6.6 %collective-permute-done.7.refs_1_ = bf16[64,4224]{1,0:T(8,128)(2,1)} collective-permute-done((bf16[64,4224]{1,0:T(8,128)(2,1)S(1)}, bf16[64,4224]{1,0:T(8,128)(2,1)}, u32[]{:S(2)}, u32[]{:S(2)}) %collective-permute-start.7) | collective-permute-done | bytes 540704 | tf_op jit(solution)/shard_map/ppermute | solution.py:32
  44.9 3.7 %collective-permute-done.8.refs_2_ = bf16[64,4224]{1,0:T(8,128)(2,1)S(1)} collective-permute-done((bf16[64,4224]{1,0:T(8,128)(2,1)S(1)}, bf16[64,4224]{1,0:T(8,128)(2,1)S(1)}, u32[]{:S(2)}, u32[]{:S(2)}) %collective-permute-start.8) | collective-permute-done | bytes 540704 | tf_op jit(solution)/shard_map/ppermute | solution.py:32
  48.6 3.2 %collective-permute-start.13 = (bf16[64,4224]{1,0:T(8,128)(2,1)}, bf16[64,4224]{1,0:T(8,128)(2,1)S(1)}, u32[]{:S(2)}, u32[]{:S(2)}) collective-permute-start(bf16[64,4224]{1,0:T(8,128)(2,1)} %collective-permute-done.7.refs_1_), channel_id=1, source_target_pairs={{0,24},{1,7},{2,26},{3,1},{4,28},{5,3},{6,30},{7,5},{8,0},{9,15},{... | collective-permute-start | bytes 1622024 | tf_op jit(solution)/shard_map/ppermute | solution.py:32
  52.9 6.1 %collective-permute-done.13.refs_2_ = bf16[64,4224]{1,0:T(8,128)(2,1)S(1)} collective-permute-done((bf16[64,4224]{1,0:T(8,128)(2,1)}, bf16[64,4224]{1,0:T(8,128)(2,1)S(1)}, u32[]{:S(2)}, u32[]{:S(2)}) %collective-permute-start.13) | collective-permute-done | bytes 540704 | tf_op jit(solution)/shard_map/ppermute | solution.py:32
  60.6 2.0 %collective-permute-start.15 = (bf16[80,4096]{1,0:T(8,128)(2,1)S(1)}, bf16[80,4096]{1,0:T(8,128)(2,1)S(1)}, u32[]{:S(2)}, u32[]{:S(2)}) collective-permute-start(bf16[80,4096]{1,0:T(8,128)(2,1)S(1)} %get-tuple-element.67), channel_id=1, source_target_pairs={{0,24},{1,7},{2,26},{3,1},{4,28},{5,3},{6,30},{7,5},{8,0},{9,15},{... | collective-permute-start | bytes 1966088 | tf_op jit(solution)/shard_map/ppermute | solution.py:32
  62.7 3.2 %collective-permute-start.18 = (bf16[64,4096]{1,0:T(8,128)(2,1)S(1)}, bf16[64,4096]{1,0:T(8,128)(2,1)S(1)}, u32[]{:S(2)}, u32[]{:S(2)}) collective-permute-start(bf16[64,4096]{1,0:T(8,128)(2,1)S(1)} %get-tuple-element.78), channel_id=1, source_target_pairs={{0,24},{1,7},{2,26},{3,1},{4,28},{5,3},{6,30},{7,5},{8,0},{9,15},{... | collective-permute-start | bytes 1572872 | tf_op jit(solution)/shard_map/ppermute | solution.py:32
  65.9 7.2 %collective-permute-done.14 = bf16[64,4096]{1,0:T(8,128)(2,1)S(1)} collective-permute-done((bf16[64,4096]{1,0:T(8,128)(2,1)S(1)}, bf16[64,4096]{1,0:T(8,128)(2,1)S(1)}, u32[]{:S(2)}, u32[]{:S(2)}) %collective-permute-start.14) | collective-permute-done | bytes 524320 | tf_op jit(solution)/shard_map/ppermute | solution.py:32
  73.0 3.8 %collective-permute-done.18 = bf16[64,4096]{1,0:T(8,128)(2,1)S(1)} collective-permute-done((bf16[64,4096]{1,0:T(8,128)(2,1)S(1)}, bf16[64,4096]{1,0:T(8,128)(2,1)S(1)}, u32[]{:S(2)}, u32[]{:S(2)}) %collective-permute-start.18) | collective-permute-done | bytes 524320 | tf_op jit(solution)/shard_map/ppermute | solution.py:32
  77.0 3.3 %collective-permute-start.19 = (bf16[64,4096]{1,0:T(8,128)(2,1)S(1)}, bf16[64,4096]{1,0:T(8,128)(2,1)S(1)}, u32[]{:S(2)}, u32[]{:S(2)}) collective-permute-start(bf16[64,4096]{1,0:T(8,128)(2,1)S(1)} %add_convert_fusion.1), channel_id=1, source_target_pairs={{0,24},{1,7},{2,26},{3,1},{4,28},{5,3},{6,30},{7,5},{8,0},{9,15},{... | collective-permute-start | bytes 1572872 | tf_op jit(solution)/shard_map/ppermute | solution.py:32
  80.5 8.3 %collective-permute-done.19 = bf16[64,4096]{1,0:T(8,128)(2,1)S(1)} collective-permute-done((bf16[64,4096]{1,0:T(8,128)(2,1)S(1)}, bf16[64,4096]{1,0:T(8,128)(2,1)S(1)}, u32[]{:S(2)}, u32[]{:S(2)}) %collective-permute-start.19) | collective-permute-done | bytes 524320 | tf_op jit(solution)/shard_map/ppermute | solution.py:32
  89.1 2.0 %collective-permute-start.20 = (bf16[18,4096]{1,0:T(8,128)(2,1)S(1)}, bf16[18,4096]{1,0:T(8,128)(2,1)S(1)}, u32[]{:S(2)}, u32[]{:S(2)}) collective-permute-start(bf16[18,4096]{1,0:T(8,128)(2,1)S(1)} %get-tuple-element.97), channel_id=1, source_target_pairs={{0,2},{1,9},{2,4},{3,11},{4,6},{5,13},{6,0},{7,15},{8,10},{9,17},{... | collective-permute-start | bytes 442376 | tf_op jit(solution)/shard_map/ppermute | solution.py:28
  92.8 3.0 %collective-permute-done.17 = bf16[80,4096]{1,0:T(8,128)(2,1)S(1)} collective-permute-done((bf16[80,4096]{1,0:T(8,128)(2,1)S(1)}, bf16[80,4096]{1,0:T(8,128)(2,1)S(1)}, u32[]{:S(2)}, u32[]{:S(2)}) %collective-permute-start.17) | collective-permute-done | bytes 655392 | tf_op jit(solution)/shard_map/ppermute | solution.py:32
  96.4 2.8 %collective-permute-start.21 = (bf16[36,4096]{1,0:T(8,128)(2,1)S(1)}, bf16[36,4096]{1,0:T(8,128)(2,1)S(1)}, u32[]{:S(2)}, u32[]{:S(2)}) collective-permute-start(bf16[36,4096]{1,0:T(8,128)(2,1)S(1)} %fusion.30), channel_id=1, source_target_pairs={{0,2},{1,9},{2,4},{3,11},{4,6},{5,13},{6,0},{7,15},{8,10},{9,17},{... | collective-permute-start | bytes 884744 | tf_op jit(solution)/shard_map/ppermute | solution.py:28
  100.3 4.8 %collective-permute-done.21 = bf16[36,4096]{1,0:T(8,128)(2,1)S(1)} collective-permute-done((bf16[36,4096]{1,0:T(8,128)(2,1)S(1)}, bf16[36,4096]{1,0:T(8,128)(2,1)S(1)}, u32[]{:S(2)}, u32[]{:S(2)}) %collective-permute-start.21) | collective-permute-done | bytes 294944 | tf_op jit(solution)/shard_map/ppermute | solution.py:28
  109.3 2.3 %conditional.1 = (bf16[2,8192]{1,0:T(2,128)(2,1)S(1)}) conditional(s32[]{:T(128)} %convert_element_type.90, (s32[2]{0:T(128)S(1)}, bf16[2,8192]{1,0:T(2,128)(2,1)S(1)}, bf16[2,1024,4,256]{3,2,1,0:T(4,128)(2,1)S(1)}, bf16[2,4,256]{2,1,0:T(4,128)(2,1)S(1)}) %tuple.39, () %tuple.20), branch_computations={%region_0.3_spmd, %region_3.4_spmd} | conditional | flops 68128512 | bytes 14426640 | solution.py:300
  111.7 10.5 %collective-permute-done.24 = bf16[12,4096]{1,0:T(8,128)(2,1)S(1)} collective-permute-done((bf16[12,4096]{1,0:T(8,128)(2,1)S(1)}, bf16[12,4096]{1,0:T(8,128)(2,1)S(1)}, u32[]{:S(2)}, u32[]{:S(2)}) %collective-permute-start.24) | collective-permute-done | bytes 98336 | tf_op jit(solution)/shard_map/ppermute | solution.py:36
  (76 shorter events, 20.8 us)
Async XLA Ops:
  0.6 37.4 %collective-permute-start.10 = (bf16[4096,1536]{1,0:T(8,128)(2,1)}, bf16[4096,1536]{1,0:T(8,128)(2,1)}, u32[]{:S(2)}, u32[]{:S(2)}) collective-permute-start(bf16[4096,1536]{1,0:T(8,128)(2,1)} %bitcast.19), channel_id=1, source_target_pairs={{0,1},{1,0},{2,3},{3,2},{4,5},{5,4},{6,7},{7,6},{8,9},{9,8},{10,11... | collective-permute-start | bytes 37748744 | tf_op jit(solution)/shard_map/ppermute | solution.py:51
  0.7 37.3 %collective-permute-start.11 = (bf16[768,4096]{1,0:T(8,128)(2,1)}, bf16[768,4096]{1,0:T(8,128)(2,1)}, u32[]{:S(2)}, u32[]{:S(2)}) collective-permute-start(bf16[768,4096]{1,0:T(8,128)(2,1)} %bitcast.21), channel_id=1, source_target_pairs={{0,1},{1,0},{2,3},{3,2},{4,5},{5,4},{6,7},{7,6},{8,9},{9,8},{10,11... | collective-permute-start | bytes 18874376 | tf_op jit(solution)/shard_map/ppermute | solution.py:51
  2.2 11.0 %collective-permute-start = (bf16[12,4224]{1,0:T(8,128)(2,1)S(1)}, bf16[12,4224]{1,0:T(8,128)(2,1)S(1)}, u32[]{:S(2)}, u32[]{:S(2)}) collective-permute-start(bf16[12,4224]{1,0:T(8,128)(2,1)S(1)} %shard_map.107), channel_id=1, source_target_pairs={{0,96},{1,97},{2,98},{3,99},{4,100},{5,101},{6,102},{7,103},{8,104... | collective-permute-start | bytes 304136 | tf_op jit(solution)/shard_map/ppermute | solution.py:36
  13.3 8.5 %collective-permute-start.3 = (bf16[36,4224]{1,0:T(8,128)(2,1)S(1)}, bf16[36,4224]{1,0:T(8,128)(2,1)S(1)}, u32[]{:S(2)}, u32[]{:S(2)}) collective-permute-start(bf16[36,4224]{1,0:T(8,128)(2,1)S(1)} %pad_maximum_fusion), channel_id=1, source_target_pairs={{0,2},{1,9},{2,4},{3,11},{4,6},{5,13},{6,0},{7,15},{8,10},{9,17},{... | collective-permute-start | bytes 912392 | tf_op jit(solution)/shard_map/ppermute | solution.py:28
  14.9 7.2 %collective-permute-start.4 = (bf16[36,4224]{1,0:T(8,128)(2,1)S(1)}, bf16[36,4224]{1,0:T(8,128)(2,1)S(1)}, u32[]{:S(2)}, u32[]{:S(2)}) collective-permute-start(bf16[36,4224]{1,0:T(8,128)(2,1)S(1)} %pad_maximum_fusion), channel_id=1, source_target_pairs={{0,6},{1,25},{2,0},{3,27},{4,2},{5,29},{6,4},{7,31},{8,14},{9,1},{... | collective-permute-start | bytes 912392 | tf_op jit(solution)/shard_map/ppermute | solution.py:28
  22.1 12.4 %collective-permute-start.6 = (bf16[36,4224]{1,0:T(8,128)(2,1)S(1)}, bf16[36,4224]{1,0:T(8,128)(2,1)S(1)}, u32[]{:S(2)}, u32[]{:S(2)}) collective-permute-start(bf16[36,4224]{1,0:T(8,128)(2,1)S(1)} %pad_maximum_fusion), channel_id=1, source_target_pairs={{0,4},{1,17},{2,6},{3,19},{4,0},{5,21},{6,2},{7,23},{8,12},{9,25},... | collective-permute-start | bytes 912392 | tf_op jit(solution)/shard_map/ppermute | solution.py:28
  25.0 13.1 %collective-permute-start.5 = (bf16[80,4224]{1,0:T(8,128)(2,1)S(1)}, bf16[80,4224]{1,0:T(8,128)(2,1)S(1)}, u32[]{:S(2)}, u32[]{:S(2)}) collective-permute-start(bf16[80,4224]{1,0:T(8,128)(2,1)S(1)} %pad_add_fusion.refs_1_), channel_id=1, source_target_pairs={{0,8},{1,3},{2,10},{3,5},{4,12},{5,7},{6,14},{7,1},{8,16},{9,11},{... | collective-permute-start | bytes 2027528 | tf_op jit(solution)/shard_map/ppermute | solution.py:32
  27.0 11.3 %collective-permute-start.9 = (bf16[80,4224]{1,0:T(8,128)(2,1)S(1)}, bf16[80,4224]{1,0:T(8,128)(2,1)S(1)}, u32[]{:S(2)}, u32[]{:S(2)}) collective-permute-start(bf16[80,4224]{1,0:T(8,128)(2,1)S(1)} %pad_add_fusion.refs_1_), channel_id=1, source_target_pairs={{0,24},{1,7},{2,26},{3,1},{4,28},{5,3},{6,30},{7,5},{8,0},{9,15},{... | collective-permute-start | bytes 2027528 | tf_op jit(solution)/shard_map/ppermute | solution.py:32
  34.6 10.3 %collective-permute-start.7 = (bf16[64,4224]{1,0:T(8,128)(2,1)S(1)}, bf16[64,4224]{1,0:T(8,128)(2,1)}, u32[]{:S(2)}, u32[]{:S(2)}) collective-permute-start(bf16[64,4224]{1,0:T(8,128)(2,1)S(1)} %pad_add_fusion.1.refs_2_), channel_id=1, source_target_pairs={{0,24},{1,7},{2,26},{3,1},{4,28},{5,3},{6,30},{7,5},{8,0},{9,15},{... | collective-permute-start | bytes 1622024 | tf_op jit(solution)/shard_map/ppermute | solution.py:32
  38.1 10.6 %collective-permute-start.8 = (bf16[64,4224]{1,0:T(8,128)(2,1)S(1)}, bf16[64,4224]{1,0:T(8,128)(2,1)S(1)}, u32[]{:S(2)}, u32[]{:S(2)}) collective-permute-start(bf16[64,4224]{1,0:T(8,128)(2,1)S(1)} %pad_add_fusion.1.refs_2_), channel_id=1, source_target_pairs={{0,8},{1,3},{2,10},{3,5},{4,12},{5,7},{6,14},{7,1},{8,16},{9,11},{... | collective-permute-start | bytes 1622024 | tf_op jit(solution)/shard_map/ppermute | solution.py:32
  48.6 12.0 %collective-permute-start.12 = (bf16[80,4224]{1,0:T(8,128)(2,1)S(1)}, bf16[80,4224]{1,0:T(8,128)(2,1)S(1)}, u32[]{:S(2)}, u32[]{:S(2)}) collective-permute-start(bf16[80,4224]{1,0:T(8,128)(2,1)S(1)} %collective-permute-done.5.refs_2_), channel_id=1, source_target_pairs={{0,8},{1,3},{2,10},{3,5},{4,12},{5,7},{6,14},{7,1},{8,16},{9,11},{... | collective-permute-start | bytes 2027528 | tf_op jit(solution)/shard_map/ppermute | solution.py:32
  48.6 10.4 %collective-permute-start.13 = (bf16[64,4224]{1,0:T(8,128)(2,1)}, bf16[64,4224]{1,0:T(8,128)(2,1)S(1)}, u32[]{:S(2)}, u32[]{:S(2)}) collective-permute-start(bf16[64,4224]{1,0:T(8,128)(2,1)} %collective-permute-done.7.refs_1_), channel_id=1, source_target_pairs={{0,24},{1,7},{2,26},{3,1},{4,28},{5,3},{6,30},{7,5},{8,0},{9,15},{... | collective-permute-start | bytes 1622024 | tf_op jit(solution)/shard_map/ppermute | solution.py:32
  60.6 12.4 %collective-permute-start.15 = (bf16[80,4096]{1,0:T(8,128)(2,1)S(1)}, bf16[80,4096]{1,0:T(8,128)(2,1)S(1)}, u32[]{:S(2)}, u32[]{:S(2)}) collective-permute-start(bf16[80,4096]{1,0:T(8,128)(2,1)S(1)} %get-tuple-element.67), channel_id=1, source_target_pairs={{0,24},{1,7},{2,26},{3,1},{4,28},{5,3},{6,30},{7,5},{8,0},{9,15},{... | collective-permute-start | bytes 1966088 | tf_op jit(solution)/shard_map/ppermute | solution.py:32
  62.6 10.4 %collective-permute-start.14 = (bf16[64,4096]{1,0:T(8,128)(2,1)S(1)}, bf16[64,4096]{1,0:T(8,128)(2,1)S(1)}, u32[]{:S(2)}, u32[]{:S(2)}) collective-permute-start(bf16[64,4096]{1,0:T(8,128)(2,1)S(1)} %get-tuple-element.66), channel_id=1, source_target_pairs={{0,8},{1,3},{2,10},{3,5},{4,12},{5,7},{6,14},{7,1},{8,16},{9,11},{... | collective-permute-start | bytes 1572872 | tf_op jit(solution)/shard_map/ppermute | solution.py:32
  62.7 14.2 %collective-permute-start.18 = (bf16[64,4096]{1,0:T(8,128)(2,1)S(1)}, bf16[64,4096]{1,0:T(8,128)(2,1)S(1)}, u32[]{:S(2)}, u32[]{:S(2)}) collective-permute-start(bf16[64,4096]{1,0:T(8,128)(2,1)S(1)} %get-tuple-element.78), channel_id=1, source_target_pairs={{0,24},{1,7},{2,26},{3,1},{4,28},{5,3},{6,30},{7,5},{8,0},{9,15},{... | collective-permute-start | bytes 1572872 | tf_op jit(solution)/shard_map/ppermute | solution.py:32
  65.9 14.4 %collective-permute-start.16 = (bf16[80,4096]{1,0:T(8,128)(2,1)S(1)}, bf16[80,4096]{1,0:T(8,128)(2,1)S(1)}, u32[]{:S(2)}, u32[]{:S(2)}) collective-permute-start(bf16[80,4096]{1,0:T(8,128)(2,1)S(1)} %get-tuple-element.70), channel_id=1, source_target_pairs={{0,8},{1,3},{2,10},{3,5},{4,12},{5,7},{6,14},{7,1},{8,16},{9,11},{... | collective-permute-start | bytes 1966088 | tf_op jit(solution)/shard_map/ppermute | solution.py:32
  77.0 11.8 %collective-permute-start.19 = (bf16[64,4096]{1,0:T(8,128)(2,1)S(1)}, bf16[64,4096]{1,0:T(8,128)(2,1)S(1)}, u32[]{:S(2)}, u32[]{:S(2)}) collective-permute-start(bf16[64,4096]{1,0:T(8,128)(2,1)S(1)} %add_convert_fusion.1), channel_id=1, source_target_pairs={{0,24},{1,7},{2,26},{3,1},{4,28},{5,3},{6,30},{7,5},{8,0},{9,15},{... | collective-permute-start | bytes 1572872 | tf_op jit(solution)/shard_map/ppermute | solution.py:32
  80.4 15.4 %collective-permute-start.17 = (bf16[80,4096]{1,0:T(8,128)(2,1)S(1)}, bf16[80,4096]{1,0:T(8,128)(2,1)S(1)}, u32[]{:S(2)}, u32[]{:S(2)}) collective-permute-start(bf16[80,4096]{1,0:T(8,128)(2,1)S(1)} %add_convert_fusion), channel_id=1, source_target_pairs={{0,8},{1,3},{2,10},{3,5},{4,12},{5,7},{6,14},{7,1},{8,16},{9,11},{... | collective-permute-start | bytes 1966088 | tf_op jit(solution)/shard_map/ppermute | solution.py:32
  89.1 7.2 %collective-permute-start.20 = (bf16[18,4096]{1,0:T(8,128)(2,1)S(1)}, bf16[18,4096]{1,0:T(8,128)(2,1)S(1)}, u32[]{:S(2)}, u32[]{:S(2)}) collective-permute-start(bf16[18,4096]{1,0:T(8,128)(2,1)S(1)} %get-tuple-element.97), channel_id=1, source_target_pairs={{0,2},{1,9},{2,4},{3,11},{4,6},{5,13},{6,0},{7,15},{8,10},{9,17},{... | collective-permute-start | bytes 442376 | tf_op jit(solution)/shard_map/ppermute | solution.py:28
  91.1 8.1 %collective-permute-start.22 = (bf16[18,4096]{1,0:T(8,128)(2,1)S(1)}, bf16[18,4096]{1,0:T(8,128)(2,1)S(1)}, u32[]{:S(2)}, u32[]{:S(2)}) collective-permute-start(bf16[18,4096]{1,0:T(8,128)(2,1)S(1)} %get-tuple-element.98), channel_id=1, source_target_pairs={{0,6},{1,25},{2,0},{3,27},{4,2},{5,29},{6,4},{7,31},{8,14},{9,1},{... | collective-permute-start | bytes 442376 | tf_op jit(solution)/shard_map/ppermute | solution.py:28
  96.4 8.8 %collective-permute-start.21 = (bf16[36,4096]{1,0:T(8,128)(2,1)S(1)}, bf16[36,4096]{1,0:T(8,128)(2,1)S(1)}, u32[]{:S(2)}, u32[]{:S(2)}) collective-permute-start(bf16[36,4096]{1,0:T(8,128)(2,1)S(1)} %fusion.30), channel_id=1, source_target_pairs={{0,2},{1,9},{2,4},{3,11},{4,6},{5,13},{6,0},{7,15},{8,10},{9,17},{... | collective-permute-start | bytes 884744 | tf_op jit(solution)/shard_map/ppermute | solution.py:28
  106.6 15.5 %collective-permute-start.24 = (bf16[12,4096]{1,0:T(8,128)(2,1)S(1)}, bf16[12,4096]{1,0:T(8,128)(2,1)S(1)}, u32[]{:S(2)}, u32[]{:S(2)}) collective-permute-start(bf16[12,4096]{1,0:T(8,128)(2,1)S(1)} %get-tuple-element.101), channel_id=1, source_target_pairs={{96,0},{97,1},{98,2},{99,3},{100,4},{101,5},{102,6},{103,7},{104,8... | collective-permute-start | bytes 294920 | tf_op jit(solution)/shard_map/ppermute | solution.py:36
  107.9 14.2 %collective-permute-start.25 = (bf16[12,4096]{1,0:T(8,128)(2,1)S(1)}, bf16[12,4096]{1,0:T(8,128)(2,1)S(1)}, u32[]{:S(2)}, u32[]{:S(2)}) collective-permute-start(bf16[12,4096]{1,0:T(8,128)(2,1)S(1)} %get-tuple-element.99), channel_id=1, source_target_pairs={{96,32},{97,33},{98,34},{99,35},{100,36},{101,37},{102,38},{103,39... | collective-permute-start | bytes 294920 | tf_op jit(solution)/shard_map/ppermute | solution.py:36
  108.6 13.5 %collective-permute-start.26 = (bf16[12,4096]{1,0:T(8,128)(2,1)S(1)}, bf16[12,4096]{1,0:T(8,128)(2,1)S(1)}, u32[]{:S(2)}, u32[]{:S(2)}) collective-permute-start(bf16[12,4096]{1,0:T(8,128)(2,1)S(1)} %get-tuple-element.100), channel_id=1, source_target_pairs={{96,64},{97,65},{98,66},{99,67},{100,68},{101,69},{102,70},{103,71... | collective-permute-start | bytes 294920 | tf_op jit(solution)/shard_map/ppermute | solution.py:36
  (8 other events, 81.5 us)
